TPU v7x, 32 devices: a whole 2x2x4 slice. The times are simulated.
32 devices in a mesh: groups: 2 (over y), fsdp: 8 (over z, x), section: 2 (over core).
Axes of the slice: x: 2, y: 2, z: 4, core: 2. Of those that a mesh axis runs over, the one named last changes fastest.
Arguments:
- tokens: bfloat16 [512, 8192], P(('groups', 'section'), 'fsdp'), parts along dimension 0, may hold values from -6 to 6
- cotangent: bfloat16 [512, 8192], P(('groups', 'section'), 'fsdp'), parts along dimension 0, may hold values from -6 to 6
- gate_blocks: bfloat16 [128, 128, 128], P('fsdp'), may hold values from -0.125 to 0.125
- up_blocks: bfloat16 [128, 128, 128], P('fsdp'), may hold values from -0.125 to 0.125
- down_blocks: bfloat16 [128, 128, 128], P('fsdp'), may hold values from -0.125 to 0.125
- gate_dest: int32 [128, 1], P('fsdp'), may hold values from 0 to 7; in each aligned block of 16 rows (0 to 15, 16 to 31, ...) at most 3 rows name the same one
- up_dest: int32 [128, 1], P('fsdp'), may hold values from 0 to 7; in each aligned block of 16 rows (0 to 15, 16 to 31, ...) at most 3 rows name the same one
- down_dest: int32 [128, 1], P('fsdp'), may hold values from 0 to 7; in each aligned block of 16 rows (0 to 15, 16 to 31, ...) at most 3 rows name the same one
- gate_rows: int32 [128], P('fsdp'), may hold values from 0 to 63
- up_rows: int32 [128], P('fsdp'), may hold values from 0 to 63
- down_rows: int32 [128], P('fsdp'), may hold values from 0 to 63
Outputs:
- input_grad: bfloat16 [512, 8192], P(('groups', 'section'), 'fsdp'), parts along dimension 0
- gate_grad: float32 [256, 128, 128], P(('groups', 'fsdp')), parts along dimension 0
- up_grad: float32 [256, 128, 128], P(('groups', 'fsdp')), parts along dimension 0
- down_block_gradient: float32 [256, 128, 128], P(('groups', 'fsdp')), parts along dimension 0
There are 2 independent parts, one for each index of `groups`. A program takes and returns all parts, laid end to end along the dimension named above; an argument that names none is the same for every part. Nothing has to cross between parts.
Inputs may be any that keep to these rules, and one draw needn't show every extreme that they name: `gate_dest`: among the 16 blocks of one projection held by one owner, at most 3 share one offset. `up_dest`: among the 16 blocks of one projection held by one owner, at most 3 share one offset. `down_dest`: among the 16 blocks of one projection held by one owner, at most 3 share one offset.
All inputs are finite; a program needn't handle non-finite values.
Results may differ from a plain program's by a relative error of at most 0.0085.
Values may be sent and summed in bfloat16 or wider, within the bound.
No kernel may reach another device: no remote copies, remote signals or barrier semaphores. Data moves between devices by JAX's collectives and lax.ppermute only.
A program may use at most 64 MiB of HBM per device.

v0:
```python
import jax
import jax.numpy as jnp
from jax import lax
from jax.sharding import PartitionSpec as P

BLK = 128
SPREAD = 8
CAP = 3


def shifted(block, axis, distance):
    devices = range(lax.axis_size(axis))
    route = [((i - distance) % len(devices), i) for i in devices]
    return lax.ppermute(block, axis, route)


def slot_ranks(target):
    matches = (target[:, None] == jnp.arange(SPREAD, dtype=jnp.int32)[None, :]).astype(jnp.int32)
    earlier = jnp.cumsum(matches, axis=0) - matches
    return jnp.sum(earlier * matches, axis=1)


def pack_blocks(weights, target, row_ids):
    position = target * CAP + slot_ranks(target)
    chosen = position[None, :] == jnp.arange(SPREAD * CAP, dtype=jnp.int32)[:, None]
    packed = jnp.einsum(
        "sj,jab->sab", chosen.astype(jnp.bfloat16), weights, preferred_element_type=jnp.float32
    )
    packed_rows = jnp.sum(jnp.where(chosen, row_ids[None, :], 0), axis=1)
    return (
        packed.astype(jnp.bfloat16).reshape(SPREAD, CAP, BLK, BLK),
        packed_rows.reshape(SPREAD, CAP),
        position,
    )


def row_sum(terms, row_ids, row_blocks):
    onehot = (row_ids[:, None] == jnp.arange(row_blocks, dtype=jnp.int32)[None, :]).astype(
        jnp.bfloat16
    )
    high_part = terms.astype(jnp.bfloat16)
    lower_portion = (terms - high_part.astype(jnp.float32)).astype(jnp.bfloat16)
    summed = jnp.einsum("tsk,sr->trk", high_part, onehot, preferred_element_type=jnp.float32)
    return summed + jnp.einsum(
        "tsk,sr->trk", lower_portion, onehot, preferred_element_type=jnp.float32
    )


def shards(
    tokens,
    cotangent,
    gate_blocks,
    up_blocks,
    down_blocks,
    gate_dest,
    up_dest,
    down_dest,
    gate_rows,
    up_rows,
    down_rows,
):
    whole_tokens, whole_cotan = (
        lax.all_gather(tokens, "fsdp", axis=1, tiled=True),
        lax.all_gather(cotangent, "fsdp", axis=1, tiled=True),
    )
    local_rows = whole_tokens.shape[0]
    row_blocks = whole_tokens.shape[1] // BLK
    token_grid = whole_tokens.reshape(local_rows, row_blocks, BLK)
    cotan_grid = whole_cotan.reshape(local_rows, row_blocks, BLK)
    packing_layouts = [
        pack_blocks(weights, target[:, 0], row_ids)
        for weights, target, row_ids in (
            (gate_blocks, gate_dest, gate_rows),
            (up_blocks, up_dest, up_rows),
            (down_blocks, down_dest, down_rows),
        )
    ]
    outgoing_blocks = jnp.stack(
        [packing_layout[0] for packing_layout in packing_layouts], axis=1
    ).reshape(SPREAD, 3 * CAP, BLK, BLK)
    send_rows = (
        jnp.stack([packing_layout[1] for packing_layout in packing_layouts], axis=1)
        .reshape(SPREAD, 3 * CAP)
        .astype(jnp.bfloat16)
    )
    block_list = [outgoing_blocks[0]]
    rowid_list = [send_rows[0]]
    for offset in range(1, SPREAD):
        moved_blocks, moved_rows = shifted(
            (outgoing_blocks[offset], send_rows[offset]), "fsdp", -offset
        )
        block_list.append(moved_blocks)
        rowid_list.append(moved_rows)
    got_blocks = jnp.stack(block_list, axis=0)
    got_rows = jnp.stack(rowid_list, axis=0)
    got_blocks = got_blocks.reshape(SPREAD, 3, CAP, BLK, BLK)
    got_rows = got_rows.reshape(SPREAD, 3, CAP).astype(jnp.int32)
    slot_count = SPREAD * CAP
    gate_w = got_blocks[:, 0].reshape(slot_count, BLK, BLK)
    up_w = got_blocks[:, 1].reshape(slot_count, BLK, BLK)
    down_w = got_blocks[:, 2].reshape(slot_count, BLK, BLK)
    gate_ids = got_rows[:, 0].reshape(slot_count)
    up_ids = got_rows[:, 1].reshape(slot_count)
    down_ids = got_rows[:, 2].reshape(slot_count)
    tok_gate = token_grid[:, gate_ids, :]
    tok_up = token_grid[:, up_ids, :]
    cot_down = cotan_grid[:, down_ids, :]
    gate = jnp.einsum("tsk,skn->tn", tok_gate, gate_w, preferred_element_type=jnp.float32)
    upper = jnp.einsum("tsk,skn->tn", tok_up, up_w, preferred_element_type=jnp.float32)
    sigma = jax.nn.sigmoid(gate)
    hidden = (gate * sigma * upper).astype(jnp.bfloat16)
    hidden_grad = jnp.einsum("tsn,skn->tk", cot_down, down_w, preferred_element_type=jnp.float32)
    gate_d = (hidden_grad * upper * sigma * (1.0 + gate * (1.0 - sigma))).astype(jnp.bfloat16)
    up_d = (hidden_grad * gate * sigma).astype(jnp.bfloat16)
    gate_part = jnp.einsum(
        "tsk,tn->skn", tok_gate, gate_d, preferred_element_type=jnp.float32
    ).astype(jnp.bfloat16)
    up_part = jnp.einsum("tsk,tn->skn", tok_up, up_d, preferred_element_type=jnp.float32).astype(
        jnp.bfloat16
    )
    down_part = jnp.einsum(
        "tk,tsn->skn", hidden, cot_down, preferred_element_type=jnp.float32
    ).astype(jnp.bfloat16)
    gate_terms = jnp.einsum("tn,skn->tsk", gate_d, gate_w, preferred_element_type=jnp.float32)
    up_terms = jnp.einsum("tn,skn->tsk", up_d, up_w, preferred_element_type=jnp.float32)
    partial_input = row_sum(gate_terms, gate_ids, row_blocks) + row_sum(
        up_terms, up_ids, row_blocks
    )
    partial_input = partial_input.reshape(local_rows, row_blocks * BLK)
    input_grad = lax.psum_scatter(partial_input, "fsdp", scatter_dimension=1, tiled=True).astype(
        jnp.bfloat16
    )
    grad_send = jnp.stack(
        [
            gate_part.reshape(SPREAD, CAP, BLK, BLK),
            up_part.reshape(SPREAD, CAP, BLK, BLK),
            down_part.reshape(SPREAD, CAP, BLK, BLK),
        ],
        axis=1,
    ).reshape(SPREAD, 3 * CAP, BLK, BLK)
    back_list = [grad_send[0]]
    for offset in range(1, SPREAD):
        back_list.append(shifted(grad_send[offset], "fsdp", offset))
    returned = jnp.stack(back_list, axis=0)
    returned = returned.reshape(SPREAD, 3, CAP, BLK, BLK)
    owned_by_holder = []
    for index_of_matrix in range(3):
        flattened_gradients = returned[:, index_of_matrix].reshape(slot_count, BLK, BLK)
        owned_by_holder.append(
            jnp.take(flattened_gradients, packing_layouts[index_of_matrix][2], axis=0)
        )
    gate_grad, up_grad, down_block_gradient = (
        lax.psum(owned_by_holder[0].astype(jnp.float32).astype(jnp.bfloat16), "section").astype(
            jnp.float32
        ),
        lax.psum(owned_by_holder[1].astype(jnp.float32).astype(jnp.bfloat16), "section").astype(
            jnp.float32
        ),
        lax.psum(owned_by_holder[2].astype(jnp.float32).astype(jnp.bfloat16), "section").astype(
            jnp.float32
        ),
    )
    return (input_grad, gate_grad, up_grad, down_block_gradient)


def solution(mesh):
    return jax.shard_map(
        shards,
        mesh=mesh,
        in_specs=(
            P(("groups", "section"), "fsdp"),
            P(("groups", "section"), "fsdp"),
            P("fsdp", None, None),
            P("fsdp", None, None),
            P("fsdp", None, None),
            P("fsdp", None),
            P("fsdp", None),
            P("fsdp", None),
            P("fsdp"),
            P("fsdp"),
            P("fsdp"),
        ),
        out_specs=(
            P(("groups", "section"), "fsdp"),
            P(("groups", "fsdp"), None, None),
            P(("groups", "fsdp"), None, None),
            P(("groups", "fsdp"), None, None),
        ),
        check_vma=False,
    )
```

profile of v0, /device:TPU:0, one launch (start us, length us, event | category | flops | bytes accessed | tf_op | source)
XLA Modules:
  0.0 359.0 jit_solution(8441874005911983135)
XLA Ops:
  17.4 6.0 %collective-permute-start.7 = (bf16[9,128,128]{2,1,0:T(8,128)(2,1)S(1)}, bf16[9,128,128]{2,1,0:T(8,128)(2,1)S(1)}, u32[]{:S(2)}, u32[]{:S(2)}) collective-permute-start(bf16[9,128,128]{2,1,0:T(8,128)(2,1)S(1)} %bitcast.174), channel_id=1, source_target_pairs={{2,0},{4,2},{6,4},{8,6},{10,8},{12,10},{14,12},{0,14},{3,1},{5,3},... | collective-permute-start | bytes 884744 | tf_op jit(solution)/shard_map/ppermute | solution.py:14
  23.9 3.0 collective-permute-start.10
  33.1 22.8 %collective-permute-done = bf16[9]{0:T(256)(128)(2,1)S(1)} collective-permute-done((bf16[9]{0:T(256)(128)(2,1)S(1)}, bf16[9]{0:T(256)(128)(2,1)S(1)}, u32[]{:S(2)}, u32[]{:S(2)}) %collective-permute-start) | collective-permute-done | bytes 50 | tf_op jit(solution)/shard_map/ppermute | solution.py:14
  56.6 2.8 collective-permute-done.1
  59.4 14.4 %collective-permute-start.2 = (bf16[9]{0:T(256)(128)(2,1)S(1)}, bf16[9]{0:T(256)(128)(2,1)S(1)}, u32[]{:S(2)}, u32[]{:S(2)}) collective-permute-start(bf16[9]{0:T(256)(128)(2,1)S(1)} %squeeze.77), channel_id=1, source_target_pairs={{6,0},{8,2},{10,4},{12,6},{14,8},{0,10},{2,12},{4,14},{7,1},{9,3},... | collective-permute-start | bytes 62 | tf_op jit(solution)/shard_map/ppermute | solution.py:14
  77.8 2.8 collective-permute-done.3
  80.6 3.8 %collective-permute-start.4 = (bf16[9]{0:T(256)(128)(2,1)S(1)}, bf16[9]{0:T(256)(128)(2,1)S(1)}, u32[]{:S(2)}, u32[]{:S(2)}) collective-permute-start(bf16[9]{0:T(256)(128)(2,1)S(1)} %squeeze.79), channel_id=1, source_target_pairs={{10,0},{12,2},{14,4},{0,6},{2,8},{4,10},{6,12},{8,14},{11,1},{13,3... | collective-permute-start | bytes 62 | tf_op jit(solution)/shard_map/ppermute | solution.py:14
  87.3 4.1 %collective-permute-done.5 = bf16[9]{0:T(256)(128)(2,1)S(1)} collective-permute-done((bf16[9]{0:T(256)(128)(2,1)S(1)}, bf16[9]{0:T(256)(128)(2,1)S(1)}, u32[]{:S(2)}, u32[]{:S(2)}) %collective-permute-start.5) | collective-permute-done | bytes 50 | tf_op jit(solution)/shard_map/ppermute | solution.py:14
  91.4 3.3 collective-permute-start.6
  108.5 20.7 %collective-permute-done.11 = bf16[9,128,128]{2,1,0:T(8,128)(2,1)S(1)} collective-permute-done((bf16[9,128,128]{2,1,0:T(8,128)(2,1)S(1)}, bf16[9,128,128]{2,1,0:T(8,128)(2,1)S(1)}, u32[]{:S(2)}, u32[]{:S(2)}) %collective-permute-start.11) | collective-permute-done | bytes 294944 | tf_op jit(solution)/shard_map/ppermute | solution.py:14
  131.6 2.7 fusion.51
  134.3 4.1 %copy.72 = bf16[128,64,128]{2,0,1:T(8,128)(2,1)} copy(bf16[128,64,128]{0,2,1:T(8,128)(2,1)} %bitcast.166) | data formatting | bytes 4194304 | tf_op jit(solution)/shard_map/reshape | solution.py:69
  138.3 17.6 %all-gather.5.cloned.1.call-done = bf16[128,8192]{0,1:T(8,128)(2,1)} async-done(((bf16[128,1024]{0,1:T(8,128)(2,1)}), bf16[128,8192]{0,1:T(8,128)(2,1)}) %all-gather.5.cloned.1.call-update) | async-done | bytes 2097168 | tf_op jit(solution)/shard_map/all_gather | solution.py:63
  155.9 4.1 %copy.87 = bf16[128,64,128]{2,0,1:T(8,128)(2,1)} copy(bf16[128,64,128]{0,2,1:T(8,128)(2,1)} %bitcast.167) | data formatting | bytes 4194304 | tf_op jit(solution)/shard_map/reshape | solution.py:68
  164.7 3.1 gather_fusion
  179.9 2.9 collective-permute-start.17
  182.8 2.8 fusion.11
  185.6 3.3 collective-permute-done.14
  189.0 5.7 %collective-permute-start.20 = (bf16[9,128,128]{2,1,0:T(8,128)(2,1)S(1)}, bf16[9,128,128]{2,1,0:T(8,128)(2,1)S(1)}, u32[]{:S(2)}, u32[]{:S(2)}) collective-permute-start(bf16[9,128,128]{2,1,0:T(8,128)(2,1)S(1)} %bitcast.175), channel_id=1, source_target_pairs={{2,0},{4,2},{6,4},{8,6},{10,8},{12,10},{14,12},{0,14},{3,1},{5,3},... | collective-permute-start | bytes 884744 | tf_op jit(solution)/shard_map/ppermute | solution.py:14
  194.7 17.1 %collective-permute-done.16 = bf16[9,128,128]{2,1,0:T(8,128)(2,1)S(1)} collective-permute-done((bf16[9,128,128]{2,1,0:T(8,128)(2,1)S(1)}, bf16[9,128,128]{2,1,0:T(8,128)(2,1)S(1)}, u32[]{:S(2)}, u32[]{:S(2)}) %collective-permute-start.16) | collective-permute-done | bytes 294944 | tf_op jit(solution)/shard_map/ppermute | solution.py:14
  212.0 2.8 collective-permute-done.20
  227.2 5.2 %copy.116 = f32[16,8,64,128]{3,1,2,0:T(8,128)} copy(f32[16,8,64,128]{3,2,1,0:T(8,128)S(1)} %bitcast.150) | data formatting | bytes 8388608
  232.4 24.7 %all-reduce.3.cloned.1.call-done = (bf16[16,128,128]{2,1,0:T(8,128)(2,1)}, bf16[16,128,128]{2,1,0:T(8,128)(2,1)}, bf16[16,128,128]{2,1,0:T(8,128)(2,1)}) async-done(((bf16[16,128,128]{2,1,0:T(8,128)(2,1)}, bf16[16,128,128]{2,1,0:T(8,128)(2,1)}, bf16[16,128,128]{2,1,0:T(8,128)(2,1)}), (bf16[16,128,128]{2,1,0:T(8,128)(2,1)}, bf16[16,128,128]{2,1,0:T(8,128)(2,1)}, ...) | async-done | bytes 1572880 | tf_op jit(solution)/shard_map/psum | solution.py:153
  262.5 88.2 %reduce-scatter.2.cloned.1.call-done = f32[128,1024]{1,0:T(8,128)} async-done(((f32[128,8192]{1,0:T(8,128)}), f32[128,1024]{1,0:T(8,128)}) %reduce-scatter.2.cloned.1.call-update) | async-done | bytes 524304 | tf_op jit(solution)/shard_map/reduce_scatter | solution.py:130
  (182 shorter events, 76.7 us)
Async XLA Ops:
  7.2 127.1 %all-gather.3.cloned.1.call-start = ((), (), s32[]{:S(2)}) async-start(), calls=%async_computation.1 | async-start | bytes 2359296 | tf_op jit(solution)/shard_map/all_gather | solution.py:64
  9.1 146.8 %all-gather.5.cloned.1.call-start = ((), (), s32[]{:S(2)}) async-start(), calls=%async_computation.2 | async-start | bytes 2359296 | tf_op jit(solution)/shard_map/all_gather | solution.py:63
  17.4 85.6 %collective-permute-start.7 = (bf16[9,128,128]{2,1,0:T(8,128)(2,1)S(1)}, bf16[9,128,128]{2,1,0:T(8,128)(2,1)S(1)}, u32[]{:S(2)}, u32[]{:S(2)}) collective-permute-start(bf16[9,128,128]{2,1,0:T(8,128)(2,1)S(1)} %bitcast.174), channel_id=1, source_target_pairs={{2,0},{4,2},{6,4},{8,6},{10,8},{12,10},{14,12},{0,14},{3,1},{5,3},... | collective-permute-start | bytes 884744 | tf_op jit(solution)/shard_map/ppermute | solution.py:14
  23.4 80.5 %collective-permute-start.8 = (bf16[9,128,128]{2,1,0:T(8,128)(2,1)S(1)}, bf16[9,128,128]{2,1,0:T(8,128)(2,1)S(1)}, u32[]{:S(2)}, u32[]{:S(2)}) collective-permute-start(bf16[9,128,128]{2,1,0:T(8,128)(2,1)S(1)} %bitcast.173), channel_id=1, source_target_pairs={{4,0},{6,2},{8,4},{10,6},{12,8},{14,10},{0,12},{2,14},{5,1},{7,3},... | collective-permute-start | bytes 884744 | tf_op jit(solution)/shard_map/ppermute | solution.py:14
  23.9 83.1 %collective-permute-start.9 = (bf16[9,128,128]{2,1,0:T(8,128)(2,1)S(1)}, bf16[9,128,128]{2,1,0:T(8,128)(2,1)S(1)}, u32[]{:S(2)}, u32[]{:S(2)}) collective-permute-start(bf16[9,128,128]{2,1,0:T(8,128)(2,1)S(1)} %bitcast.172), channel_id=1, source_target_pairs={{6,0},{8,2},{10,4},{12,6},{14,8},{0,10},{2,12},{4,14},{7,1},{9,3},... | collective-permute-start | bytes 884744 | tf_op jit(solution)/shard_map/ppermute | solution.py:14
  23.9 83.8 %collective-permute-start.10 = (bf16[9,128,128]{2,1,0:T(8,128)(2,1)S(1)}, bf16[9,128,128]{2,1,0:T(8,128)(2,1)S(1)}, u32[]{:S(2)}, u32[]{:S(2)}) collective-permute-start(bf16[9,128,128]{2,1,0:T(8,128)(2,1)S(1)} %bitcast.171), channel_id=1, source_target_pairs={{8,0},{10,2},{12,4},{14,6},{0,8},{2,10},{4,12},{6,14},{9,1},{11,3}... | collective-permute-start | bytes 884744 | tf_op jit(solution)/shard_map/ppermute | solution.py:14
  27.7 229.4 %all-reduce.3.cloned.1.call-start = ((), (), s32[]{:S(2)}) async-start(), calls=%async_computation.4 | async-start | bytes 3145728 | tf_op jit(solution)/shard_map/psum | solution.py:153
  29.1 26.8 %collective-permute-start = (bf16[9]{0:T(256)(128)(2,1)S(1)}, bf16[9]{0:T(256)(128)(2,1)S(1)}, u32[]{:S(2)}, u32[]{:S(2)}) collective-permute-start(bf16[9]{0:T(256)(128)(2,1)S(1)} %squeeze.75), channel_id=1, source_target_pairs={{2,0},{4,2},{6,4},{8,6},{10,8},{12,10},{14,12},{0,14},{3,1},{5,3},... | collective-permute-start | bytes 62 | tf_op jit(solution)/shard_map/ppermute | solution.py:14
  59.4 16.8 %collective-permute-start.2 = (bf16[9]{0:T(256)(128)(2,1)S(1)}, bf16[9]{0:T(256)(128)(2,1)S(1)}, u32[]{:S(2)}, u32[]{:S(2)}) collective-permute-start(bf16[9]{0:T(256)(128)(2,1)S(1)} %squeeze.77), channel_id=1, source_target_pairs={{6,0},{8,2},{10,4},{12,6},{14,8},{0,10},{2,12},{4,14},{7,1},{9,3},... | collective-permute-start | bytes 62 | tf_op jit(solution)/shard_map/ppermute | solution.py:14
  76.1 4.4 %collective-permute-start.3 = (bf16[9]{0:T(256)(128)(2,1)S(1)}, bf16[9]{0:T(256)(128)(2,1)S(1)}, u32[]{:S(2)}, u32[]{:S(2)}) collective-permute-start(bf16[9]{0:T(256)(128)(2,1)S(1)} %squeeze.78), channel_id=1, source_target_pairs={{8,0},{10,2},{12,4},{14,6},{0,8},{2,10},{4,12},{6,14},{9,1},{11,3}... | collective-permute-start | bytes 62 | tf_op jit(solution)/shard_map/ppermute | solution.py:14
  80.6 5.4 %collective-permute-start.4 = (bf16[9]{0:T(256)(128)(2,1)S(1)}, bf16[9]{0:T(256)(128)(2,1)S(1)}, u32[]{:S(2)}, u32[]{:S(2)}) collective-permute-start(bf16[9]{0:T(256)(128)(2,1)S(1)} %squeeze.79), channel_id=1, source_target_pairs={{10,0},{12,2},{14,4},{0,6},{2,8},{4,10},{6,12},{8,14},{11,1},{13,3... | collective-permute-start | bytes 62 | tf_op jit(solution)/shard_map/ppermute | solution.py:14
  86.0 5.3 %collective-permute-start.5 = (bf16[9]{0:T(256)(128)(2,1)S(1)}, bf16[9]{0:T(256)(128)(2,1)S(1)}, u32[]{:S(2)}, u32[]{:S(2)}) collective-permute-start(bf16[9]{0:T(256)(128)(2,1)S(1)} %squeeze.80), channel_id=1, source_target_pairs={{12,0},{14,2},{0,4},{2,6},{4,8},{6,10},{8,12},{10,14},{13,1},{15,3... | collective-permute-start | bytes 62 | tf_op jit(solution)/shard_map/ppermute | solution.py:14
  91.4 6.4 %collective-permute-start.6 = (bf16[9]{0:T(256)(128)(2,1)S(1)}, bf16[9]{0:T(256)(128)(2,1)S(1)}, u32[]{:S(2)}, u32[]{:S(2)}) collective-permute-start(bf16[9]{0:T(256)(128)(2,1)S(1)} %squeeze.81), channel_id=1, source_target_pairs={{14,0},{0,2},{2,4},{4,6},{6,8},{8,10},{10,12},{12,14},{15,1},{1,3}... | collective-permute-start | bytes 62 | tf_op jit(solution)/shard_map/ppermute | solution.py:14
  97.7 31.5 %collective-permute-start.11 = (bf16[9,128,128]{2,1,0:T(8,128)(2,1)S(1)}, bf16[9,128,128]{2,1,0:T(8,128)(2,1)S(1)}, u32[]{:S(2)}, u32[]{:S(2)}) collective-permute-start(bf16[9,128,128]{2,1,0:T(8,128)(2,1)S(1)} %bitcast.170), channel_id=1, source_target_pairs={{10,0},{12,2},{14,4},{0,6},{2,8},{4,10},{6,12},{8,14},{11,1},{13,3... | collective-permute-start | bytes 884744 | tf_op jit(solution)/shard_map/ppermute | solution.py:14
  103.0 26.9 %collective-permute-start.12 = (bf16[9,128,128]{2,1,0:T(8,128)(2,1)S(1)}, bf16[9,128,128]{2,1,0:T(8,128)(2,1)S(1)}, u32[]{:S(2)}, u32[]{:S(2)}) collective-permute-start(bf16[9,128,128]{2,1,0:T(8,128)(2,1)S(1)} %bitcast.169), channel_id=1, source_target_pairs={{12,0},{14,2},{0,4},{2,6},{4,8},{6,10},{8,12},{10,14},{13,1},{15,3... | collective-permute-start | bytes 884744 | tf_op jit(solution)/shard_map/ppermute | solution.py:14
  103.9 26.9 %collective-permute-start.13 = (bf16[9,128,128]{2,1,0:T(8,128)(2,1)S(1)}, bf16[9,128,128]{2,1,0:T(8,128)(2,1)S(1)}, u32[]{:S(2)}, u32[]{:S(2)}) collective-permute-start(bf16[9,128,128]{2,1,0:T(8,128)(2,1)S(1)} %bitcast.168), channel_id=1, source_target_pairs={{14,0},{0,2},{2,4},{4,6},{6,8},{8,10},{10,12},{12,14},{15,1},{1,3}... | collective-permute-start | bytes 884744 | tf_op jit(solution)/shard_map/ppermute | solution.py:14
  176.0 12.9 %collective-permute-start.14 = (bf16[9,128,128]{2,1,0:T(8,128)(2,1)S(1)}, bf16[9,128,128]{2,1,0:T(8,128)(2,1)S(1)}, u32[]{:S(2)}, u32[]{:S(2)}) collective-permute-start(bf16[9,128,128]{2,1,0:T(8,128)(2,1)S(1)} %bitcast.181), channel_id=1, source_target_pairs={{14,0},{0,2},{2,4},{4,6},{6,8},{8,10},{10,12},{12,14},{15,1},{1,3}... | collective-permute-start | bytes 884744 | tf_op jit(solution)/shard_map/ppermute | solution.py:14
  176.6 12.3 %collective-permute-start.15 = (bf16[9,128,128]{2,1,0:T(8,128)(2,1)S(1)}, bf16[9,128,128]{2,1,0:T(8,128)(2,1)S(1)}, u32[]{:S(2)}, u32[]{:S(2)}) collective-permute-start(bf16[9,128,128]{2,1,0:T(8,128)(2,1)S(1)} %bitcast.180), channel_id=1, source_target_pairs={{12,0},{14,2},{0,4},{2,6},{4,8},{6,10},{8,12},{10,14},{13,1},{15,3... | collective-permute-start | bytes 884744 | tf_op jit(solution)/shard_map/ppermute | solution.py:14
  178.1 33.7 %collective-permute-start.16 = (bf16[9,128,128]{2,1,0:T(8,128)(2,1)S(1)}, bf16[9,128,128]{2,1,0:T(8,128)(2,1)S(1)}, u32[]{:S(2)}, u32[]{:S(2)}) collective-permute-start(bf16[9,128,128]{2,1,0:T(8,128)(2,1)S(1)} %bitcast.179), channel_id=1, source_target_pairs={{10,0},{12,2},{14,4},{0,6},{2,8},{4,10},{6,12},{8,14},{11,1},{13,3... | collective-permute-start | bytes 884744 | tf_op jit(solution)/shard_map/ppermute | solution.py:14
  179.9 32.0 %collective-permute-start.17 = (bf16[9,128,128]{2,1,0:T(8,128)(2,1)S(1)}, bf16[9,128,128]{2,1,0:T(8,128)(2,1)S(1)}, u32[]{:S(2)}, u32[]{:S(2)}) collective-permute-start(bf16[9,128,128]{2,1,0:T(8,128)(2,1)S(1)} %bitcast.178), channel_id=1, source_target_pairs={{8,0},{10,2},{12,4},{14,6},{0,8},{2,10},{4,12},{6,14},{9,1},{11,3}... | collective-permute-start | bytes 884744 | tf_op jit(solution)/shard_map/ppermute | solution.py:14
  182.8 29.1 %collective-permute-start.18 = (bf16[9,128,128]{2,1,0:T(8,128)(2,1)S(1)}, bf16[9,128,128]{2,1,0:T(8,128)(2,1)S(1)}, u32[]{:S(2)}, u32[]{:S(2)}) collective-permute-start(bf16[9,128,128]{2,1,0:T(8,128)(2,1)S(1)} %bitcast.177), channel_id=1, source_target_pairs={{6,0},{8,2},{10,4},{12,6},{14,8},{0,10},{2,12},{4,14},{7,1},{9,3},... | collective-permute-start | bytes 884744 | tf_op jit(solution)/shard_map/ppermute | solution.py:14
  188.9 23.1 %collective-permute-start.19 = (bf16[9,128,128]{2,1,0:T(8,128)(2,1)S(1)}, bf16[9,128,128]{2,1,0:T(8,128)(2,1)S(1)}, u32[]{:S(2)}, u32[]{:S(2)}) collective-permute-start(bf16[9,128,128]{2,1,0:T(8,128)(2,1)S(1)} %bitcast.176), channel_id=1, source_target_pairs={{4,0},{6,2},{8,4},{10,6},{12,8},{14,10},{0,12},{2,14},{5,1},{7,3},... | collective-permute-start | bytes 884744 | tf_op jit(solution)/shard_map/ppermute | solution.py:14
  189.0 25.9 %collective-permute-start.20 = (bf16[9,128,128]{2,1,0:T(8,128)(2,1)S(1)}, bf16[9,128,128]{2,1,0:T(8,128)(2,1)S(1)}, u32[]{:S(2)}, u32[]{:S(2)}) collective-permute-start(bf16[9,128,128]{2,1,0:T(8,128)(2,1)S(1)} %bitcast.175), channel_id=1, source_target_pairs={{2,0},{4,2},{6,4},{8,6},{10,8},{12,10},{14,12},{0,14},{3,1},{5,3},... | collective-permute-start | bytes 884744 | tf_op jit(solution)/shard_map/ppermute | solution.py:14
  222.0 128.7 %reduce-scatter.2.cloned.1.call-start = ((), (), s32[]{:S(2)}) async-start(), calls=%async_computation.3 | async-start | bytes 4718592 | tf_op jit(solution)/shard_map/reduce_scatter | solution.py:130
  (20 other events, 194.4 us)
Sparse Core Ops, SparseCore 0:
  10.7 78.4 all-gather.2
  91.9 63.9 all-gather.4
  222.2 34.8 all-reduce.2
  261.0 89.6 reduce-scatter.1
where the time goes:
time: 360 us; the launch traced here: 359 us
  waiting for transfers between devices  213 us (59%)
  starting transfers between devices  50.5 us (14%)
  local copies, waits for them, and re-layouts  48 us (13%)
  other arithmetic  19.4 us (5%)
  between operations  14.3 us (4%)
  matrix products  14.2 us (4%)
    reduce_scatter x1, waiting for transfers between devices, shards(): lax.psum_scatter(partial_input, 'fsdp', scatter_dimension=1, tiled=True)  88.2 us
    ppermute x21, waiting for transfers between devices, shifted(): return lax.ppermute(block, axis, route)  82.1 us
    ppermute x21, starting transfers between devices, shifted(): return lax.ppermute(block, axis, route)  50.3 us
    psum x1, waiting for transfers between devices, shards(): lax.psum(owned_by_holder[0].astype(jnp.float32).astype(jnp.bfloat16), 'se...  24.7 us
    all_gather x1, waiting for transfers between devices, shards(): lax.all_gather(tokens, 'fsdp', axis=1, tiled=True)  17.6 us
    unnamed x55, local copies, waits for them, and re-layouts  14.3 us
  transfers between devices with their start and end apart: 25, of which 14 were waited for; matrix products, arithmetic and copies ran while one was open for 14% of the time, Pallas kernels for 0%

commit v1 on v0

v1 whole, which is shorter than its diff:
```python
import functools

import jax
import jax.numpy as jnp
from jax import lax
from jax.experimental import pallas as pl
from jax.experimental.pallas import tpu as pltpu
from jax.sharding import PartitionSpec as P

BLK = 128
SPREAD = 8
CAP = 3
KINDS = 3
PER = KINDS * CAP
VMEM_LIMIT = 56 * 1024 * 1024

F32 = jnp.float32
BF16 = jnp.bfloat16
ANY = pl.BlockSpec(memory_space=pl.ANY)
VMEM = pl.BlockSpec(memory_space=pltpu.VMEM)
SMEM = pl.BlockSpec(memory_space=pltpu.SMEM)


def params():
    return pltpu.CompilerParams(vmem_limit_bytes=VMEM_LIMIT)


def shape(dims, dtype=BF16):
    return jax.ShapeDtypeStruct(dims, dtype)


def ring_order(count):
    return [*range(0, count, 2), *range(count - 1, 0, -2)]


def ring_routes(count):
    order = ring_order(count)
    onward = [(order[i], order[(i + 1) % count]) for i in range(count)]
    return onward, [(b, a) for a, b in onward]


def shift(block, axis, distance):
    count = lax.axis_size(axis)
    return lax.ppermute(block, axis, [(i, (i + distance) % count) for i in range(count)])


def swap(block, axis):
    return lax.ppermute(block, axis, [(0, 1), (1, 0)])


def ring_gather(block, axis):
    count = lax.axis_size(axis)
    onward, back = ring_routes(count)
    order = ring_order(count)
    place = jnp.array([order.index(i) for i in range(count)], jnp.int32)[lax.axis_index(axis)]
    table = jnp.array(order, jnp.int32)
    half = block.shape[0] // 2
    pieces = [(block, lax.axis_index(axis), 0)]
    left = right = block
    for step in range(1, count // 2):
        left = lax.ppermute(left, axis, onward)
        right = lax.ppermute(right, axis, back)
        pieces.append((left, table[(place - step) % count], 0))
        pieces.append((right, table[(place + step) % count], 0))
    far = table[(place + count // 2) % count]
    pieces.append((lax.ppermute(left[:half], axis, onward), far, 0))
    pieces.append((lax.ppermute(right[half:], axis, back), far, half))
    return pieces


def pack_kernel(info, gd, ud, dd, gr, ur, dr, gate, up, down, *refs):
    own = refs[0]
    sends = refs[1:SPREAD]
    slab, ids, used = refs[SPREAD:]
    quarter = info[0]
    rows = BLK // 4
    slab[...] = jnp.zeros_like(slab)
    own[...] = jnp.zeros_like(own)
    ids[...] = jnp.zeros_like(ids)
    for kind, (dest, row_ids, blocks) in enumerate(((gd, gr, gate), (ud, ur, up), (dd, dr, down))):
        for offset in range(SPREAD):
            used[offset] = 0

        def place(j, carry, kind=kind, dest=dest, row_ids=row_ids, blocks=blocks):
            offset = dest[j]
            rank = used[offset]
            used[offset] = rank + 1
            slot = kind * CAP + rank
            start = pl.multiple_of(quarter * rows, rows)
            slab[offset, slot] = blocks[j, pl.ds(start, rows), :]
            ids[offset, pl.ds(slot, 1), :] = jnp.full((1, BLK), row_ids[j].astype(F32), F32)

            @pl.when(offset == 0)
            def _():
                own[slot] = blocks[j]

            return carry

        lax.fori_loop(0, blocks.shape[0], place, 0)
    for offset in range(1, SPREAD):
        sends[offset - 1][0:PER] = slab[offset]
        sends[offset - 1][PER] = ids[offset].astype(BF16)
    own[PER, 0:rows] = ids[0].astype(BF16)


def pack(quarter, dests, row_ids, blocks):
    rows = BLK // 4
    return pl.pallas_call(
        pack_kernel,
        out_shape=[shape((PER + 1, BLK, BLK))] + [shape((PER + 1, rows, BLK))] * (SPREAD - 1),
        in_specs=[SMEM] * 7 + [VMEM] * 3,
        out_specs=[VMEM] * SPREAD,
        scratch_shapes=[
            pltpu.VMEM((SPREAD, PER, rows, BLK), BF16),
            pltpu.VMEM((SPREAD, rows, BLK), F32),
            pltpu.SMEM((SPREAD,), jnp.int32),
        ],
        compiler_params=params(),
        name="pack",
    )(quarter, *dests, *row_ids, *blocks)


def forward_kernel(layout, tokens_here, split, info, own, w0, w1, w2, w3, *refs):
    count = len(layout)
    shards = refs[:count]
    refs = refs[count:]
    field_out, hidden_out = refs[0], refs[1]
    outs = refs[2 : 3 + 3 * split]
    field, weights, id_rows, id_ints, id_scalars, left, total, shard_sems, sems = refs[3 + 3 * split :]
    width = field.shape[2]
    per_piece = width // BLK
    t = tokens_here

    own_copies = [
        pltpu.make_async_copy(own.at[0:PER], weights.at[0], sems.at[0]),
        pltpu.make_async_copy(own.at[PER, 0 : BLK // 4], id_rows.at[0], sems.at[1]),
        pltpu.make_async_copy(w0.at[:, PER], id_rows.at[1:SPREAD], sems.at[2]),
    ]
    weight_copies = []
    for n, ref in enumerate((w0, w1, w2, w3)):
        begin = pl.multiple_of(info[1 + n] * (BLK // 4), BLK // 4)
        weight_copies.append(
            pltpu.make_async_copy(
                ref.at[:, 0:PER],
                weights.at[1:SPREAD, :, pl.ds(begin, BLK // 4), :],
                sems.at[3 + n],
            )
        )
    shard_copies = []
    for n, (first, length) in enumerate(layout):
        shard_copies.append(
            pltpu.make_async_copy(
                shards[n], field.at[info[5 + n], first : first + length], shard_sems.at[n]
            )
        )
    for copy in own_copies + shard_copies + weight_copies:
        copy.start()
    total[...] = jnp.zeros_like(total)
    for copy in own_copies[1:]:
        copy.wait()
    id_ints[...] = id_rows[:, 0:16, :].astype(F32).astype(jnp.int32)
    id_copy = pltpu.make_async_copy(id_ints, id_scalars, sems.at[7])
    id_copy.start()
    for copy in shard_copies:
        copy.wait()
    field_copy = pltpu.make_async_copy(field, field_out, sems.at[8])
    field_copy.start()
    id_copy.wait()

    def where(offset, kind, rank):
        row = id_scalars[offset, kind * CAP + rank, 0]
        return row // per_piece, pl.multiple_of((row % per_piece) * BLK, BLK)

    for kind in range(KINDS):
        first = t if kind == 2 else 0
        for offset in range(SPREAD):
            for rank in range(CAP):
                piece, column = where(offset, kind, rank)
                n = offset * CAP + rank
                left[kind, :, n * BLK : (n + 1) * BLK] = field[
                    piece, first : first + t, pl.ds(column, BLK)
                ]
    own_copies[0].wait()
    for copy in weight_copies:
        copy.wait()

    def block_group(kind):
        return weights[:, kind * CAP : (kind + 1) * CAP].reshape(SPREAD * CAP * BLK, BLK)

    gate = jnp.dot(left[0], block_group(0), preferred_element_type=F32)
    upper = jnp.dot(left[1], block_group(1), preferred_element_type=F32)
    nt = (((1,), (1,)), ((), ()))
    hidden_grad = jnp.zeros((t, BLK), F32)
    for offset in range(SPREAD):
        for rank in range(CAP):
            n = offset * CAP + rank
            hidden_grad = hidden_grad + lax.dot_general(
                left[2, :, n * BLK : (n + 1) * BLK],
                weights[offset, 2 * CAP + rank],
                nt,
                preferred_element_type=F32,
            )
    sigma = 1.0 / (1.0 + jnp.exp(-gate))
    hidden = (gate * sigma * upper).astype(BF16)
    gate_d = (hidden_grad * upper * sigma * (1.0 + gate * (1.0 - sigma))).astype(BF16)
    up_d = (hidden_grad * gate * sigma).astype(BF16)
    hidden_out[0] = gate_d
    hidden_out[1] = up_d
    hidden_out[2] = hidden
    for kind, grad in ((0, gate_d), (1, up_d)):
        for offset in range(SPREAD):
            terms = lax.dot_general(
                grad,
                weights[offset, kind * CAP : (kind + 1) * CAP].reshape(CAP * BLK, BLK),
                nt,
                preferred_element_type=F32,
            )
            for rank in range(CAP):
                piece, column = where(offset, kind, rank)
                total[piece, :, pl.ds(column, BLK)] += terms[:, rank * BLK : (rank + 1) * BLK]
    if split:
        side = info[0]
        send_a, send_b, keep_a, keep_b = outs
        h = t // 2
        for z in range(send_a.shape[0]):
            away = total[2 * z + 1 - side].astype(BF16)
            here = total[2 * z + side].astype(BF16)
            send_a[z] = away[:h]
            send_b[z] = away[h:]
            keep_a[z] = here[:h]
            keep_b[z] = here[h:]
    else:
        outs[0][...] = total[...].astype(BF16)
    field_copy.wait()


def forward(info, own, quarters, pieces, split, piece_count):
    layout = [(first, block.shape[0]) for block, _, first in pieces]
    t = pieces[0][0].shape[0] // 2
    width = pieces[0][0].shape[1]
    if split:
        outs = [shape((piece_count // 2, t // 2, width))] * 4
    else:
        outs = [shape((piece_count, t, width))]
    field = (piece_count, 2 * t, width)
    return pl.pallas_call(
        functools.partial(forward_kernel, layout, t, int(split)),
        out_shape=[shape(field), shape((KINDS, t, BLK))] + outs,
        in_specs=[SMEM] + [ANY] * (5 + len(pieces)),
        out_specs=[ANY] + [VMEM] * (1 + len(outs)),
        scratch_shapes=[
            pltpu.VMEM(field, BF16),
            pltpu.VMEM((SPREAD, PER, BLK, BLK), BF16),
            pltpu.VMEM((SPREAD, BLK // 4, BLK), BF16),
            pltpu.VMEM((SPREAD, 16, BLK), jnp.int32),
            pltpu.SMEM((SPREAD, 16, BLK), jnp.int32),
            pltpu.VMEM((KINDS, t, SPREAD * CAP * BLK), BF16),
            pltpu.VMEM((piece_count, t, width), F32),
            pltpu.SemaphoreType.DMA((len(pieces),)),
            pltpu.SemaphoreType.DMA((9,)),
        ],
        compiler_params=params(),
        name="forward",
    )(info, own, *quarters, *[block for block, _, _ in pieces])


def pair_kernel(info, keep, got, here, one, two, three):
    z = info[0]
    for step, ref in enumerate((here, one, two, three)):
        at = lax.rem(z + step, keep.shape[0])
        ref[...] = (keep[at].astype(F32) + got[at].astype(F32)).astype(BF16)


def pair(z, keep, got):
    piece = shape(keep.shape[1:])
    return pl.pallas_call(
        pair_kernel,
        out_shape=[piece] * 4,
        in_specs=[SMEM, VMEM, VMEM],
        out_specs=[VMEM] * 4,
        compiler_params=params(),
        name="pair",
    )(z, keep, got)


def grads_kernel(layout, info, gd, ud, dd, gr, ur, dr, field, *refs):
    count = len(layout)
    arrived = refs[:count]
    out, columns, sems = refs[count:]
    t = field.shape[1] // 2
    per_piece = field.shape[2] // BLK
    copies = []
    for n, (first, length) in enumerate(layout):
        copies.append(
            pltpu.make_async_copy(
                arrived[n], columns.at[info[n], first : first + length], sems.at[n]
            )
        )
    for copy in copies:
        copy.start()
    for copy in copies:
        copy.wait()
    tn = (((0,), (0,)), ((), ()))
    slots = gd.shape[0]
    for kind, (dest, row_ids) in enumerate(((gd, gr), (ud, ur), (dd, dr))):
        first = t if kind == 2 else 0

        def one(j, carry, kind=kind, dest=dest, row_ids=row_ids, first=first):
            row = row_ids[j]
            column = pl.multiple_of((row % per_piece) * BLK, BLK)
            part = field[row // per_piece, first : first + t, pl.ds(column, BLK)]
            side = columns[dest[j], kind * t : (kind + 1) * t, :]
            pair_of = (side, part) if kind == 2 else (part, side)
            out[kind * slots + j] = lax.dot_general(
                *pair_of, tn, preferred_element_type=F32
            ).astype(BF16)
            return carry

        lax.fori_loop(0, slots, one, 0, unroll=4)


def grads(info, dests, row_ids, field, pieces):
    layout = [(first, block.shape[0]) for block, _, first in pieces]
    rows = pieces[0][0].shape[0]
    slots = dests[0].shape[0]
    return pl.pallas_call(
        functools.partial(grads_kernel, layout),
        out_shape=shape((KINDS * slots, BLK, BLK)),
        in_specs=[SMEM] * 7 + [VMEM] + [ANY] * len(pieces),
        out_specs=VMEM,
        scratch_shapes=[
            pltpu.VMEM((SPREAD, rows, BLK), BF16),
            pltpu.SemaphoreType.DMA((len(pieces),)),
        ],
        compiler_params=params(),
        name="grads",
    )(info, *dests, *row_ids, field, *[block for block, _, _ in pieces])


def shards(
    tokens,
    cotangent,
    gate_blocks,
    up_blocks,
    down_blocks,
    gate_dest,
    up_dest,
    down_dest,
    gate_rows,
    up_rows,
    down_rows,
):
    count = lax.axis_size("fsdp")
    me = lax.axis_index("fsdp")
    group = lax.axis_index("groups")
    section = lax.axis_index("section")
    grid = count == SPREAD and tokens.shape[1] % BLK == 0
    t = tokens.shape[0]
    dests = [target[:, 0] for target in (gate_dest, up_dest, down_dest)]
    row_ids = [gate_rows, up_rows, down_rows]

    both = jnp.concatenate([tokens, cotangent], axis=0)
    if grid:
        pieces = ring_gather(both, "fsdp")
        piece_count = count
    else:
        pieces = [(lax.all_gather(both, "fsdp", axis=1, tiled=True), jnp.int32(0), 0)]
        piece_count = 1

    quarter = jnp.reshape(2 * group + section, (1,)).astype(jnp.int32)
    own, *sends = pack(quarter, dests, row_ids, (gate_blocks, up_blocks, down_blocks))
    mine = jnp.stack([shift(block, "fsdp", -d) for d, block in enumerate(sends, 1)], axis=0)
    across = swap(mine, "groups")
    beside = swap(mine, "section")
    diagonal = swap(across, "section")
    quarters = (mine, beside, across, diagonal)
    order_of_quarters = [
        2 * group + section,
        2 * group + 1 - section,
        2 * (1 - group) + section,
        2 * (1 - group) + 1 - section,
    ]
    info = jnp.stack(
        [me % 2, *order_of_quarters, *[source for _, source, _ in pieces]]
    ).astype(jnp.int32)
    field, columns, *partial_input = forward(info, own, quarters, pieces, grid, piece_count)

    flat = columns.reshape(KINDS * t, BLK)
    if grid:
        arrived = [
            (block, (me - source) % count, first)
            for block, source, first in ring_gather(flat, "fsdp")
        ]
    else:
        arrived = [(flat, jnp.int32(0), 0)] + [
            (shift(flat, "fsdp", d), jnp.int32(d), 0) for d in range(1, SPREAD)
        ]
    offsets = jnp.stack([offset for _, offset, _ in arrived]).astype(jnp.int32)
    part = grads(offsets, dests, row_ids, field, arrived)
    other = swap(part, "section")
    summed = part.astype(F32) + other.astype(F32)
    slots = gate_blocks.shape[0]
    gate_grad, up_grad, down_grad = (
        summed[kind * slots : (kind + 1) * slots] for kind in range(KINDS)
    )

    if grid:
        beside_x = [(i, i ^ 1) for i in range(count)]
        along_z = [
            [(i, (i + 2 * step) % count) for i in range(count)] for step in range(1, count // 2)
        ]
        z = jnp.reshape(me // 2, (1,)).astype(jnp.int32)
        send_a, send_b, keep_a, keep_b = partial_input
        halves = []
        for send, keep in ((send_a, keep_a), (send_b, keep_b)):
            got = lax.ppermute(send, "fsdp", beside_x)
            here, *away = pair(z, keep, got)
            result = here.astype(F32)
            for block, route in zip(away, along_z, strict=True):
                result = result + lax.ppermute(block, "fsdp", route).astype(F32)
            halves.append(result.astype(BF16))
        input_grad = jnp.concatenate(halves, axis=0)
    else:
        input_grad = lax.psum_scatter(
            partial_input[0].reshape(t, -1), "fsdp", scatter_dimension=1, tiled=True
        )
    return input_grad, gate_grad, up_grad, down_grad


def solution(mesh):
    return jax.shard_map(
        shards,
        mesh=mesh,
        in_specs=(
            P(("groups", "section"), "fsdp"),
            P(("groups", "section"), "fsdp"),
            P("fsdp", None, None),
            P("fsdp", None, None),
            P("fsdp", None, None),
            P("fsdp", None),
            P("fsdp", None),
            P("fsdp", None),
            P("fsdp"),
            P("fsdp"),
            P("fsdp"),
        ),
        out_specs=(
            P(("groups", "section"), "fsdp"),
            P(("groups", "fsdp"), None, None),
            P(("groups", "fsdp"), None, None),
            P(("groups", "fsdp"), None, None),
        ),
        check_vma=False,
    )
```

time: 360 us -> 165 us (0.46)
  waiting for transfers between devices: 213 us -> 61.2 us
  local copies, waits for them, and re-layouts: 48 us -> 16.1 us
  Pallas kernels: 0 us -> 23.9 us
  other arithmetic: 19.4 us -> 3.26 us
  matrix products: 14.2 us -> 0 us
  between operations: 14.3 us -> 10.2 us
    reduce_scatter x1 -> x0, waiting for transfers between devices: 88.2 us -> none  [shards(): lax.psum_scatter(partial_input, 'fsdp', scatter_dimension=1, tiled=True)]
    psum x1 -> x0, waiting for transfers between devices: 24.7 us -> none  [shards(): lax.psum(owned_by_holder[0].astype(jnp.float32).astype(jnp.bfloat16), 'se...]
    pallas_call x0 -> x5, Pallas kernels: none -> 23.9 us  [the longest x1 9.29 us: forward(): pl.pallas_call(functools.partial(forward_kernel, layout, t, int(split)),...]
    ppermute x21 -> x35, waiting for transfers between devices: 82.1 us -> 61.2 us  [the longest x6 22.5 us: ring_gather(): right = lax.ppermute(right, axis, back)]
    all_gather x2 -> x0, waiting for transfers between devices: 17.6 us -> none  [the longest x1 17.6 us: shards(): lax.all_gather(tokens, 'fsdp', axis=1, tiled=True)]
    dot_general x15 -> x0, matrix products: 14.2 us -> none  [the longest x2 3.63 us: row_sum(): jnp.einsum('tsk,sr->trk', high_part, onehot, preferred_element_type=jnp.f...]
    unnamed x55 -> x47, local copies, waits for them, and re-layouts: 14.3 us -> 2.49 us
    gather x6 -> x0, local copies, waits for them, and re-layouts: 10.9 us -> none  [the longest x1 3.14 us: shards(): cot_down = cotan_grid[:, down_ids, :]]
  transfers between devices with their start and end apart: 25 -> 35, of which waited for: 14 -> 16; matrix products, arithmetic and copies ran while one was open for 14% -> 10% of each run, Pallas kernels for 0% -> 2%
where the time goes in v1:
time: 165 us; the launch traced here: 164 us
  waiting for transfers between devices  61.2 us (37%)
  starting transfers between devices  49.4 us (30%)
  Pallas kernels  23.9 us (14%)
  local copies, waits for them, and re-layouts  16.1 us (10%)
  between operations  10.2 us (6%)
  other arithmetic  3.26 us (2%)
    ppermute x6, waiting for transfers between devices, ring_gather(): right = lax.ppermute(right, axis, back)  22.5 us
    ppermute x2, waiting for transfers between devices, shards(): got = lax.ppermute(send, 'fsdp', beside_x)  17.2 us
    ppermute x7, waiting for transfers between devices, shift(): lax.ppermute(block, axis, [(i, (i + distance) % count) for i in range(cou...  14.9 us
    ppermute x7, starting transfers between devices, shift(): lax.ppermute(block, axis, [(i, (i + distance) % count) for i in range(cou...  14.6 us
    ppermute x6, starting transfers between devices, ring_gather(): right = lax.ppermute(right, axis, back)  13.1 us
    ppermute x6, starting transfers between devices, shards(): result = result + lax.ppermute(block, 'fsdp', route).astype(F32)  10.1 us
    pallas_call x1, Pallas kernels, forward(): pl.pallas_call(functools.partial(forward_kernel, layout, t, int(split)),...  9.29 us
    pallas_call x1, Pallas kernels, grads(): pl.pallas_call(functools.partial(grads_kernel, layout), out_shape=shape((...  7.33 us
  transfers between devices with their start and end apart: 35, of which 16 were waited for; matrix products, arithmetic and copies ran while one was open for 10% of the time, Pallas kernels for 2%

profile of v1, /device:TPU:0, one launch (start us, length us, event | category | flops | bytes accessed | tf_op | source)
XLA Modules:
  0.0 164.0 jit_solution(12052546119212870161)
XLA Ops:
  0.6 3.2 %pack.1 = (bf16[10,128,128]{2,1,0:T(8,128)(2,1)}, bf16[10,32,128]{2,1,0:T(8,128)(2,1)}, bf16[10,32,128]{2,1,0:T(8,128)(2,1)}, bf16[10,32,128]{2,1,0:T(8,128)(2,1...) custom-call(s32[1]{0:T(128)} %bitcast.2.info, ...), custom_call_target="tpu_custom_call" | custom-call | tf_op jit(solution)/shard_map/pack/pallas_call | solution.py:108
  3.9 6.0 %collective-permute-start = (bf16[10,32,128]{2,1,0:T(8,128)(2,1)}, bf16[10,32,128]{2,1,0:T(8,128)(2,1)S(1)}, u32[]{:S(2)}, u32[]{:S(2)}) collective-permute-start(bf16[10,32,128]{2,1,0:T(8,128)(2,1)} %get-tuple-element.27), channel_id=1, source_target_pairs={{0,14},{2,0},{4,2},{6,4},{8,6},{10,8},{12,10},{14,12},{1,15},{3,1}... | collective-permute-start | bytes 245768 | tf_op jit(solution)/shard_map/ppermute | solution.py:44
  14.4 3.0 %collective-permute-start.3 = (bf16[10,32,128]{2,1,0:T(8,128)(2,1)}, bf16[10,32,128]{2,1,0:T(8,128)(2,1)S(1)}, u32[]{:S(2)}, u32[]{:S(2)}) collective-permute-start(bf16[10,32,128]{2,1,0:T(8,128)(2,1)} %get-tuple-element.30), channel_id=1, source_target_pairs={{0,8},{2,10},{4,12},{6,14},{8,0},{10,2},{12,4},{14,6},{1,9},{3,11}... | collective-permute-start | bytes 245768 | tf_op jit(solution)/shard_map/ppermute | solution.py:44
  17.4 10.9 %collective-permute-done.1 = bf16[10,32,128]{2,1,0:T(8,128)(2,1)S(1)} collective-permute-done((bf16[10,32,128]{2,1,0:T(8,128)(2,1)}, bf16[10,32,128]{2,1,0:T(8,128)(2,1)S(1)}, u32[]{:S(2)}, u32[]{:S(2)}) %collective-permute-start.1) | collective-permute-done | bytes 81952 | tf_op jit(solution)/shard_map/ppermute | solution.py:44
  30.0 3.2 %collective-permute-start.5 = (bf16[10,32,128]{2,1,0:T(8,128)(2,1)}, bf16[10,32,128]{2,1,0:T(8,128)(2,1)S(1)}, u32[]{:S(2)}, u32[]{:S(2)}) collective-permute-start(bf16[10,32,128]{2,1,0:T(8,128)(2,1)} %get-tuple-element.32), channel_id=1, source_target_pairs={{0,4},{2,6},{4,8},{6,10},{8,12},{10,14},{12,0},{14,2},{1,5},{3,7},... | collective-permute-start | bytes 245768 | tf_op jit(solution)/shard_map/ppermute | solution.py:44
  36.5 5.2 %collective-permute-start.13 = (bf16[256,1024]{1,0:T(8,128)(2,1)S(1)}, bf16[256,1024]{1,0:T(8,128)(2,1)S(1)}, u32[]{:S(2)}, u32[]{:S(2)}) collective-permute-start(bf16[256,1024]{1,0:T(8,128)(2,1)S(1)} %collective-permute-done.11.refs_2_), channel_id=1, source_target_pairs={{4,0},{8,4},{12,8},{14,12},{10,14},{6,10},{2,6},{0,2},{5,1},{9,5},... | collective-permute-start | bytes 1572872 | tf_op jit(solution)/shard_map/ppermute | solution.py:62
  44.4 6.1 %collective-permute-done.13.refs_4_ = bf16[256,1024]{1,0:T(8,128)(2,1)S(1)} collective-permute-done((bf16[256,1024]{1,0:T(8,128)(2,1)S(1)}, bf16[256,1024]{1,0:T(8,128)(2,1)S(1)}, u32[]{:S(2)}, u32[]{:S(2)}) %collective-permute-start.13) | collective-permute-done | bytes 524320 | tf_op jit(solution)/shard_map/ppermute | solution.py:62
  50.4 2.5 %collective-permute-start.15 = (bf16[256,1024]{1,0:T(8,128)(2,1)S(1)}, bf16[256,1024]{1,0:T(8,128)(2,1)S(1)}, u32[]{:S(2)}, u32[]{:S(2)}) collective-permute-start(bf16[256,1024]{1,0:T(8,128)(2,1)S(1)} %collective-permute-done.13.refs_4_), channel_id=1, source_target_pairs={{4,0},{8,4},{12,8},{14,12},{10,14},{6,10},{2,6},{0,2},{5,1},{9,5},... | collective-permute-start | bytes 1572872 | tf_op jit(solution)/shard_map/ppermute | solution.py:62
  53.7 8.1 %collective-permute-done.15.refs_6_ = bf16[256,1024]{1,0:T(8,128)(2,1)S(1)} collective-permute-done((bf16[256,1024]{1,0:T(8,128)(2,1)S(1)}, bf16[256,1024]{1,0:T(8,128)(2,1)S(1)}, u32[]{:S(2)}, u32[]{:S(2)}) %collective-permute-start.15) | collective-permute-done | bytes 524320 | tf_op jit(solution)/shard_map/ppermute | solution.py:62
  62.6 2.5 %collective-permute-start.17 = (bf16[128,1024]{1,0:T(8,128)(2,1)}, bf16[128,1024]{1,0:T(8,128)(2,1)S(1)}, u32[]{:S(2)}, u32[]{:S(2)}) collective-permute-start(bf16[128,1024]{1,0:T(8,128)(2,1)} %slice.29), channel_id=1, source_target_pairs={{4,0},{8,4},{12,8},{14,12},{10,14},{6,10},{2,6},{0,2},{5,1},{9,5},... | collective-permute-start | bytes 786440 | tf_op jit(solution)/shard_map/ppermute | solution.py:67
  73.4 5.8 %stack.77.info = s32[14]{0:T(128)} concatenate(s32[1]{0:T(128)} %bitcast.1, s32[1]{0:T(128)} %bitcast.2.info, s32[1]{0:T(128)} %bitcast.3, s32[1]{0:T(128)} %bitcast.4, s32[1]{0:T(128)} %bitcast.5, s32[1]{0:T(128)} %bitcast.6, s32[1]{0:T(128)} %get-tuple-element.56, s32[1]{0:T(128)} %get-tuple-element.55, s32[1]{0:T(128)} %get-tuple-element.54, s32[1]{0:T(128)} %get-tuple-element.53, ...), dimensions={0} | concatenate | bytes 112 | tf_op jit(solution)/shard_map/stack | solution.py:383
  80.1 9.3 %forward.1 = (bf16[8,256,1024]{2,1,0:T(8,128)(2,1)}, bf16[3,128,128]{2,1,0:T(8,128)(2,1)}, bf16[4,64,1024]{2,1,0:T(8,128)(2,1)}, bf16[4,64,1024]{2,1,0:T(8,128)(...) custom-call(s32[14]{0:T(128)} %stack.77.info, bf16[10,128,128]{2,1,0:T(8,128)(2,1)} %get-tuple-element.26.own, ...), custom_call_target="tpu_custom_call" | custom-call | tf_op jit(solution)/shard_map/forward/pallas_call | solution.py:246
  89.4 2.1 %collective-permute-start.27 = (bf16[384,128]{1,0:T(8,128)(2,1)}, bf16[384,128]{1,0:T(8,128)(2,1)S(1)}, u32[]{:S(2)}, u32[]{:S(2)}) collective-permute-start(bf16[384,128]{1,0:T(8,128)(2,1)} %bitcast.46), channel_id=1, source_target_pairs={{4,0},{8,4},{12,8},{14,12},{10,14},{6,10},{2,6},{0,2},{5,1},{9,5},... | collective-permute-start | bytes 294920 | tf_op jit(solution)/shard_map/ppermute | solution.py:62
  91.4 3.2 %collective-permute-done.27.refs_2_ = bf16[384,128]{1,0:T(8,128)(2,1)S(1)} collective-permute-done((bf16[384,128]{1,0:T(8,128)(2,1)}, bf16[384,128]{1,0:T(8,128)(2,1)S(1)}, u32[]{:S(2)}, u32[]{:S(2)}) %collective-permute-start.27) | collective-permute-done | bytes 98336 | tf_op jit(solution)/shard_map/ppermute | solution.py:62
  96.7 2.6 %collective-permute-done.29.refs_4_ = bf16[384,128]{1,0:T(8,128)(2,1)S(1)} collective-permute-done((bf16[384,128]{1,0:T(8,128)(2,1)S(1)}, bf16[384,128]{1,0:T(8,128)(2,1)S(1)}, u32[]{:S(2)}, u32[]{:S(2)}) %collective-permute-start.29) | collective-permute-done | bytes 98336 | tf_op jit(solution)/shard_map/ppermute | solution.py:62
  101.3 2.6 %collective-permute-done.31.refs_6_ = bf16[384,128]{1,0:T(8,128)(2,1)S(1)} collective-permute-done((bf16[384,128]{1,0:T(8,128)(2,1)S(1)}, bf16[384,128]{1,0:T(8,128)(2,1)S(1)}, u32[]{:S(2)}, u32[]{:S(2)}) %collective-permute-start.31) | collective-permute-done | bytes 98336 | tf_op jit(solution)/shard_map/ppermute | solution.py:62
  111.8 7.3 %grads.1 = bf16[48,128,128]{2,1,0:T(8,128)(2,1)} custom-call(s32[9]{0:T(128)} %stack.93.info, s32[16]{0:T(128)} %bitcast.50, s32[16]{0:T(128)} %bitcast.52, s32[16]{0:T(128)} %bitcast.54, s32[16]{0:T(128)} %gr.3, s32[16]{0:T(128)} %ur.3, s32[16]{0:T(128)} %dr.3, bf16[8,256,1024]{2,1,0:T(8,128)(2,1)} %get-tuple-element.46.field, bf16[384,128]{1,0:T(8,128)(2,1)} %bitcast.48, ...), custom_call_target="tpu_custom_call" | custom-call | tf_op jit(solution)/shard_map/grads/pallas_call | solution.py:326
  121.4 13.0 %collective-permute-done.18.got = bf16[4,64,1024]{2,1,0:T(8,128)(2,1)} collective-permute-done((bf16[4,64,1024]{2,1,0:T(8,128)(2,1)}, bf16[4,64,1024]{2,1,0:T(8,128)(2,1)}, u32[]{:S(2)}, u32[]{:S(2)}) %collective-permute-start.18) | collective-permute-done | bytes 524320 | tf_op jit(solution)/shard_map/ppermute | solution.py:416
  134.4 2.0 %pair.2 = (bf16[64,1024]{1,0:T(8,128)(2,1)}, bf16[64,1024]{1,0:T(8,128)(2,1)}, bf16[64,1024]{1,0:T(8,128)(2,1)}, bf16[64,1024]{1,0:T(8,128)(2,1)}) custom-call(s32[1]{0:T(128)} %bitcast.info, bf16[4,64,1024]{2,1,0:T(8,128)(2,1)} %get-tuple-element.34.keep, bf16[4,64,1024]{2,1,0:T(8,128)(2,1)} %collective-permute-done.18.got), custom_call_target="tpu_custom_call" | custom-call | tf_op jit(solution)/shard_map/pair/pallas_call | solution.py:276
  136.7 3.4 %collective-permute-start.20 = (bf16[64,1024]{1,0:T(8,128)(2,1)}, bf16[64,1024]{1,0:T(8,128)(2,1)S(1)}, u32[]{:S(2)}, u32[]{:S(2)}) collective-permute-start(bf16[64,1024]{1,0:T(8,128)(2,1)} %get-tuple-element.38), channel_id=1, source_target_pairs={{0,8},{2,10},{4,12},{6,14},{8,0},{10,2},{12,4},{14,6},{1,9},{3,11}... | collective-permute-start | bytes 393224 | tf_op jit(solution)/shard_map/ppermute | solution.py:420
  141.0 4.1 %collective-permute-done.22.got = bf16[4,64,1024]{2,1,0:T(8,128)(2,1)} collective-permute-done((bf16[4,64,1024]{2,1,0:T(8,128)(2,1)}, bf16[4,64,1024]{2,1,0:T(8,128)(2,1)}, u32[]{:S(2)}, u32[]{:S(2)}) %collective-permute-start.22) | collective-permute-done | bytes 524320 | tf_op jit(solution)/shard_map/ppermute | solution.py:416
  147.6 3.4 %collective-permute-start.24 = (bf16[64,1024]{1,0:T(8,128)(2,1)}, bf16[64,1024]{1,0:T(8,128)(2,1)S(1)}, u32[]{:S(2)}, u32[]{:S(2)}) collective-permute-start(bf16[64,1024]{1,0:T(8,128)(2,1)} %get-tuple-element.44), channel_id=1, source_target_pairs={{0,8},{2,10},{4,12},{6,14},{8,0},{10,2},{12,4},{14,6},{1,9},{3,11}... | collective-permute-start | bytes 393224 | tf_op jit(solution)/shard_map/ppermute | solution.py:420
  153.7 2.1 %collective-permute-done.23 = bf16[64,1024]{1,0:T(8,128)(2,1)S(1)} collective-permute-done((bf16[64,1024]{1,0:T(8,128)(2,1)}, bf16[64,1024]{1,0:T(8,128)(2,1)S(1)}, u32[]{:S(2)}, u32[]{:S(2)}) %collective-permute-start.23) | collective-permute-done | bytes 131104 | tf_op jit(solution)/shard_map/ppermute | solution.py:420
  155.7 4.3 %collective-permute-done.24 = bf16[64,1024]{1,0:T(8,128)(2,1)S(1)} collective-permute-done((bf16[64,1024]{1,0:T(8,128)(2,1)}, bf16[64,1024]{1,0:T(8,128)(2,1)S(1)}, u32[]{:S(2)}, u32[]{:S(2)}) %collective-permute-start.24) | collective-permute-done | bytes 131104 | tf_op jit(solution)/shard_map/ppermute | solution.py:420
  (113 shorter events, 38.1 us)
Async XLA Ops:
  3.9 10.5 %collective-permute-start = (bf16[10,32,128]{2,1,0:T(8,128)(2,1)}, bf16[10,32,128]{2,1,0:T(8,128)(2,1)S(1)}, u32[]{:S(2)}, u32[]{:S(2)}) collective-permute-start(bf16[10,32,128]{2,1,0:T(8,128)(2,1)} %get-tuple-element.27), channel_id=1, source_target_pairs={{0,14},{2,0},{4,2},{6,4},{8,6},{10,8},{12,10},{14,12},{1,15},{3,1}... | collective-permute-start | bytes 245768 | tf_op jit(solution)/shard_map/ppermute | solution.py:44
  11.9 24.6 %collective-permute-start.11 = (bf16[256,1024]{1,0:T(8,128)(2,1)S(1)}, bf16[256,1024]{1,0:T(8,128)(2,1)S(1)}, u32[]{:S(2)}, u32[]{:S(2)}) collective-permute-start(bf16[256,1024]{1,0:T(8,128)(2,1)S(1)} %constant_dynamic-update-slice_fusion.refs_0_), channel_id=1, source_target_pairs={{4,0},{8,4},{12,8},{14,12},{10,14},{6,10},{2,6},{0,2},{5,1},{9,5},... | collective-permute-start | bytes 1572872 | tf_op jit(solution)/shard_map/ppermute | solution.py:62
  11.9 29.8 %collective-permute-start.10 = (bf16[256,1024]{1,0:T(8,128)(2,1)S(1)}, bf16[256,1024]{1,0:T(8,128)(2,1)S(1)}, u32[]{:S(2)}, u32[]{:S(2)}) collective-permute-start(bf16[256,1024]{1,0:T(8,128)(2,1)S(1)} %constant_dynamic-update-slice_fusion.refs_0_), channel_id=1, source_target_pairs={{0,4},{4,8},{8,12},{12,14},{14,10},{10,6},{6,2},{2,0},{1,5},{5,9},... | collective-permute-start | bytes 1572872 | tf_op jit(solution)/shard_map/ppermute | solution.py:61
  13.9 14.4 %collective-permute-start.1 = (bf16[10,32,128]{2,1,0:T(8,128)(2,1)}, bf16[10,32,128]{2,1,0:T(8,128)(2,1)S(1)}, u32[]{:S(2)}, u32[]{:S(2)}) collective-permute-start(bf16[10,32,128]{2,1,0:T(8,128)(2,1)} %get-tuple-element.28), channel_id=1, source_target_pairs={{0,12},{2,14},{4,0},{6,2},{8,4},{10,6},{12,8},{14,10},{1,13},{3,15... | collective-permute-start | bytes 245768 | tf_op jit(solution)/shard_map/ppermute | solution.py:44
  14.4 15.6 %collective-permute-start.2 = (bf16[10,32,128]{2,1,0:T(8,128)(2,1)}, bf16[10,32,128]{2,1,0:T(8,128)(2,1)S(1)}, u32[]{:S(2)}, u32[]{:S(2)}) collective-permute-start(bf16[10,32,128]{2,1,0:T(8,128)(2,1)} %get-tuple-element.29), channel_id=1, source_target_pairs={{0,10},{2,12},{4,14},{6,0},{8,2},{10,4},{12,6},{14,8},{1,11},{3,13... | collective-permute-start | bytes 245768 | tf_op jit(solution)/shard_map/ppermute | solution.py:44
  14.4 19.3 %collective-permute-start.3 = (bf16[10,32,128]{2,1,0:T(8,128)(2,1)}, bf16[10,32,128]{2,1,0:T(8,128)(2,1)S(1)}, u32[]{:S(2)}, u32[]{:S(2)}) collective-permute-start(bf16[10,32,128]{2,1,0:T(8,128)(2,1)} %get-tuple-element.30), channel_id=1, source_target_pairs={{0,8},{2,10},{4,12},{6,14},{8,0},{10,2},{12,4},{14,6},{1,9},{3,11}... | collective-permute-start | bytes 245768 | tf_op jit(solution)/shard_map/ppermute | solution.py:44
  33.7 9.0 %collective-permute-start.6 = (bf16[10,32,128]{2,1,0:T(8,128)(2,1)}, bf16[10,32,128]{2,1,0:T(8,128)(2,1)S(1)}, u32[]{:S(2)}, u32[]{:S(2)}) collective-permute-start(bf16[10,32,128]{2,1,0:T(8,128)(2,1)} %get-tuple-element.33), channel_id=1, source_target_pairs={{0,2},{2,4},{4,6},{6,8},{8,10},{10,12},{12,14},{14,0},{1,3},{3,5},... | collective-permute-start | bytes 245768 | tf_op jit(solution)/shard_map/ppermute | solution.py:44
  36.5 14.0 %collective-permute-start.13 = (bf16[256,1024]{1,0:T(8,128)(2,1)S(1)}, bf16[256,1024]{1,0:T(8,128)(2,1)S(1)}, u32[]{:S(2)}, u32[]{:S(2)}) collective-permute-start(bf16[256,1024]{1,0:T(8,128)(2,1)S(1)} %collective-permute-done.11.refs_2_), channel_id=1, source_target_pairs={{4,0},{8,4},{12,8},{14,12},{10,14},{6,10},{2,6},{0,2},{5,1},{9,5},... | collective-permute-start | bytes 1572872 | tf_op jit(solution)/shard_map/ppermute | solution.py:62
  41.7 11.5 %collective-permute-start.12 = (bf16[256,1024]{1,0:T(8,128)(2,1)S(1)}, bf16[256,1024]{1,0:T(8,128)(2,1)S(1)}, u32[]{:S(2)}, u32[]{:S(2)}) collective-permute-start(bf16[256,1024]{1,0:T(8,128)(2,1)S(1)} %collective-permute-done.10.refs_1_), channel_id=1, source_target_pairs={{0,4},{4,8},{8,12},{12,14},{14,10},{10,6},{6,2},{2,0},{1,5},{5,9},... | collective-permute-start | bytes 1572872 | tf_op jit(solution)/shard_map/ppermute | solution.py:61
  42.8 10.4 %collective-permute-start.8 = (bf16[7,10,32,128]{3,2,1,0:T(8,128)(2,1)S(1)}, bf16[7,10,32,128]{3,2,1,0:T(8,128)(2,1)S(1)}, u32[]{:S(2)}, u32[]{:S(2)}) collective-permute-start(bf16[7,10,32,128]{3,2,1,0:T(8,128)(2,1)S(1)} %bitcast_dynamic-update-slice_fusion.w0), channel_id=1, source_target_pairs={{0,16},{16,0},{1,17},{17,1},{2,18},{18,2},{3,19},{19,3},{4,20},{20... | collective-permute-start | bytes 1720328 | tf_op jit(solution)/shard_map/ppermute | solution.py:48
  50.4 11.3 %collective-permute-start.15 = (bf16[256,1024]{1,0:T(8,128)(2,1)S(1)}, bf16[256,1024]{1,0:T(8,128)(2,1)S(1)}, u32[]{:S(2)}, u32[]{:S(2)}) collective-permute-start(bf16[256,1024]{1,0:T(8,128)(2,1)S(1)} %collective-permute-done.13.refs_4_), channel_id=1, source_target_pairs={{4,0},{8,4},{12,8},{14,12},{10,14},{6,10},{2,6},{0,2},{5,1},{9,5},... | collective-permute-start | bytes 1572872 | tf_op jit(solution)/shard_map/ppermute | solution.py:62
  53.1 11.9 %collective-permute-start.14 = (bf16[256,1024]{1,0:T(8,128)(2,1)S(1)}, bf16[256,1024]{1,0:T(8,128)(2,1)S(1)}, u32[]{:S(2)}, u32[]{:S(2)}) collective-permute-start(bf16[256,1024]{1,0:T(8,128)(2,1)S(1)} %collective-permute-done.12.refs_3_), channel_id=1, source_target_pairs={{0,4},{4,8},{8,12},{12,14},{14,10},{10,6},{6,2},{2,0},{1,5},{5,9},... | collective-permute-start | bytes 1572872 | tf_op jit(solution)/shard_map/ppermute | solution.py:61
  53.1 26.0 %collective-permute-start.7 = (bf16[7,10,32,128]{3,2,1,0:T(8,128)(2,1)S(1)}, bf16[7,10,32,128]{3,2,1,0:T(8,128)(2,1)S(1)}, u32[]{:S(2)}, u32[]{:S(2)}) collective-permute-start(bf16[7,10,32,128]{3,2,1,0:T(8,128)(2,1)S(1)} %bitcast_dynamic-update-slice_fusion.w0), channel_id=1, source_target_pairs={{0,1},{1,0},{2,3},{3,2},{4,5},{5,4},{6,7},{7,6},{8,9},{9,8},{10,11... | collective-permute-start | bytes 1720328 | tf_op jit(solution)/shard_map/ppermute | solution.py:48
  53.2 26.0 %collective-permute-start.9 = (bf16[7,10,32,128]{3,2,1,0:T(8,128)(2,1)S(1)}, bf16[7,10,32,128]{3,2,1,0:T(8,128)(2,1)}, u32[]{:S(2)}, u32[]{:S(2)}) collective-permute-start(bf16[7,10,32,128]{3,2,1,0:T(8,128)(2,1)S(1)} %collective-permute-done.8.w2), channel_id=1, source_target_pairs={{0,1},{1,0},{2,3},{3,2},{4,5},{5,4},{6,7},{7,6},{8,9},{9,8},{10,11... | collective-permute-start | bytes 1720328 | tf_op jit(solution)/shard_map/ppermute | solution.py:48
  62.6 16.6 %collective-permute-start.17 = (bf16[128,1024]{1,0:T(8,128)(2,1)}, bf16[128,1024]{1,0:T(8,128)(2,1)S(1)}, u32[]{:S(2)}, u32[]{:S(2)}) collective-permute-start(bf16[128,1024]{1,0:T(8,128)(2,1)} %slice.29), channel_id=1, source_target_pairs={{4,0},{8,4},{12,8},{14,12},{10,14},{6,10},{2,6},{0,2},{5,1},{9,5},... | collective-permute-start | bytes 786440 | tf_op jit(solution)/shard_map/ppermute | solution.py:67
  65.8 13.4 %collective-permute-start.16 = (bf16[128,1024]{1,0:T(8,128)(2,1)}, bf16[128,1024]{1,0:T(8,128)(2,1)}, u32[]{:S(2)}, u32[]{:S(2)}) collective-permute-start(bf16[128,1024]{1,0:T(8,128)(2,1)} %slice.28), channel_id=1, source_target_pairs={{0,4},{4,8},{8,12},{12,14},{14,10},{10,6},{6,2},{2,0},{1,5},{5,9},... | collective-permute-start | bytes 786440 | tf_op jit(solution)/shard_map/ppermute | solution.py:66
  119.2 42.5 %collective-permute-start.34 = (bf16[48,128,128]{2,1,0:T(8,128)(2,1)}, bf16[48,128,128]{2,1,0:T(8,128)(2,1)S(1)}, u32[]{:S(2)}, u32[]{:S(2)}) collective-permute-start(bf16[48,128,128]{2,1,0:T(8,128)(2,1)} %grads.1), channel_id=1, source_target_pairs={{0,1},{1,0},{2,3},{3,2},{4,5},{5,4},{6,7},{7,6},{8,9},{9,8},{10,11... | collective-permute-start | bytes 4718600 | tf_op jit(solution)/shard_map/ppermute | solution.py:48
  119.3 15.1 %collective-permute-start.18 = (bf16[4,64,1024]{2,1,0:T(8,128)(2,1)}, bf16[4,64,1024]{2,1,0:T(8,128)(2,1)}, u32[]{:S(2)}, u32[]{:S(2)}) collective-permute-start(bf16[4,64,1024]{2,1,0:T(8,128)(2,1)} %get-tuple-element.35), channel_id=1, source_target_pairs={{0,2},{2,0},{4,6},{6,4},{8,10},{10,8},{12,14},{14,12},{1,3},{3,1},... | collective-permute-start | bytes 1572872 | tf_op jit(solution)/shard_map/ppermute | solution.py:416
  121.0 24.2 %collective-permute-start.22 = (bf16[4,64,1024]{2,1,0:T(8,128)(2,1)}, bf16[4,64,1024]{2,1,0:T(8,128)(2,1)}, u32[]{:S(2)}, u32[]{:S(2)}) collective-permute-start(bf16[4,64,1024]{2,1,0:T(8,128)(2,1)} %get-tuple-element.41), channel_id=1, source_target_pairs={{0,2},{2,0},{4,6},{6,4},{8,10},{10,8},{12,14},{14,12},{1,3},{3,1},... | collective-permute-start | bytes 1572872 | tf_op jit(solution)/shard_map/ppermute | solution.py:416
  136.4 11.2 %collective-permute-start.19 = (bf16[64,1024]{1,0:T(8,128)(2,1)}, bf16[64,1024]{1,0:T(8,128)(2,1)S(1)}, u32[]{:S(2)}, u32[]{:S(2)}) collective-permute-start(bf16[64,1024]{1,0:T(8,128)(2,1)} %get-tuple-element.37), channel_id=1, source_target_pairs={{0,4},{2,6},{4,8},{6,10},{8,12},{10,14},{12,0},{14,2},{1,5},{3,7},... | collective-permute-start | bytes 393224 | tf_op jit(solution)/shard_map/ppermute | solution.py:420
  136.7 14.3 %collective-permute-start.20 = (bf16[64,1024]{1,0:T(8,128)(2,1)}, bf16[64,1024]{1,0:T(8,128)(2,1)S(1)}, u32[]{:S(2)}, u32[]{:S(2)}) collective-permute-start(bf16[64,1024]{1,0:T(8,128)(2,1)} %get-tuple-element.38), channel_id=1, source_target_pairs={{0,8},{2,10},{4,12},{6,14},{8,0},{10,2},{12,4},{14,6},{1,9},{3,11}... | collective-permute-start | bytes 393224 | tf_op jit(solution)/shard_map/ppermute | solution.py:420
  140.1 12.6 %collective-permute-start.21 = (bf16[64,1024]{1,0:T(8,128)(2,1)}, bf16[64,1024]{1,0:T(8,128)(2,1)S(1)}, u32[]{:S(2)}, u32[]{:S(2)}) collective-permute-start(bf16[64,1024]{1,0:T(8,128)(2,1)} %get-tuple-element.39), channel_id=1, source_target_pairs={{0,12},{2,14},{4,0},{6,2},{8,4},{10,6},{12,8},{14,10},{1,13},{3,15... | collective-permute-start | bytes 393224 | tf_op jit(solution)/shard_map/ppermute | solution.py:420
  147.6 12.4 %collective-permute-start.24 = (bf16[64,1024]{1,0:T(8,128)(2,1)}, bf16[64,1024]{1,0:T(8,128)(2,1)S(1)}, u32[]{:S(2)}, u32[]{:S(2)}) collective-permute-start(bf16[64,1024]{1,0:T(8,128)(2,1)} %get-tuple-element.44), channel_id=1, source_target_pairs={{0,8},{2,10},{4,12},{6,14},{8,0},{10,2},{12,4},{14,6},{1,9},{3,11}... | collective-permute-start | bytes 393224 | tf_op jit(solution)/shard_map/ppermute | solution.py:420
  151.0 9.0 %collective-permute-start.25 = (bf16[64,1024]{1,0:T(8,128)(2,1)}, bf16[64,1024]{1,0:T(8,128)(2,1)S(1)}, u32[]{:S(2)}, u32[]{:S(2)}) collective-permute-start(bf16[64,1024]{1,0:T(8,128)(2,1)} %get-tuple-element.45), channel_id=1, source_target_pairs={{0,12},{2,14},{4,0},{6,2},{8,4},{10,6},{12,8},{14,10},{1,13},{3,15... | collective-permute-start | bytes 393224 | tf_op jit(solution)/shard_map/ppermute | solution.py:420
  (31 other events, 405.3 us)

commit v2 on v1

--- a/solution.py
+++ b/solution.py
@@ -29,12 +29,17 @@
     return jax.ShapeDtypeStruct(dims, dtype)
 
 
-def ring_order(count):
-    return [*range(0, count, 2), *range(count - 1, 0, -2)]
+def ring_at(place, count):
+    place = place % count
+    return jnp.where(place < count // 2, 2 * place, 2 * (count - 1 - place) + 1)
+
+
+def ring_place(index, count):
+    return jnp.where(index % 2 == 0, index // 2, count - 1 - index // 2)
 
 
 def ring_routes(count):
-    order = ring_order(count)
+    order = [*range(0, count, 2), *range(count - 1, 0, -2)]
     onward = [(order[i], order[(i + 1) % count]) for i in range(count)]
     return onward, [(b, a) for a, b in onward]
 
@@ -48,31 +53,36 @@
     return lax.ppermute(block, axis, [(0, 1), (1, 0)])
 
 
-def ring_gather(block, axis):
+def tie(block, *others):
+    return lax.optimization_barrier((block, *others))[0]
+
+
+def ring_gather(block, axis, hold=None):
     count = lax.axis_size(axis)
     onward, back = ring_routes(count)
-    order = ring_order(count)
-    place = jnp.array([order.index(i) for i in range(count)], jnp.int32)[lax.axis_index(axis)]
-    table = jnp.array(order, jnp.int32)
     half = block.shape[0] // 2
-    pieces = [(block, lax.axis_index(axis), 0)]
+    pieces = [(block, 0, 0)]
     left = right = block
     for step in range(1, count // 2):
+        if hold is not None and step == hold[0]:
+            left, right, _ = lax.optimization_barrier((left, right, hold[1]))
         left = lax.ppermute(left, axis, onward)
         right = lax.ppermute(right, axis, back)
-        pieces.append((left, table[(place - step) % count], 0))
-        pieces.append((right, table[(place + step) % count], 0))
-    far = table[(place + count // 2) % count]
-    pieces.append((lax.ppermute(left[:half], axis, onward), far, 0))
-    pieces.append((lax.ppermute(right[half:], axis, back), far, half))
+        pieces.append((left, -step, 0))
+        pieces.append((right, step, 0))
+    pieces.append((lax.ppermute(left[:half], axis, onward), count // 2, 0))
+    pieces.append((lax.ppermute(right[half:], axis, back), count // 2, half))
     return pieces
 
 
-def pack_kernel(info, gd, ud, dd, gr, ur, dr, gate, up, down, *refs):
-    own = refs[0]
-    sends = refs[1:SPREAD]
-    slab, ids, used = refs[SPREAD:]
-    quarter = info[0]
+def pack_kernel(gd, ud, dd, gr, ur, dr, tokens, cotangent, gate, up, down, *refs):
+    both, own = refs[:2]
+    sends = refs[2 : SPREAD + 1]
+    slab, ids, used = refs[SPREAD + 1 :]
+    quarter = 2 * lax.axis_index("groups") + lax.axis_index("section")
+    t = tokens.shape[0]
+    both[0:t] = tokens[...]
+    both[t : 2 * t] = cotangent[...]
     rows = BLK // 4
     slab[...] = jnp.zeros_like(slab)
     own[...] = jnp.zeros_like(own)
@@ -103,13 +113,15 @@
     own[PER, 0:rows] = ids[0].astype(BF16)
 
 
-def pack(quarter, dests, row_ids, blocks):
+def pack(tokens, cotangent, dests, row_ids, blocks):
     rows = BLK // 4
+    t, width = tokens.shape
     return pl.pallas_call(
         pack_kernel,
-        out_shape=[shape((PER + 1, BLK, BLK))] + [shape((PER + 1, rows, BLK))] * (SPREAD - 1),
-        in_specs=[SMEM] * 7 + [VMEM] * 3,
-        out_specs=[VMEM] * SPREAD,
+        out_shape=[shape((2 * t, width)), shape((PER + 1, BLK, BLK))]
+        + [shape((PER + 1, rows, BLK))] * (SPREAD - 1),
+        in_specs=[SMEM] * 6 + [VMEM] * 5,
+        out_specs=[VMEM] * (SPREAD + 1),
         scratch_shapes=[
             pltpu.VMEM((SPREAD, PER, rows, BLK), BF16),
             pltpu.VMEM((SPREAD, rows, BLK), F32),
@@ -117,10 +129,10 @@
         ],
         compiler_params=params(),
         name="pack",
-    )(quarter, *dests, *row_ids, *blocks)
-
-
-def forward_kernel(layout, tokens_here, split, info, own, w0, w1, w2, w3, *refs):
+    )(*dests, *row_ids, tokens, cotangent, *blocks)
+
+
+def forward_kernel(layout, tokens_here, split, own, w0, w1, w2, w3, *refs):
     count = len(layout)
     shards = refs[:count]
     refs = refs[count:]
@@ -130,6 +142,16 @@
     width = field.shape[2]
     per_piece = width // BLK
     t = tokens_here
+    axis_size = lax.axis_size("fsdp")
+    me = lax.axis_index("fsdp")
+    group = lax.axis_index("groups")
+    section = lax.axis_index("section")
+    quarters = (
+        2 * group + section,
+        2 * group + 1 - section,
+        2 * (1 - group) + section,
+        2 * (1 - group) + 1 - section,
+    )
 
     own_copies = [
         pltpu.make_async_copy(own.at[0:PER], weights.at[0], sems.at[0]),
@@ -138,7 +160,7 @@
     ]
     weight_copies = []
     for n, ref in enumerate((w0, w1, w2, w3)):
-        begin = pl.multiple_of(info[1 + n] * (BLK // 4), BLK // 4)
+        begin = pl.multiple_of(quarters[n] * (BLK // 4), BLK // 4)
         weight_copies.append(
             pltpu.make_async_copy(
                 ref.at[:, 0:PER],
@@ -147,10 +169,11 @@
             )
         )
     shard_copies = []
-    for n, (first, length) in enumerate(layout):
+    for n, (steps, first, length) in enumerate(layout):
+        piece = ring_at(ring_place(me, axis_size) + steps, axis_size) if split else 0
         shard_copies.append(
             pltpu.make_async_copy(
-                shards[n], field.at[info[5 + n], first : first + length], shard_sems.at[n]
+                shards[n], field.at[piece, first : first + length], shard_sems.at[n]
             )
         )
     for copy in own_copies + shard_copies + weight_copies:
@@ -219,7 +242,7 @@
                 piece, column = where(offset, kind, rank)
                 total[piece, :, pl.ds(column, BLK)] += terms[:, rank * BLK : (rank + 1) * BLK]
     if split:
-        side = info[0]
+        side = me % 2
         send_a, send_b, keep_a, keep_b = outs
         h = t // 2
         for z in range(send_a.shape[0]):
@@ -234,8 +257,8 @@
     field_copy.wait()
 
 
-def forward(info, own, quarters, pieces, split, piece_count):
-    layout = [(first, block.shape[0]) for block, _, first in pieces]
+def forward(own, quarters, pieces, split, piece_count):
+    layout = [(steps, first, block.shape[0]) for block, steps, first in pieces]
     t = pieces[0][0].shape[0] // 2
     width = pieces[0][0].shape[1]
     if split:
@@ -246,7 +269,7 @@
     return pl.pallas_call(
         functools.partial(forward_kernel, layout, t, int(split)),
         out_shape=[shape(field), shape((KINDS, t, BLK))] + outs,
-        in_specs=[SMEM] + [ANY] * (5 + len(pieces)),
+        in_specs=[ANY] * (5 + len(pieces)),
         out_specs=[ANY] + [VMEM] * (1 + len(outs)),
         scratch_shapes=[
             pltpu.VMEM(field, BF16),
@@ -261,39 +284,45 @@
         ],
         compiler_params=params(),
         name="forward",
-    )(info, own, *quarters, *[block for block, _, _ in pieces])
-
-
-def pair_kernel(info, keep, got, here, one, two, three):
-    z = info[0]
+    )(own, *quarters, *[block for block, _, _ in pieces])
+
+
+def pair_kernel(keep, got, here, one, two, three):
+    z = lax.axis_index("fsdp") // 2
     for step, ref in enumerate((here, one, two, three)):
         at = lax.rem(z + step, keep.shape[0])
         ref[...] = (keep[at].astype(F32) + got[at].astype(F32)).astype(BF16)
 
 
-def pair(z, keep, got):
+def pair(keep, got):
     piece = shape(keep.shape[1:])
     return pl.pallas_call(
         pair_kernel,
         out_shape=[piece] * 4,
-        in_specs=[SMEM, VMEM, VMEM],
+        in_specs=[VMEM, VMEM],
         out_specs=[VMEM] * 4,
         compiler_params=params(),
         name="pair",
-    )(z, keep, got)
-
-
-def grads_kernel(layout, info, gd, ud, dd, gr, ur, dr, field, *refs):
+    )(keep, got)
+
+
+def grads_kernel(layout, grid, gd, ud, dd, gr, ur, dr, field, *refs):
     count = len(layout)
     arrived = refs[:count]
-    out, columns, sems = refs[count:]
+    out, columns, sems = refs[-3:]
+    axis_size = lax.axis_size("fsdp")
+    me = lax.axis_index("fsdp")
     t = field.shape[1] // 2
     per_piece = field.shape[2] // BLK
     copies = []
-    for n, (first, length) in enumerate(layout):
+    for n, (steps, first, length) in enumerate(layout):
+        offset = steps
+        if grid:
+            source = ring_at(ring_place(me, axis_size) + steps, axis_size)
+            offset = (me - source + axis_size) % axis_size
         copies.append(
             pltpu.make_async_copy(
-                arrived[n], columns.at[info[n], first : first + length], sems.at[n]
+                arrived[n], columns.at[offset, first : first + length], sems.at[n]
             )
         )
     for copy in copies:
@@ -319,14 +348,14 @@
         lax.fori_loop(0, slots, one, 0, unroll=4)
 
 
-def grads(info, dests, row_ids, field, pieces):
-    layout = [(first, block.shape[0]) for block, _, first in pieces]
+def grads(dests, row_ids, field, pieces, grid, after):
+    layout = [(steps, first, block.shape[0]) for block, steps, first in pieces]
     rows = pieces[0][0].shape[0]
     slots = dests[0].shape[0]
     return pl.pallas_call(
-        functools.partial(grads_kernel, layout),
+        functools.partial(grads_kernel, layout, grid),
         out_shape=shape((KINDS * slots, BLK, BLK)),
-        in_specs=[SMEM] * 7 + [VMEM] + [ANY] * len(pieces),
+        in_specs=[SMEM] * 6 + [VMEM] + [ANY] * (len(pieces) + len(after)),
         out_specs=VMEM,
         scratch_shapes=[
             pltpu.VMEM((SPREAD, rows, BLK), BF16),
@@ -334,7 +363,7 @@
         ],
         compiler_params=params(),
         name="grads",
-    )(info, *dests, *row_ids, field, *[block for block, _, _ in pieces])
+    )(*dests, *row_ids, field, *[block for block, _, _ in pieces], *after)
 
 
 def shards(
@@ -351,79 +380,66 @@
     down_rows,
 ):
     count = lax.axis_size("fsdp")
-    me = lax.axis_index("fsdp")
-    group = lax.axis_index("groups")
-    section = lax.axis_index("section")
     grid = count == SPREAD and tokens.shape[1] % BLK == 0
     t = tokens.shape[0]
     dests = [target[:, 0] for target in (gate_dest, up_dest, down_dest)]
     row_ids = [gate_rows, up_rows, down_rows]
 
-    both = jnp.concatenate([tokens, cotangent], axis=0)
+    both, own, *sends = pack(
+        tokens, cotangent, dests, row_ids, (gate_blocks, up_blocks, down_blocks)
+    )
     if grid:
         pieces = ring_gather(both, "fsdp")
         piece_count = count
     else:
-        pieces = [(lax.all_gather(both, "fsdp", axis=1, tiled=True), jnp.int32(0), 0)]
+        pieces = [(lax.all_gather(both, "fsdp", axis=1, tiled=True), 0, 0)]
         piece_count = 1
 
-    quarter = jnp.reshape(2 * group + section, (1,)).astype(jnp.int32)
-    own, *sends = pack(quarter, dests, row_ids, (gate_blocks, up_blocks, down_blocks))
     mine = jnp.stack([shift(block, "fsdp", -d) for d, block in enumerate(sends, 1)], axis=0)
     across = swap(mine, "groups")
     beside = swap(mine, "section")
     diagonal = swap(across, "section")
     quarters = (mine, beside, across, diagonal)
-    order_of_quarters = [
-        2 * group + section,
-        2 * group + 1 - section,
-        2 * (1 - group) + section,
-        2 * (1 - group) + 1 - section,
-    ]
-    info = jnp.stack(
-        [me % 2, *order_of_quarters, *[source for _, source, _ in pieces]]
-    ).astype(jnp.int32)
-    field, columns, *partial_input = forward(info, own, quarters, pieces, grid, piece_count)
-
+    field, columns, *partial_input = forward(own, quarters, pieces, grid, piece_count)
     flat = columns.reshape(KINDS * t, BLK)
+
     if grid:
-        arrived = [
-            (block, (me - source) % count, first)
-            for block, source, first in ring_gather(flat, "fsdp")
+        beside_x = [(i, i ^ 1) for i in range(count)]
+        along_z = [
+            [(i, (i + 2 * step) % count) for i in range(count)] for step in range(1, count // 2)
         ]
+        send_a, send_b, keep_a, keep_b = partial_input
+        got_a = lax.ppermute(send_a, "fsdp", beside_x)
+        got_b = lax.ppermute(send_b, "fsdp", beside_x)
+        halves = []
+        for keep, got in ((keep_a, got_a), (keep_b, got_b)):
+            here, *away = pair(keep, got)
+            halves.append((here, [(b, r) for b, r in zip(away, along_z, strict=True)]))
+        sums = []
+        for here, away in halves:
+            result = here.astype(F32)
+            for block, route in away:
+                result = result + lax.ppermute(block, "fsdp", route).astype(F32)
+            sums.append(result.astype(BF16))
+        input_grad = jnp.concatenate(sums, axis=0)
     else:
-        arrived = [(flat, jnp.int32(0), 0)] + [
-            (shift(flat, "fsdp", d), jnp.int32(d), 0) for d in range(1, SPREAD)
-        ]
-    offsets = jnp.stack([offset for _, offset, _ in arrived]).astype(jnp.int32)
-    part = grads(offsets, dests, row_ids, field, arrived)
+        input_grad = lax.psum_scatter(
+            partial_input[0].reshape(t, -1), "fsdp", scatter_dimension=1, tiled=True
+        )
+
+    if grid:
+        arrived = ring_gather(flat, "fsdp", (3, halves[0][0]))
+        after = [got_b]
+    else:
+        arrived = [(flat, 0, 0)] + [(shift(flat, "fsdp", d), d, 0) for d in range(1, SPREAD)]
+        after = []
+    part = grads(dests, row_ids, field, arrived, grid, after)
     other = swap(part, "section")
     summed = part.astype(F32) + other.astype(F32)
     slots = gate_blocks.shape[0]
     gate_grad, up_grad, down_grad = (
         summed[kind * slots : (kind + 1) * slots] for kind in range(KINDS)
     )
-
-    if grid:
-        beside_x = [(i, i ^ 1) for i in range(count)]
-        along_z = [
-            [(i, (i + 2 * step) % count) for i in range(count)] for step in range(1, count // 2)
-        ]
-        z = jnp.reshape(me // 2, (1,)).astype(jnp.int32)
-        send_a, send_b, keep_a, keep_b = partial_input
-        halves = []
-        for send, keep in ((send_a, keep_a), (send_b, keep_b)):
-            got = lax.ppermute(send, "fsdp", beside_x)
-            here, *away = pair(z, keep, got)
-            result = here.astype(F32)
-            for block, route in zip(away, along_z, strict=True):
-                result = result + lax.ppermute(block, "fsdp", route).astype(F32)
-            halves.append(result.astype(BF16))
-        input_grad = jnp.concatenate(halves, axis=0)
-    else:
-        input_grad = lax.psum_scatter(
-            partial_input[0].reshape(t, -1), "fsdp", scatter_dimension=1, tiled=True
-        )
     return input_grad, gate_grad, up_grad, down_grad
 
 

time: 165 us -> 157 us (0.952)
  local copies, waits for them, and re-layouts: 16.1 us -> 3.95 us
  between operations: 10.2 us -> 1.03 us
  starting transfers between devices: 49.4 us -> 57.9 us
  waiting for transfers between devices: 61.2 us -> 67.7 us
    ppermute x6, waiting for transfers between devices: 22.5 us -> 32.5 us  [ring_gather(): right = lax.ppermute(right, axis, back)]
    ppermute x6, waiting for transfers between devices: 17.2 us -> 8.4 us  [the longest x2 4.55 us: ring_gather(): pieces.append((lax.ppermute(left[:half], axis, onward), count // 2, 0))]
    ppermute x6, starting transfers between devices: 10.1 us -> 17.6 us  [shards(): result = result + lax.ppermute(block, 'fsdp', route).astype(F32)]
    another operation x2 -> x0, local copies, waits for them, and re-layouts: 6.44 us -> none  [the longest x1 5.77 us: shards(): jnp.stack([me % 2, *order_of_quarters, *[source for _, source, _ in piece...]
    ppermute x6, waiting for transfers between devices: 0.22 us -> 4.63 us  [ring_gather(): left = lax.ppermute(left, axis, onward)]
    dynamic_slice x2 -> x0, local copies, waits for them, and re-layouts: 2.86 us -> none  [the longest x1 1.62 us: ring_gather(): far = table[(place + count // 2) % count]]
    ppermute x7, waiting for transfers between devices: 14.9 us -> 17 us  [shift(): lax.ppermute(block, axis, [(i, (i + distance) % count) for i in range(cou...]
  transfers between devices with their start and end apart: 35 -> 35, of which waited for: 16 -> 16; matrix products, arithmetic and copies ran while one was open for 10% -> 1% of each run, Pallas kernels for 2% -> 3%
where the time goes in v2:
time: 157 us
  waiting for transfers between devices  67.7 us (43%)
  starting transfers between devices  57.9 us (37%)
  Pallas kernels  23.6 us (15%)
  local copies, waits for them, and re-layouts  3.95 us (3%)
  other arithmetic  2.36 us (2%)
    ppermute x6, waiting for transfers between devices, ring_gather(): right = lax.ppermute(right, axis, back)  32.5 us
    ppermute x6, starting transfers between devices, shards(): result = result + lax.ppermute(block, 'fsdp', route).astype(F32)  17.6 us
    ppermute x7, waiting for transfers between devices, shift(): lax.ppermute(block, axis, [(i, (i + distance) % count) for i in range(cou...  17 us
    ppermute x7, starting transfers between devices, shift(): lax.ppermute(block, axis, [(i, (i + distance) % count) for i in range(cou...  14.1 us
    ppermute x6, starting transfers between devices, ring_gather(): right = lax.ppermute(right, axis, back)  13.2 us
    pallas_call x1, Pallas kernels, forward(): pl.pallas_call(functools.partial(forward_kernel, layout, t, int(split)),...  8.6 us
    pallas_call x1, Pallas kernels, grads(): pl.pallas_call(functools.partial(grads_kernel, layout, grid), out_shape=s...  7.44 us
    ppermute x6, waiting for transfers between devices, shards(): result = result + lax.ppermute(block, 'fsdp', route).astype(F32)  5.16 us
  transfers between devices with their start and end apart: 35, of which 16 were waited for; matrix products, arithmetic and copies ran while one was open for 1% of the time, Pallas kernels for 3%

profile of v2, /device:TPU:0, one launch (start us, length us, event | category | flops | bytes accessed | tf_op | source)
XLA Modules:
  0.0 156.6 jit_solution(16189430592489340229)
XLA Ops:
  0.6 3.5 %pack.1 = (bf16[256,1024]{1,0:T(8,128)(2,1)}, bf16[10,128,128]{2,1,0:T(8,128)(2,1)}, bf16[10,32,128]{2,1,0:T(8,128)(2,1)}, bf16[10,32,128]{2,1,0:T(8,128)(2,1)},...) custom-call(s32[16]{0:T(128)} %bitcast.21, ...), custom_call_target="tpu_custom_call" | custom-call | tf_op jit(solution)/shard_map/pack/pallas_call | solution.py:119
  4.2 6.0 %collective-permute-start = (bf16[10,32,128]{2,1,0:T(8,128)(2,1)}, bf16[10,32,128]{2,1,0:T(8,128)(2,1)S(1)}, u32[]{:S(2)}, u32[]{:S(2)}) collective-permute-start(bf16[10,32,128]{2,1,0:T(8,128)(2,1)} %get-tuple-element.30), channel_id=1, source_target_pairs={{0,14},{2,0},{4,2},{6,4},{8,6},{10,8},{12,10},{14,12},{1,15},{3,1}... | collective-permute-start | bytes 245768 | tf_op jit(solution)/shard_map/ppermute | solution.py:49
  13.0 2.7 %collective-permute-start.3 = (bf16[10,32,128]{2,1,0:T(8,128)(2,1)}, bf16[10,32,128]{2,1,0:T(8,128)(2,1)S(1)}, u32[]{:S(2)}, u32[]{:S(2)}) collective-permute-start(bf16[10,32,128]{2,1,0:T(8,128)(2,1)} %get-tuple-element.33), channel_id=1, source_target_pairs={{0,8},{2,10},{4,12},{6,14},{8,0},{10,2},{12,4},{14,6},{1,9},{3,11}... | collective-permute-start | bytes 245768 | tf_op jit(solution)/shard_map/ppermute | solution.py:49
  15.7 11.0 %collective-permute-done.1 = bf16[10,32,128]{2,1,0:T(8,128)(2,1)S(1)} collective-permute-done((bf16[10,32,128]{2,1,0:T(8,128)(2,1)}, bf16[10,32,128]{2,1,0:T(8,128)(2,1)S(1)}, u32[]{:S(2)}, u32[]{:S(2)}) %collective-permute-start.1) | collective-permute-done | bytes 81952 | tf_op jit(solution)/shard_map/ppermute | solution.py:49
  28.4 3.9 %collective-permute-start.5 = (bf16[10,32,128]{2,1,0:T(8,128)(2,1)}, bf16[10,32,128]{2,1,0:T(8,128)(2,1)S(1)}, u32[]{:S(2)}, u32[]{:S(2)}) collective-permute-start(bf16[10,32,128]{2,1,0:T(8,128)(2,1)} %get-tuple-element.35), channel_id=1, source_target_pairs={{0,4},{2,6},{4,8},{6,10},{8,12},{10,14},{12,0},{14,2},{1,5},{3,7},... | collective-permute-start | bytes 245768 | tf_op jit(solution)/shard_map/ppermute | solution.py:49
  32.4 3.1 %collective-permute-done.3 = bf16[10,32,128]{2,1,0:T(8,128)(2,1)S(1)} collective-permute-done((bf16[10,32,128]{2,1,0:T(8,128)(2,1)}, bf16[10,32,128]{2,1,0:T(8,128)(2,1)S(1)}, u32[]{:S(2)}, u32[]{:S(2)}) %collective-permute-start.3) | collective-permute-done | bytes 81952 | tf_op jit(solution)/shard_map/ppermute | solution.py:49
  35.6 6.2 %collective-permute-start.13 = (bf16[256,1024]{1,0:T(8,128)(2,1)S(1)}, bf16[256,1024]{1,0:T(8,128)(2,1)S(1)}, u32[]{:S(2)}, u32[]{:S(2)}) collective-permute-start(bf16[256,1024]{1,0:T(8,128)(2,1)S(1)} %collective-permute-done.11.refs_2_), channel_id=1, source_target_pairs={{4,0},{8,4},{12,8},{14,12},{10,14},{6,10},{2,6},{0,2},{5,1},{9,5},... | collective-permute-start | bytes 1572872 | tf_op jit(solution)/shard_map/ppermute | solution.py:70
  45.3 6.1 %collective-permute-done.13.refs_4_ = bf16[256,1024]{1,0:T(8,128)(2,1)S(1)} collective-permute-done((bf16[256,1024]{1,0:T(8,128)(2,1)S(1)}, bf16[256,1024]{1,0:T(8,128)(2,1)S(1)}, u32[]{:S(2)}, u32[]{:S(2)}) %collective-permute-start.13) | collective-permute-done | bytes 524320 | tf_op jit(solution)/shard_map/ppermute | solution.py:70
  51.4 2.5 %collective-permute-start.15 = (bf16[256,1024]{1,0:T(8,128)(2,1)S(1)}, bf16[256,1024]{1,0:T(8,128)(2,1)S(1)}, u32[]{:S(2)}, u32[]{:S(2)}) collective-permute-start(bf16[256,1024]{1,0:T(8,128)(2,1)S(1)} %collective-permute-done.13.refs_4_), channel_id=1, source_target_pairs={{4,0},{8,4},{12,8},{14,12},{10,14},{6,10},{2,6},{0,2},{5,1},{9,5},... | collective-permute-start | bytes 1572872 | tf_op jit(solution)/shard_map/ppermute | solution.py:70
  54.5 8.9 %collective-permute-done.15.refs_6_ = bf16[256,1024]{1,0:T(8,128)(2,1)S(1)} collective-permute-done((bf16[256,1024]{1,0:T(8,128)(2,1)S(1)}, bf16[256,1024]{1,0:T(8,128)(2,1)S(1)}, u32[]{:S(2)}, u32[]{:S(2)}) %collective-permute-start.15) | collective-permute-done | bytes 524320 | tf_op jit(solution)/shard_map/ppermute | solution.py:70
  63.5 2.5 %collective-permute-start.17 = (bf16[128,1024]{1,0:T(8,128)(2,1)S(1)}, bf16[128,1024]{1,0:T(8,128)(2,1)S(1)}, u32[]{:S(2)}, u32[]{:S(2)}) collective-permute-start(bf16[128,1024]{1,0:T(8,128)(2,1)S(1)} %slice.29), channel_id=1, source_target_pairs={{4,0},{8,4},{12,8},{14,12},{10,14},{6,10},{2,6},{0,2},{5,1},{9,5},... | collective-permute-start | bytes 786440 | tf_op jit(solution)/shard_map/ppermute | solution.py:74
  66.1 3.8 %collective-permute-done.17.refs_8_ = bf16[128,1024]{1,0:T(8,128)(2,1)S(1)} collective-permute-done((bf16[128,1024]{1,0:T(8,128)(2,1)S(1)}, bf16[128,1024]{1,0:T(8,128)(2,1)S(1)}, u32[]{:S(2)}, u32[]{:S(2)}) %collective-permute-start.17) | collective-permute-done | bytes 262176 | tf_op jit(solution)/shard_map/ppermute | solution.py:74
  69.9 2.6 %collective-permute-done.16.refs_7_ = bf16[128,1024]{1,0:T(8,128)(2,1)S(1)} collective-permute-done((bf16[128,1024]{1,0:T(8,128)(2,1)S(1)}, bf16[128,1024]{1,0:T(8,128)(2,1)S(1)}, u32[]{:S(2)}, u32[]{:S(2)}) %collective-permute-start.16) | collective-permute-done | bytes 262176 | tf_op jit(solution)/shard_map/ppermute | solution.py:73
  73.2 8.6 %forward.1 = (bf16[8,256,1024]{2,1,0:T(8,128)(2,1)}, bf16[3,128,128]{2,1,0:T(8,128)(2,1)}, bf16[4,64,1024]{2,1,0:T(8,128)(2,1)}, bf16[4,64,1024]{2,1,0:T(8,128)(...) custom-call(bf16[10,128,128]{2,1,0:T(8,128)(2,1)} %get-tuple-element.29.own, ...), custom_call_target="tpu_custom_call" | custom-call | tf_op jit(solution)/shard_map/forward/pallas_call | solution.py:269
  85.9 17.2 %collective-permute-done.27.refs_2_ = bf16[384,128]{1,0:T(8,128)(2,1)S(1)} collective-permute-done((bf16[384,128]{1,0:T(8,128)(2,1)}, bf16[384,128]{1,0:T(8,128)(2,1)S(1)}, u32[]{:S(2)}, u32[]{:S(2)}) %collective-permute-start.27) | collective-permute-done | bytes 98336 | tf_op jit(solution)/shard_map/ppermute | solution.py:70
  103.1 2.4 %collective-permute-start.29 = (bf16[384,128]{1,0:T(8,128)(2,1)S(1)}, bf16[384,128]{1,0:T(8,128)(2,1)S(1)}, u32[]{:S(2)}, u32[]{:S(2)}) collective-permute-start(bf16[384,128]{1,0:T(8,128)(2,1)S(1)} %collective-permute-done.27.refs_2_), channel_id=1, source_target_pairs={{4,0},{8,4},{12,8},{14,12},{10,14},{6,10},{2,6},{0,2},{5,1},{9,5},... | collective-permute-start | bytes 294920 | tf_op jit(solution)/shard_map/ppermute | solution.py:70
  108.6 2.0 %collective-permute-done.28.refs_3_ = bf16[384,128]{1,0:T(8,128)(2,1)S(1)} collective-permute-done((bf16[384,128]{1,0:T(8,128)(2,1)S(1)}, bf16[384,128]{1,0:T(8,128)(2,1)S(1)}, u32[]{:S(2)}, u32[]{:S(2)}) %collective-permute-start.28) | collective-permute-done | bytes 98336 | tf_op jit(solution)/shard_map/ppermute | solution.py:69
  112.6 2.6 %collective-permute-done.30.refs_5_ = bf16[384,128]{1,0:T(8,128)(2,1)S(1)} collective-permute-done((bf16[384,128]{1,0:T(8,128)(2,1)S(1)}, bf16[384,128]{1,0:T(8,128)(2,1)S(1)}, u32[]{:S(2)}, u32[]{:S(2)}) %collective-permute-start.30) | collective-permute-done | bytes 98336 | tf_op jit(solution)/shard_map/ppermute | solution.py:69
  115.3 2.0 %collective-permute-start.33 = (bf16[192,128]{1,0:T(8,128)(2,1)S(1)}, bf16[192,128]{1,0:T(8,128)(2,1)S(1)}, u32[]{:S(2)}, u32[]{:S(2)}) collective-permute-start(bf16[192,128]{1,0:T(8,128)(2,1)S(1)} %slice.31), channel_id=1, source_target_pairs={{4,0},{8,4},{12,8},{14,12},{10,14},{6,10},{2,6},{0,2},{5,1},{9,5},... | collective-permute-start | bytes 147464 | tf_op jit(solution)/shard_map/ppermute | solution.py:74
  120.0 7.4 %grads.1 = bf16[48,128,128]{2,1,0:T(8,128)(2,1)} custom-call(s32[16]{0:T(128)} %bitcast.22, s32[16]{0:T(128)} %bitcast.24, s32[16]{0:T(128)} %bitcast.26, s32[16]{0:T(128)} %gr.3, s32[16]{0:T(128)} %ur.3, s32[16]{0:T(128)} %dr.3, bf16[8,256,1024]{2,1,0:T(8,128)(2,1)} %get-tuple-element.50.field, bf16[384,128]{1,0:T(8,128)(2,1)} %bitcast.20, ...), custom_call_target="tpu_custom_call" | custom-call | tf_op jit(solution)/shard_map/grads/pallas_call | solution.py:355
  129.1 2.9 %collective-permute-start.20 = (bf16[64,1024]{1,0:T(8,128)(2,1)S(1)}, bf16[64,1024]{1,0:T(8,128)(2,1)S(1)}, u32[]{:S(2)}, u32[]{:S(2)}) collective-permute-start(bf16[64,1024]{1,0:T(8,128)(2,1)S(1)} %copy-done.25), channel_id=1, source_target_pairs={{0,8},{2,10},{4,12},{6,14},{8,0},{10,2},{12,4},{14,6},{1,9},{3,11}... | collective-permute-start | bytes 393224 | tf_op jit(solution)/shard_map/ppermute | solution.py:422
  136.1 6.0 %collective-permute-start.24 = (bf16[64,1024]{1,0:T(8,128)(2,1)}, bf16[64,1024]{1,0:T(8,128)(2,1)S(1)}, u32[]{:S(2)}, u32[]{:S(2)}) collective-permute-start(bf16[64,1024]{1,0:T(8,128)(2,1)} %get-tuple-element.48), channel_id=1, source_target_pairs={{0,8},{2,10},{4,12},{6,14},{8,0},{10,2},{12,4},{14,6},{1,9},{3,11}... | collective-permute-start | bytes 393224 | tf_op jit(solution)/shard_map/ppermute | solution.py:422
  142.1 5.1 %collective-permute-start.25 = (bf16[64,1024]{1,0:T(8,128)(2,1)}, bf16[64,1024]{1,0:T(8,128)(2,1)S(1)}, u32[]{:S(2)}, u32[]{:S(2)}) collective-permute-start(bf16[64,1024]{1,0:T(8,128)(2,1)} %get-tuple-element.49), channel_id=1, source_target_pairs={{0,12},{2,14},{4,0},{6,2},{8,4},{10,6},{12,8},{14,10},{1,13},{3,15... | collective-permute-start | bytes 393224 | tf_op jit(solution)/shard_map/ppermute | solution.py:422
  147.4 5.2 %collective-permute-done.24 = bf16[64,1024]{1,0:T(8,128)(2,1)S(1)} collective-permute-done((bf16[64,1024]{1,0:T(8,128)(2,1)}, bf16[64,1024]{1,0:T(8,128)(2,1)S(1)}, u32[]{:S(2)}, u32[]{:S(2)}) %collective-permute-start.24) | collective-permute-done | bytes 131104 | tf_op jit(solution)/shard_map/ppermute | solution.py:422
  (121 shorter events, 31.2 us)
Async XLA Ops:
  4.2 8.8 %collective-permute-start = (bf16[10,32,128]{2,1,0:T(8,128)(2,1)}, bf16[10,32,128]{2,1,0:T(8,128)(2,1)S(1)}, u32[]{:S(2)}, u32[]{:S(2)}) collective-permute-start(bf16[10,32,128]{2,1,0:T(8,128)(2,1)} %get-tuple-element.30), channel_id=1, source_target_pairs={{0,14},{2,0},{4,2},{6,4},{8,6},{10,8},{12,10},{14,12},{1,15},{3,1}... | collective-permute-start | bytes 245768 | tf_op jit(solution)/shard_map/ppermute | solution.py:49
  10.2 25.4 %collective-permute-start.11 = (bf16[256,1024]{1,0:T(8,128)(2,1)}, bf16[256,1024]{1,0:T(8,128)(2,1)S(1)}, u32[]{:S(2)}, u32[]{:S(2)}) collective-permute-start(bf16[256,1024]{1,0:T(8,128)(2,1)} %get-tuple-element.37.refs_0_), channel_id=1, source_target_pairs={{4,0},{8,4},{12,8},{14,12},{10,14},{6,10},{2,6},{0,2},{5,1},{9,5},... | collective-permute-start | bytes 1572872 | tf_op jit(solution)/shard_map/ppermute | solution.py:70
  10.2 31.7 %collective-permute-start.10 = (bf16[256,1024]{1,0:T(8,128)(2,1)}, bf16[256,1024]{1,0:T(8,128)(2,1)S(1)}, u32[]{:S(2)}, u32[]{:S(2)}) collective-permute-start(bf16[256,1024]{1,0:T(8,128)(2,1)} %get-tuple-element.37.refs_0_), channel_id=1, source_target_pairs={{0,4},{4,8},{8,12},{12,14},{14,10},{10,6},{6,2},{2,0},{1,5},{5,9},... | collective-permute-start | bytes 1572872 | tf_op jit(solution)/shard_map/ppermute | solution.py:69
  12.2 14.5 %collective-permute-start.1 = (bf16[10,32,128]{2,1,0:T(8,128)(2,1)}, bf16[10,32,128]{2,1,0:T(8,128)(2,1)S(1)}, u32[]{:S(2)}, u32[]{:S(2)}) collective-permute-start(bf16[10,32,128]{2,1,0:T(8,128)(2,1)} %get-tuple-element.31), channel_id=1, source_target_pairs={{0,12},{2,14},{4,0},{6,2},{8,4},{10,6},{12,8},{14,10},{1,13},{3,15... | collective-permute-start | bytes 245768 | tf_op jit(solution)/shard_map/ppermute | solution.py:49
  12.6 15.8 %collective-permute-start.2 = (bf16[10,32,128]{2,1,0:T(8,128)(2,1)}, bf16[10,32,128]{2,1,0:T(8,128)(2,1)S(1)}, u32[]{:S(2)}, u32[]{:S(2)}) collective-permute-start(bf16[10,32,128]{2,1,0:T(8,128)(2,1)} %get-tuple-element.32), channel_id=1, source_target_pairs={{0,10},{2,12},{4,14},{6,0},{8,2},{10,4},{12,6},{14,8},{1,11},{3,13... | collective-permute-start | bytes 245768 | tf_op jit(solution)/shard_map/ppermute | solution.py:49
  13.0 22.5 %collective-permute-start.3 = (bf16[10,32,128]{2,1,0:T(8,128)(2,1)}, bf16[10,32,128]{2,1,0:T(8,128)(2,1)S(1)}, u32[]{:S(2)}, u32[]{:S(2)}) collective-permute-start(bf16[10,32,128]{2,1,0:T(8,128)(2,1)} %get-tuple-element.33), channel_id=1, source_target_pairs={{0,8},{2,10},{4,12},{6,14},{8,0},{10,2},{12,4},{14,6},{1,9},{3,11}... | collective-permute-start | bytes 245768 | tf_op jit(solution)/shard_map/ppermute | solution.py:49
  26.7 8.8 %collective-permute-start.4 = (bf16[10,32,128]{2,1,0:T(8,128)(2,1)}, bf16[10,32,128]{2,1,0:T(8,128)(2,1)S(1)}, u32[]{:S(2)}, u32[]{:S(2)}) collective-permute-start(bf16[10,32,128]{2,1,0:T(8,128)(2,1)} %get-tuple-element.34), channel_id=1, source_target_pairs={{0,6},{2,8},{4,10},{6,12},{8,14},{10,0},{12,2},{14,4},{1,7},{3,9},... | collective-permute-start | bytes 245768 | tf_op jit(solution)/shard_map/ppermute | solution.py:49
  35.6 15.8 %collective-permute-start.13 = (bf16[256,1024]{1,0:T(8,128)(2,1)S(1)}, bf16[256,1024]{1,0:T(8,128)(2,1)S(1)}, u32[]{:S(2)}, u32[]{:S(2)}) collective-permute-start(bf16[256,1024]{1,0:T(8,128)(2,1)S(1)} %collective-permute-done.11.refs_2_), channel_id=1, source_target_pairs={{4,0},{8,4},{12,8},{14,12},{10,14},{6,10},{2,6},{0,2},{5,1},{9,5},... | collective-permute-start | bytes 1572872 | tf_op jit(solution)/shard_map/ppermute | solution.py:70
  41.8 12.1 %collective-permute-start.12 = (bf16[256,1024]{1,0:T(8,128)(2,1)S(1)}, bf16[256,1024]{1,0:T(8,128)(2,1)S(1)}, u32[]{:S(2)}, u32[]{:S(2)}) collective-permute-start(bf16[256,1024]{1,0:T(8,128)(2,1)S(1)} %collective-permute-done.10.refs_1_), channel_id=1, source_target_pairs={{0,4},{4,8},{8,12},{12,14},{14,10},{10,6},{6,2},{2,0},{1,5},{5,9},... | collective-permute-start | bytes 1572872 | tf_op jit(solution)/shard_map/ppermute | solution.py:69
  43.7 10.3 %collective-permute-start.8 = (bf16[7,10,32,128]{3,2,1,0:T(8,128)(2,1)S(1)}, bf16[7,10,32,128]{3,2,1,0:T(8,128)(2,1)S(1)}, u32[]{:S(2)}, u32[]{:S(2)}) collective-permute-start(bf16[7,10,32,128]{3,2,1,0:T(8,128)(2,1)S(1)} %bitcast_dynamic-update-slice_fusion.w0), channel_id=1, source_target_pairs={{0,16},{16,0},{1,17},{17,1},{2,18},{18,2},{3,19},{19,3},{4,20},{20... | collective-permute-start | bytes 1720328 | tf_op jit(solution)/shard_map/ppermute | solution.py:53
  51.4 12.0 %collective-permute-start.15 = (bf16[256,1024]{1,0:T(8,128)(2,1)S(1)}, bf16[256,1024]{1,0:T(8,128)(2,1)S(1)}, u32[]{:S(2)}, u32[]{:S(2)}) collective-permute-start(bf16[256,1024]{1,0:T(8,128)(2,1)S(1)} %collective-permute-done.13.refs_4_), channel_id=1, source_target_pairs={{4,0},{8,4},{12,8},{14,12},{10,14},{6,10},{2,6},{0,2},{5,1},{9,5},... | collective-permute-start | bytes 1572872 | tf_op jit(solution)/shard_map/ppermute | solution.py:70
  53.9 12.1 %collective-permute-start.14 = (bf16[256,1024]{1,0:T(8,128)(2,1)S(1)}, bf16[256,1024]{1,0:T(8,128)(2,1)S(1)}, u32[]{:S(2)}, u32[]{:S(2)}) collective-permute-start(bf16[256,1024]{1,0:T(8,128)(2,1)S(1)} %collective-permute-done.12.refs_3_), channel_id=1, source_target_pairs={{0,4},{4,8},{8,12},{12,14},{14,10},{10,6},{6,2},{2,0},{1,5},{5,9},... | collective-permute-start | bytes 1572872 | tf_op jit(solution)/shard_map/ppermute | solution.py:69
  53.9 12.2 %collective-permute-start.7 = (bf16[7,10,32,128]{3,2,1,0:T(8,128)(2,1)S(1)}, bf16[7,10,32,128]{3,2,1,0:T(8,128)(2,1)S(1)}, u32[]{:S(2)}, u32[]{:S(2)}) collective-permute-start(bf16[7,10,32,128]{3,2,1,0:T(8,128)(2,1)S(1)} %bitcast_dynamic-update-slice_fusion.w0), channel_id=1, source_target_pairs={{0,1},{1,0},{2,3},{3,2},{4,5},{5,4},{6,7},{7,6},{8,9},{9,8},{10,11... | collective-permute-start | bytes 1720328 | tf_op jit(solution)/shard_map/ppermute | solution.py:53
  54.0 12.1 %collective-permute-start.9 = (bf16[7,10,32,128]{3,2,1,0:T(8,128)(2,1)S(1)}, bf16[7,10,32,128]{3,2,1,0:T(8,128)(2,1)S(1)}, u32[]{:S(2)}, u32[]{:S(2)}) collective-permute-start(bf16[7,10,32,128]{3,2,1,0:T(8,128)(2,1)S(1)} %collective-permute-done.8.w2), channel_id=1, source_target_pairs={{0,1},{1,0},{2,3},{3,2},{4,5},{5,4},{6,7},{7,6},{8,9},{9,8},{10,11... | collective-permute-start | bytes 1720328 | tf_op jit(solution)/shard_map/ppermute | solution.py:53
  81.8 23.7 %collective-permute-start.18 = (bf16[4,64,1024]{2,1,0:T(8,128)(2,1)}, bf16[4,64,1024]{2,1,0:T(8,128)(2,1)S(1)}, u32[]{:S(2)}, u32[]{:S(2)}) collective-permute-start(bf16[4,64,1024]{2,1,0:T(8,128)(2,1)} %get-tuple-element.39), channel_id=1, source_target_pairs={{0,2},{2,0},{4,6},{6,4},{8,10},{10,8},{12,14},{14,12},{1,3},{3,1},... | collective-permute-start | bytes 1572872 | tf_op jit(solution)/shard_map/ppermute | solution.py:412
  81.9 35.5 %collective-permute-start.22 = (bf16[4,64,1024]{2,1,0:T(8,128)(2,1)}, bf16[4,64,1024]{2,1,0:T(8,128)(2,1)S(1)}, u32[]{:S(2)}, u32[]{:S(2)}) collective-permute-start(bf16[4,64,1024]{2,1,0:T(8,128)(2,1)} %get-tuple-element.45), channel_id=1, source_target_pairs={{0,2},{2,0},{4,6},{6,4},{8,10},{10,8},{12,14},{14,12},{1,3},{3,1},... | collective-permute-start | bytes 1572872 | tf_op jit(solution)/shard_map/ppermute | solution.py:413
  83.9 19.2 %collective-permute-start.27 = (bf16[384,128]{1,0:T(8,128)(2,1)}, bf16[384,128]{1,0:T(8,128)(2,1)S(1)}, u32[]{:S(2)}, u32[]{:S(2)}) collective-permute-start(bf16[384,128]{1,0:T(8,128)(2,1)} %bitcast.18), channel_id=1, source_target_pairs={{4,0},{8,4},{12,8},{14,12},{10,14},{6,10},{2,6},{0,2},{5,1},{9,5},... | collective-permute-start | bytes 294920 | tf_op jit(solution)/shard_map/ppermute | solution.py:70
  83.9 21.5 %collective-permute-start.26 = (bf16[384,128]{1,0:T(8,128)(2,1)}, bf16[384,128]{1,0:T(8,128)(2,1)S(1)}, u32[]{:S(2)}, u32[]{:S(2)}) collective-permute-start(bf16[384,128]{1,0:T(8,128)(2,1)} %bitcast.19), channel_id=1, source_target_pairs={{0,4},{4,8},{8,12},{12,14},{14,10},{10,6},{6,2},{2,0},{1,5},{5,9},... | collective-permute-start | bytes 294920 | tf_op jit(solution)/shard_map/ppermute | solution.py:69
  127.5 26.7 %collective-permute-start.34 = (bf16[48,128,128]{2,1,0:T(8,128)(2,1)}, bf16[48,128,128]{2,1,0:T(8,128)(2,1)S(1)}, u32[]{:S(2)}, u32[]{:S(2)}) collective-permute-start(bf16[48,128,128]{2,1,0:T(8,128)(2,1)} %grads.1), channel_id=1, source_target_pairs={{0,1},{1,0},{2,3},{3,2},{4,5},{5,4},{6,7},{7,6},{8,9},{9,8},{10,11... | collective-permute-start | bytes 4718600 | tf_op jit(solution)/shard_map/ppermute | solution.py:53
  129.1 13.0 %collective-permute-start.20 = (bf16[64,1024]{1,0:T(8,128)(2,1)S(1)}, bf16[64,1024]{1,0:T(8,128)(2,1)S(1)}, u32[]{:S(2)}, u32[]{:S(2)}) collective-permute-start(bf16[64,1024]{1,0:T(8,128)(2,1)S(1)} %copy-done.25), channel_id=1, source_target_pairs={{0,8},{2,10},{4,12},{6,14},{8,0},{10,2},{12,4},{14,6},{1,9},{3,11}... | collective-permute-start | bytes 393224 | tf_op jit(solution)/shard_map/ppermute | solution.py:422
  132.1 15.2 %collective-permute-start.21 = (bf16[64,1024]{1,0:T(8,128)(2,1)S(1)}, bf16[64,1024]{1,0:T(8,128)(2,1)S(1)}, u32[]{:S(2)}, u32[]{:S(2)}) collective-permute-start(bf16[64,1024]{1,0:T(8,128)(2,1)S(1)} %copy-done.24), channel_id=1, source_target_pairs={{0,12},{2,14},{4,0},{6,2},{8,4},{10,6},{12,8},{14,10},{1,13},{3,15... | collective-permute-start | bytes 393224 | tf_op jit(solution)/shard_map/ppermute | solution.py:422
  135.1 12.2 %collective-permute-start.23 = (bf16[64,1024]{1,0:T(8,128)(2,1)}, bf16[64,1024]{1,0:T(8,128)(2,1)S(1)}, u32[]{:S(2)}, u32[]{:S(2)}) collective-permute-start(bf16[64,1024]{1,0:T(8,128)(2,1)} %get-tuple-element.47), channel_id=1, source_target_pairs={{0,4},{2,6},{4,8},{6,10},{8,12},{10,14},{12,0},{14,2},{1,5},{3,7},... | collective-permute-start | bytes 393224 | tf_op jit(solution)/shard_map/ppermute | solution.py:422
  136.1 16.4 %collective-permute-start.24 = (bf16[64,1024]{1,0:T(8,128)(2,1)}, bf16[64,1024]{1,0:T(8,128)(2,1)S(1)}, u32[]{:S(2)}, u32[]{:S(2)}) collective-permute-start(bf16[64,1024]{1,0:T(8,128)(2,1)} %get-tuple-element.48), channel_id=1, source_target_pairs={{0,8},{2,10},{4,12},{6,14},{8,0},{10,2},{12,4},{14,6},{1,9},{3,11}... | collective-permute-start | bytes 393224 | tf_op jit(solution)/shard_map/ppermute | solution.py:422
  142.1 10.4 %collective-permute-start.25 = (bf16[64,1024]{1,0:T(8,128)(2,1)}, bf16[64,1024]{1,0:T(8,128)(2,1)S(1)}, u32[]{:S(2)}, u32[]{:S(2)}) collective-permute-start(bf16[64,1024]{1,0:T(8,128)(2,1)} %get-tuple-element.49), channel_id=1, source_target_pairs={{0,12},{2,14},{4,0},{6,2},{8,4},{10,6},{12,8},{14,10},{1,13},{3,15... | collective-permute-start | bytes 393224 | tf_op jit(solution)/shard_map/ppermute | solution.py:422
  (38 other events, 396.2 us)

commit v3 on v2

--- a/solution.py
+++ b/solution.py
@@ -25,6 +25,10 @@
     return pltpu.CompilerParams(vmem_limit_bytes=VMEM_LIMIT)
 
 
+def cost(micros):
+    return pl.CostEstimate(flops=0, bytes_accessed=int(micros * 3.5e6), transcendentals=0)
+
+
 def shape(dims, dtype=BF16):
     return jax.ShapeDtypeStruct(dims, dtype)
 
@@ -57,15 +61,23 @@
     return lax.optimization_barrier((block, *others))[0]
 
 
-def ring_gather(block, axis, hold=None):
+def first_part(t):
+    return t * 5 // 8 // 16 * 16
+
+
+def flip(block, axis, bit):
+    return lax.ppermute(block, axis, [(i, i ^ bit) for i in range(lax.axis_size(axis))])
+
+
+def ring_gather(block, axis, ahead):
     count = lax.axis_size(axis)
     onward, back = ring_routes(count)
     half = block.shape[0] // 2
     pieces = [(block, 0, 0)]
     left = right = block
     for step in range(1, count // 2):
-        if hold is not None and step == hold[0]:
-            left, right, _ = lax.optimization_barrier((left, right, hold[1]))
+        if step == 2:
+            left, right, *_ = lax.optimization_barrier((left, right, *ahead))
         left = lax.ppermute(left, axis, onward)
         right = lax.ppermute(right, axis, back)
         pieces.append((left, -step, 0))
@@ -75,14 +87,31 @@
     return pieces
 
 
-def pack_kernel(gd, ud, dd, gr, ur, dr, tokens, cotangent, gate, up, down, *refs):
-    both, own = refs[:2]
-    sends = refs[2 : SPREAD + 1]
-    slab, ids, used = refs[SPREAD + 1 :]
+def join_kernel(tokens, cotangent, both):
+    t = tokens.shape[0]
+    both[:t] = tokens[...]
+    both[t:] = cotangent[...]
+
+
+def join(tokens, cotangent):
+    t, width = tokens.shape
+    return pl.pallas_call(
+        join_kernel,
+        out_shape=shape((2 * t, width)),
+        in_specs=[VMEM] * 2,
+        out_specs=VMEM,
+        compiler_params=params(),
+        name="join",
+        cost_estimate=cost(2),
+    )(tokens, cotangent)
+
+
+def pack_kernel(grid, gd, ud, dd, gr, ur, dr, gate, up, down, after, *refs):
+    own = refs[0]
+    sends = refs[1:SPREAD]
+    slab, ids, used = refs[SPREAD:]
+    me = lax.axis_index("fsdp")
     quarter = 2 * lax.axis_index("groups") + lax.axis_index("section")
-    t = tokens.shape[0]
-    both[0:t] = tokens[...]
-    both[t : 2 * t] = cotangent[...]
     rows = BLK // 4
     slab[...] = jnp.zeros_like(slab)
     own[...] = jnp.zeros_like(own)
@@ -93,6 +122,8 @@
 
         def place(j, carry, kind=kind, dest=dest, row_ids=row_ids, blocks=blocks):
             offset = dest[j]
+            if grid:
+                offset = me ^ lax.rem(me - offset + SPREAD, SPREAD)
             rank = used[offset]
             used[offset] = rank + 1
             slot = kind * CAP + rank
@@ -113,15 +144,13 @@
     own[PER, 0:rows] = ids[0].astype(BF16)
 
 
-def pack(tokens, cotangent, dests, row_ids, blocks):
+def pack(grid, dests, row_ids, blocks, after):
     rows = BLK // 4
-    t, width = tokens.shape
     return pl.pallas_call(
-        pack_kernel,
-        out_shape=[shape((2 * t, width)), shape((PER + 1, BLK, BLK))]
-        + [shape((PER + 1, rows, BLK))] * (SPREAD - 1),
-        in_specs=[SMEM] * 6 + [VMEM] * 5,
-        out_specs=[VMEM] * (SPREAD + 1),
+        functools.partial(pack_kernel, grid),
+        out_shape=[shape((PER + 1, BLK, BLK))] + [shape((PER + 1, rows, BLK))] * (SPREAD - 1),
+        in_specs=[SMEM] * 6 + [VMEM] * 3 + [ANY],
+        out_specs=[VMEM] * SPREAD,
         scratch_shapes=[
             pltpu.VMEM((SPREAD, PER, rows, BLK), BF16),
             pltpu.VMEM((SPREAD, rows, BLK), F32),
@@ -129,7 +158,8 @@
         ],
         compiler_params=params(),
         name="pack",
-    )(*dests, *row_ids, tokens, cotangent, *blocks)
+        cost_estimate=cost(3),
+    )(*dests, *row_ids, *blocks, after)
 
 
 def forward_kernel(layout, tokens_here, split, own, w0, w1, w2, w3, *refs):
@@ -242,16 +272,17 @@
                 piece, column = where(offset, kind, rank)
                 total[piece, :, pl.ds(column, BLK)] += terms[:, rank * BLK : (rank + 1) * BLK]
     if split:
-        side = me % 2
+        h = first_part(t)
         send_a, send_b, keep_a, keep_b = outs
-        h = t // 2
-        for z in range(send_a.shape[0]):
-            away = total[2 * z + 1 - side].astype(BF16)
-            here = total[2 * z + side].astype(BF16)
-            send_a[z] = away[:h]
-            send_b[z] = away[h:]
-            keep_a[z] = here[:h]
-            keep_b[z] = here[h:]
+        for high in range(2):
+            for low in range(2):
+                a = me ^ (2 * high + 4 * low)
+                b = me ^ (4 * high + low)
+                n = 2 * high + low
+                send_a[n] = total[a ^ 1, :h].astype(BF16)
+                keep_a[n] = total[a, :h].astype(BF16)
+                send_b[n] = total[b ^ 2, h:].astype(BF16)
+                keep_b[n] = total[b, h:].astype(BF16)
     else:
         outs[0][...] = total[...].astype(BF16)
     field_copy.wait()
@@ -262,7 +293,8 @@
     t = pieces[0][0].shape[0] // 2
     width = pieces[0][0].shape[1]
     if split:
-        outs = [shape((piece_count // 2, t // 2, width))] * 4
+        rows = first_part(t), t - first_part(t)
+        outs = [shape((piece_count // 2, rows[n % 2], width)) for n in range(4)]
     else:
         outs = [shape((piece_count, t, width))]
     field = (piece_count, 2 * t, width)
@@ -284,46 +316,21 @@
         ],
         compiler_params=params(),
         name="forward",
+        cost_estimate=cost(8),
     )(own, *quarters, *[block for block, _, _ in pieces])
 
 
-def pair_kernel(keep, got, here, one, two, three):
-    z = lax.axis_index("fsdp") // 2
-    for step, ref in enumerate((here, one, two, three)):
-        at = lax.rem(z + step, keep.shape[0])
-        ref[...] = (keep[at].astype(F32) + got[at].astype(F32)).astype(BF16)
-
-
-def pair(keep, got):
-    piece = shape(keep.shape[1:])
-    return pl.pallas_call(
-        pair_kernel,
-        out_shape=[piece] * 4,
-        in_specs=[VMEM, VMEM],
-        out_specs=[VMEM] * 4,
-        compiler_params=params(),
-        name="pair",
-    )(keep, got)
-
-
 def grads_kernel(layout, grid, gd, ud, dd, gr, ur, dr, field, *refs):
-    count = len(layout)
-    arrived = refs[:count]
     out, columns, sems = refs[-3:]
     axis_size = lax.axis_size("fsdp")
     me = lax.axis_index("fsdp")
     t = field.shape[1] // 2
     per_piece = field.shape[2] // BLK
     copies = []
-    for n, (steps, first, length) in enumerate(layout):
-        offset = steps
-        if grid:
-            source = ring_at(ring_place(me, axis_size) + steps, axis_size)
-            offset = (me - source + axis_size) % axis_size
+    for n, (array, row, away) in enumerate(layout):
+        offset = (me - (me ^ away) + axis_size) % axis_size if grid else away
         copies.append(
-            pltpu.make_async_copy(
-                arrived[n], columns.at[offset, first : first + length], sems.at[n]
-            )
+            pltpu.make_async_copy(refs[array].at[row], columns.at[offset], sems.at[n])
         )
     for copy in copies:
         copy.start()
@@ -348,22 +355,22 @@
         lax.fori_loop(0, slots, one, 0, unroll=4)
 
 
-def grads(dests, row_ids, field, pieces, grid, after):
-    layout = [(steps, first, block.shape[0]) for block, steps, first in pieces]
-    rows = pieces[0][0].shape[0]
+def grads(dests, row_ids, field, arrived, layout, grid, after):
+    rows = arrived[0].shape[1]
     slots = dests[0].shape[0]
     return pl.pallas_call(
         functools.partial(grads_kernel, layout, grid),
         out_shape=shape((KINDS * slots, BLK, BLK)),
-        in_specs=[SMEM] * 6 + [VMEM] + [ANY] * (len(pieces) + len(after)),
+        in_specs=[SMEM] * 2 * KINDS + [VMEM] + [ANY] * (len(arrived) + len(after)),
         out_specs=VMEM,
         scratch_shapes=[
             pltpu.VMEM((SPREAD, rows, BLK), BF16),
-            pltpu.SemaphoreType.DMA((len(pieces),)),
+            pltpu.SemaphoreType.DMA((SPREAD,)),
         ],
         compiler_params=params(),
         name="grads",
-    )(*dests, *row_ids, field, *[block for block, _, _ in pieces], *after)
+        cost_estimate=cost(7.5),
+    )(*dests, *row_ids, field, *arrived, *after)
 
 
 def shards(
@@ -385,58 +392,63 @@
     dests = [target[:, 0] for target in (gate_dest, up_dest, down_dest)]
     row_ids = [gate_rows, up_rows, down_rows]
 
-    both, own, *sends = pack(
-        tokens, cotangent, dests, row_ids, (gate_blocks, up_blocks, down_blocks)
-    )
+    both = join(tokens, cotangent)
+    own, *sends = pack(grid, dests, row_ids, (gate_blocks, up_blocks, down_blocks), both)
     if grid:
-        pieces = ring_gather(both, "fsdp")
+        pieces = ring_gather(both, "fsdp", sends)
+        first_step, second_step = ([block for block, _, _ in pieces[n : n + 2]] for n in (1, 3))
+        sends = lax.optimization_barrier((*sends, *first_step))[:-2]
+        slabs = [flip(block, "fsdp", bits) for bits, block in enumerate(sends, 1)]
+        slabs = lax.optimization_barrier((*slabs, *second_step))[:-2]
         piece_count = count
     else:
         pieces = [(lax.all_gather(both, "fsdp", axis=1, tiled=True), 0, 0)]
+        slabs = [shift(block, "fsdp", -d) for d, block in enumerate(sends, 1)]
         piece_count = 1
 
-    mine = jnp.stack([shift(block, "fsdp", -d) for d, block in enumerate(sends, 1)], axis=0)
+    mine = jnp.stack(slabs, axis=0)
     across = swap(mine, "groups")
     beside = swap(mine, "section")
     diagonal = swap(across, "section")
     quarters = (mine, beside, across, diagonal)
     field, columns, *partial_input = forward(own, quarters, pieces, grid, piece_count)
-    flat = columns.reshape(KINDS * t, BLK)
+    flat = columns.reshape(1, KINDS * t, BLK)
 
     if grid:
-        beside_x = [(i, i ^ 1) for i in range(count)]
-        along_z = [
-            [(i, (i + 2 * step) % count) for i in range(count)] for step in range(1, count // 2)
-        ]
         send_a, send_b, keep_a, keep_b = partial_input
-        got_a = lax.ppermute(send_a, "fsdp", beside_x)
-        got_b = lax.ppermute(send_b, "fsdp", beside_x)
-        halves = []
-        for keep, got in ((keep_a, got_a), (keep_b, got_b)):
-            here, *away = pair(keep, got)
-            halves.append((here, [(b, r) for b, r in zip(away, along_z, strict=True)]))
-        sums = []
-        for here, away in halves:
-            result = here.astype(F32)
-            for block, route in away:
-                result = result + lax.ppermute(block, "fsdp", route).astype(F32)
-            sums.append(result.astype(BF16))
-        input_grad = jnp.concatenate(sums, axis=0)
+        got_a = flip(send_a, "fsdp", 1)
+        got_b = flip(send_b, "fsdp", 2)
+        two = jnp.concatenate([flat, flip(flat, "fsdp", 4)], axis=0)
+        four = jnp.concatenate([two, flip(two, "fsdp", 2)], axis=0)
+        four, got_b = lax.optimization_barrier((four, got_b))
+        rest = flip(four, "fsdp", 1)
+        sum_b = keep_b + got_b
+        away_b = tie(sum_b[2:])
+        got_b = flip(away_b, "fsdp", 4)
+        sum_a = keep_a + got_a
+        away_a = tie(sum_a[2:])
+        got_a = flip(away_a, "fsdp", 2)
+        arrived = [four, rest]
+        layout = [(n, row, n + bits) for n in range(2) for row, bits in enumerate((0, 4, 2, 6))]
+        part = grads(dests, row_ids, field, arrived, layout, grid, [away_a, away_b])
+        got_a, got_b, part = lax.optimization_barrier((got_a, got_b, part))
+        sum_a = sum_a[:2] + got_a
+        away_a = tie(sum_a[1:])
+        got_a = flip(away_a, "fsdp", 4)
+        part = tie(part, away_a)
+        sum_b = sum_b[:2] + got_b
+        got_b = flip(sum_b[1:], "fsdp", 1)
+        input_grad = jnp.concatenate([sum_a[0] + got_a[0], sum_b[0] + got_b[0]], axis=0)
     else:
         input_grad = lax.psum_scatter(
             partial_input[0].reshape(t, -1), "fsdp", scatter_dimension=1, tiled=True
         )
-
-    if grid:
-        arrived = ring_gather(flat, "fsdp", (3, halves[0][0]))
-        after = [got_b]
-    else:
-        arrived = [(flat, 0, 0)] + [(shift(flat, "fsdp", d), d, 0) for d in range(1, SPREAD)]
-        after = []
-    part = grads(dests, row_ids, field, arrived, grid, after)
+        arrived = [flat] + [shift(flat, "fsdp", d) for d in range(1, SPREAD)]
+        layout = [(d, 0, d) for d in range(SPREAD)]
+        part = grads(dests, row_ids, field, arrived, layout, grid, [])
+    slots = gate_blocks.shape[0]
     other = swap(part, "section")
     summed = part.astype(F32) + other.astype(F32)
-    slots = gate_blocks.shape[0]
     gate_grad, up_grad, down_grad = (
         summed[kind * slots : (kind + 1) * slots] for kind in range(KINDS)
     )

time: 157 us -> 134 us (0.85)
  starting transfers between devices: 57.9 us -> 32 us
  Pallas kernels: 23.6 us -> 21.2 us
  other arithmetic: 2.36 us -> 4.71 us
  waiting for transfers between devices: 67.7 us -> 69.8 us
    ppermute x15 -> x16, waiting for transfers between devices: 22.1 us -> 47.1 us  [flip(): lax.ppermute(block, axis, [(i, i ^ bit) for i in range(lax.axis_size(axis...]
    ppermute x6 -> x3, waiting for transfers between devices: 32.5 us -> 8.73 us  [ring_gather(): right = lax.ppermute(right, axis, back)]
    ppermute x15 -> x16, starting transfers between devices: 33.9 us -> 20.9 us  [flip(): lax.ppermute(block, axis, [(i, i ^ bit) for i in range(lax.axis_size(axis...]
    ppermute x6 -> x3, starting transfers between devices: 13.2 us -> 6.57 us  [ring_gather(): right = lax.ppermute(right, axis, back)]
    ppermute x4, waiting for transfers between devices: 0.01 us -> 5.86 us  [swap(): return lax.ppermute(block, axis, [(0, 1), (1, 0)])]
    ppermute x2 -> x1, waiting for transfers between devices: 3.85 us -> 0.11 us  [ring_gather(): pieces.append((lax.ppermute(right[half:], axis, back), count // 2, half))]
    ppermute x6 -> x3, starting transfers between devices: 3.98 us -> 0.51 us  [ring_gather(): left = lax.ppermute(left, axis, onward)]
    ppermute x2 -> x1, starting transfers between devices: 4.58 us -> 2.04 us  [ring_gather(): pieces.append((lax.ppermute(right[half:], axis, back), count // 2, half))]
  transfers between devices with their start and end apart: 35 -> 28, of which waited for: 16 -> 16; matrix products, arithmetic and copies ran while one was open for 1% -> 3% of each run, Pallas kernels for 3% -> 8%
where the time goes in v3:
time: 134 us; the launch traced here: 132 us
  waiting for transfers between devices  69.8 us (52%)
  starting transfers between devices  32 us (24%)
  Pallas kernels  21.2 us (16%)
  other arithmetic  4.71 us (4%)
  local copies, waits for them, and re-layouts  3.56 us (3%)
    ppermute x16, waiting for transfers between devices, flip(): lax.ppermute(block, axis, [(i, i ^ bit) for i in range(lax.axis_size(axis...  47.1 us
    ppermute x16, starting transfers between devices, flip(): lax.ppermute(block, axis, [(i, i ^ bit) for i in range(lax.axis_size(axis...  20.9 us
    ppermute x3, waiting for transfers between devices, ring_gather(): right = lax.ppermute(right, axis, back)  8.73 us
    pallas_call x1, Pallas kernels, forward(): pl.pallas_call(functools.partial(forward_kernel, layout, t, int(split)),...  8.56 us
    pallas_call x1, Pallas kernels, grads(): pl.pallas_call(functools.partial(grads_kernel, layout, grid), out_shape=s...  7.4 us
    ppermute x3, starting transfers between devices, ring_gather(): right = lax.ppermute(right, axis, back)  6.57 us
    ppermute x4, waiting for transfers between devices, swap(): return lax.ppermute(block, axis, [(0, 1), (1, 0)])  5.86 us
    ppermute x1, waiting for transfers between devices, ring_gather(): pieces.append((lax.ppermute(left[:half], axis, onward), count // 2, 0))  5.31 us
  transfers between devices with their start and end apart: 28, of which 16 were waited for; matrix products, arithmetic and copies ran while one was open for 3% of the time, Pallas kernels for 8%

profile of v3, /device:TPU:0, one launch (start us, length us, event | category | flops | bytes accessed | tf_op | source)
XLA Modules:
  0.0 132.3 jit_solution(6624661979277347783)
XLA Ops:
  0.6 1.9 %join.1.after.refs_0_ = bf16[256,1024]{1,0:T(8,128)(2,1)} custom-call(bf16[128,1024]{1,0:T(8,128)(2,1)} %tokens.1, bf16[128,1024]{1,0:T(8,128)(2,1)} %cotangent.1), custom_call_target="tpu_custom_call" | custom-call | bytes 7000000 | tf_op jit(solution)/shard_map/join/pallas_call | solution.py:98
  2.5 2.9 %collective-permute-start.1 = (bf16[256,1024]{1,0:T(8,128)(2,1)}, bf16[256,1024]{1,0:T(8,128)(2,1)S(1)}, u32[]{:S(2)}, u32[]{:S(2)}) collective-permute-start(bf16[256,1024]{1,0:T(8,128)(2,1)} %join.1.after.refs_0_), channel_id=1, source_target_pairs={{4,0},{8,4},{12,8},{14,12},{10,14},{6,10},{2,6},{0,2},{5,1},{9,5},... | collective-permute-start | bytes 1572872 | tf_op jit(solution)/shard_map/ppermute | solution.py:82
  5.5 3.4 %pack.1 = (bf16[10,128,128]{2,1,0:T(8,128)(2,1)}, bf16[10,32,128]{2,1,0:T(8,128)(2,1)}, bf16[10,32,128]{2,1,0:T(8,128)(2,1)}, bf16[10,32,128]{2,1,0:T(8,128)(2,1...) custom-call(s32[16]{0:T(128)} %bitcast.25, ...), custom_call_target="tpu_custom_call" | custom-call | bytes 10500000 | tf_op jit(solution)/shard_map/pack/pallas_call | solution.py:149
  8.9 8.7 %collective-permute-done.1.refs_2_ = bf16[256,1024]{1,0:T(8,128)(2,1)S(1)} collective-permute-done((bf16[256,1024]{1,0:T(8,128)(2,1)}, bf16[256,1024]{1,0:T(8,128)(2,1)S(1)}, u32[]{:S(2)}, u32[]{:S(2)}) %collective-permute-start.1) | collective-permute-done | bytes 524320 | tf_op jit(solution)/shard_map/ppermute | solution.py:82
  24.6 9.6 %collective-permute-done.2 = bf16[10,32,128]{2,1,0:T(8,128)(2,1)S(1)} collective-permute-done((bf16[10,32,128]{2,1,0:T(8,128)(2,1)}, bf16[10,32,128]{2,1,0:T(8,128)(2,1)S(1)}, u32[]{:S(2)}, u32[]{:S(2)}) %collective-permute-start.2) | collective-permute-done | bytes 81952 | tf_op jit(solution)/shard_map/ppermute | solution.py:69
  34.6 4.0 %collective-permute-start.6 = (bf16[10,32,128]{2,1,0:T(8,128)(2,1)}, bf16[10,32,128]{2,1,0:T(8,128)(2,1)S(1)}, u32[]{:S(2)}, u32[]{:S(2)}) collective-permute-start(bf16[10,32,128]{2,1,0:T(8,128)(2,1)} %get-tuple-element.52), channel_id=1, source_target_pairs={{0,10},{2,8},{4,14},{6,12},{8,2},{10,0},{12,6},{14,4},{1,11},{3,9}... | collective-permute-start | bytes 245768 | tf_op jit(solution)/shard_map/ppermute | solution.py:69
  38.6 2.9 %collective-permute-start.7 = (bf16[10,32,128]{2,1,0:T(8,128)(2,1)}, bf16[10,32,128]{2,1,0:T(8,128)(2,1)S(1)}, u32[]{:S(2)}, u32[]{:S(2)}) collective-permute-start(bf16[10,32,128]{2,1,0:T(8,128)(2,1)} %get-tuple-element.53), channel_id=1, source_target_pairs={{0,12},{2,14},{4,8},{6,10},{8,4},{10,6},{12,0},{14,2},{1,13},{3,15... | collective-permute-start | bytes 245768 | tf_op jit(solution)/shard_map/ppermute | solution.py:69
  41.6 3.9 %collective-permute-done.5 = bf16[10,32,128]{2,1,0:T(8,128)(2,1)S(1)} collective-permute-done((bf16[10,32,128]{2,1,0:T(8,128)(2,1)}, bf16[10,32,128]{2,1,0:T(8,128)(2,1)S(1)}, u32[]{:S(2)}, u32[]{:S(2)}) %collective-permute-start.5) | collective-permute-done | bytes 81952 | tf_op jit(solution)/shard_map/ppermute | solution.py:69
  47.0 6.3 %collective-permute-done.8 = bf16[10,32,128]{2,1,0:T(8,128)(2,1)S(1)} collective-permute-done((bf16[10,32,128]{2,1,0:T(8,128)(2,1)}, bf16[10,32,128]{2,1,0:T(8,128)(2,1)S(1)}, u32[]{:S(2)}, u32[]{:S(2)}) %collective-permute-start.8) | collective-permute-done | bytes 81952 | tf_op jit(solution)/shard_map/ppermute | solution.py:69
  53.5 1.9 %collective-permute-start.12 = (bf16[7,10,32,128]{3,2,1,0:T(8,128)(2,1)S(1)}, bf16[7,10,32,128]{3,2,1,0:T(8,128)(2,1)S(1)}, u32[]{:S(2)}, u32[]{:S(2)}) collective-permute-start(bf16[7,10,32,128]{3,2,1,0:T(8,128)(2,1)S(1)} %bitcast_dynamic-update-slice_fusion.w0), channel_id=1, source_target_pairs={{0,16},{16,0},{1,17},{17,1},{2,18},{18,2},{3,19},{19,3},{4,20},{20... | collective-permute-start | bytes 1720328 | tf_op jit(solution)/shard_map/ppermute | solution.py:57
  55.4 2.0 %collective-permute-start.15 = (bf16[256,1024]{1,0:T(8,128)(2,1)S(1)}, bf16[256,1024]{1,0:T(8,128)(2,1)S(1)}, u32[]{:S(2)}, u32[]{:S(2)}) collective-permute-start(bf16[256,1024]{1,0:T(8,128)(2,1)S(1)} %collective-permute-done.10.refs_4_), channel_id=1, source_target_pairs={{4,0},{8,4},{12,8},{14,12},{10,14},{6,10},{2,6},{0,2},{5,1},{9,5},... | collective-permute-start | bytes 1572872 | tf_op jit(solution)/shard_map/ppermute | solution.py:82
  57.4 5.8 %collective-permute-done.12.w2 = bf16[7,10,32,128]{3,2,1,0:T(8,128)(2,1)S(1)} collective-permute-done((bf16[7,10,32,128]{3,2,1,0:T(8,128)(2,1)S(1)}, bf16[7,10,32,128]{3,2,1,0:T(8,128)(2,1)S(1)}, u32[]{:S(2)}, u32[]{:S(2)}) %collective-permute-start.12) | collective-permute-done | bytes 573472 | tf_op jit(solution)/shard_map/ppermute | solution.py:57
  64.7 2.0 %collective-permute-start.17 = (bf16[128,1024]{1,0:T(8,128)(2,1)S(1)}, bf16[128,1024]{1,0:T(8,128)(2,1)S(1)}, u32[]{:S(2)}, u32[]{:S(2)}) collective-permute-start(bf16[128,1024]{1,0:T(8,128)(2,1)S(1)} %slice.53), channel_id=1, source_target_pairs={{4,0},{8,4},{12,8},{14,12},{10,14},{6,10},{2,6},{0,2},{5,1},{9,5},... | collective-permute-start | bytes 786440 | tf_op jit(solution)/shard_map/ppermute | solution.py:86
  66.8 5.3 %collective-permute-done.16.refs_7_ = bf16[128,1024]{1,0:T(8,128)(2,1)S(1)} collective-permute-done((bf16[128,1024]{1,0:T(8,128)(2,1)S(1)}, bf16[128,1024]{1,0:T(8,128)(2,1)S(1)}, u32[]{:S(2)}, u32[]{:S(2)}) %collective-permute-start.16) | collective-permute-done | bytes 262176 | tf_op jit(solution)/shard_map/ppermute | solution.py:85
  73.1 8.6 %forward.1 = (bf16[8,256,1024]{2,1,0:T(8,128)(2,1)}, bf16[3,128,128]{2,1,0:T(8,128)(2,1)}, bf16[4,80,1024]{2,1,0:T(8,128)(2,1)}, bf16[4,48,1024]{2,1,0:T(8,128)(...) custom-call(bf16[10,128,128]{2,1,0:T(8,128)(2,1)} %get-tuple-element.40.own, ...), custom_call_target="tpu_custom_call" | custom-call | bytes 28000000 | tf_op jit(solution)/shard_map/forward/pallas_call | solution.py:301
  81.7 1.8 %collective-permute-start.18 = (bf16[4,80,1024]{2,1,0:T(8,128)(2,1)}, bf16[4,80,1024]{2,1,0:T(8,128)(2,1)S(1)}, u32[]{:S(2)}, u32[]{:S(2)}) collective-permute-start(bf16[4,80,1024]{2,1,0:T(8,128)(2,1)} %get-tuple-element.65), channel_id=1, source_target_pairs={{0,2},{2,0},{4,6},{6,4},{8,10},{10,8},{12,14},{14,12},{1,3},{3,1},... | collective-permute-start | bytes 1966088 | tf_op jit(solution)/shard_map/ppermute | solution.py:69
  85.0 4.3 %collective-permute-done.20 = bf16[1,384,128]{2,1,0:T(8,128)(2,1)S(1)} collective-permute-done((bf16[1,384,128]{2,1,0:T(8,128)(2,1)}, bf16[1,384,128]{2,1,0:T(8,128)(2,1)S(1)}, u32[]{:S(2)}, u32[]{:S(2)}) %collective-permute-start.20) | collective-permute-done | bytes 98336 | tf_op jit(solution)/shard_map/ppermute | solution.py:69
  90.2 2.6 %collective-permute-start.21 = (bf16[2,384,128]{2,1,0:T(8,128)(2,1)S(1)}, bf16[2,384,128]{2,1,0:T(8,128)(2,1)S(1)}, u32[]{:S(2)}, u32[]{:S(2)}) collective-permute-start(bf16[2,384,128]{2,1,0:T(8,128)(2,1)S(1)} %pad_maximum_fusion.2), channel_id=1, source_target_pairs={{0,4},{2,6},{4,0},{6,2},{8,12},{10,14},{12,8},{14,10},{1,5},{3,7},... | collective-permute-start | bytes 589832 | tf_op jit(solution)/shard_map/ppermute | solution.py:69
  92.8 7.2 %collective-permute-done.21 = bf16[2,384,128]{2,1,0:T(8,128)(2,1)S(1)} collective-permute-done((bf16[2,384,128]{2,1,0:T(8,128)(2,1)S(1)}, bf16[2,384,128]{2,1,0:T(8,128)(2,1)S(1)}, u32[]{:S(2)}, u32[]{:S(2)}) %collective-permute-start.21) | collective-permute-done | bytes 196640 | tf_op jit(solution)/shard_map/ppermute | solution.py:69
  105.2 5.0 %collective-permute-done.24.refs_1_ = bf16[4,384,128]{2,1,0:T(8,128)(2,1)S(1)} collective-permute-done((bf16[4,384,128]{2,1,0:T(8,128)(2,1)S(1)}, bf16[4,384,128]{2,1,0:T(8,128)(2,1)S(1)}, u32[]{:S(2)}, u32[]{:S(2)}) %collective-permute-start.24) | collective-permute-done | bytes 393248 | tf_op jit(solution)/shard_map/ppermute | solution.py:69
  110.9 7.4 %grads.1 = bf16[48,128,128]{2,1,0:T(8,128)(2,1)} custom-call(s32[16]{0:T(128)} %bitcast.26, s32[16]{0:T(128)} %bitcast.28, s32[16]{0:T(128)} %bitcast.30, s32[16]{0:T(128)} %gr.3, s32[16]{0:T(128)} %ur.3, s32[16]{0:T(128)} %dr.3, bf16[8,256,1024]{2,1,0:T(8,128)(2,1)} %get-tuple-element.70.field, bf16[4,384,128]{2,1,0:T(8,128)(2,1)} %copy-done.1, ...), custom_call_target="tpu_custom_call" | custom-call | bytes 26250000 | tf_op jit(solution)/shard_map/grads/pallas_call | solution.py:361
  119.8 4.0 %collective-permute-done.26 = bf16[1,48,1024]{2,1,0:T(8,128)(2,1)S(1)} collective-permute-done((bf16[1,48,1024]{2,1,0:T(8,128)(2,1)S(1)}, bf16[1,48,1024]{2,1,0:T(8,128)(2,1)S(1)}, u32[]{:S(2)}, u32[]{:S(2)}) %collective-permute-start.26) | collective-permute-done | bytes 98336 | tf_op jit(solution)/shard_map/ppermute | solution.py:69
  123.8 5.4 %collective-permute-done.25 = bf16[1,80,1024]{2,1,0:T(8,128)(2,1)S(1)} collective-permute-done((bf16[1,80,1024]{2,1,0:T(8,128)(2,1)S(1)}, bf16[1,80,1024]{2,1,0:T(8,128)(2,1)S(1)}, u32[]{:S(2)}, u32[]{:S(2)}) %collective-permute-start.25) | collective-permute-done | bytes 163872 | tf_op jit(solution)/shard_map/ppermute | solution.py:69
  130.6 1.7 %fusion.2 = (f32[16,128,128]{2,1,0:T(8,128)}, f32[16,128,128]{2,1,0:T(8,128)}, f32[16,128,128]{2,1,0:T(8,128)}) fusion(f32[48,128,128]{2,1,0:T(8,128)S(1)} %convert_add_fusion), kind=kLoop, calls=%fused_computation.17 | loop fusion | bytes 6291456 | tf_op jit(solution)/shard_map/slice | solution.py:453
  (96 shorter events, 22.5 us)
Async XLA Ops:
  2.5 15.2 %collective-permute-start.1 = (bf16[256,1024]{1,0:T(8,128)(2,1)}, bf16[256,1024]{1,0:T(8,128)(2,1)S(1)}, u32[]{:S(2)}, u32[]{:S(2)}) collective-permute-start(bf16[256,1024]{1,0:T(8,128)(2,1)} %join.1.after.refs_0_), channel_id=1, source_target_pairs={{4,0},{8,4},{12,8},{14,12},{10,14},{6,10},{2,6},{0,2},{5,1},{9,5},... | collective-permute-start | bytes 1572872 | tf_op jit(solution)/shard_map/ppermute | solution.py:82
  5.4 13.6 %collective-permute-start = (bf16[256,1024]{1,0:T(8,128)(2,1)}, bf16[256,1024]{1,0:T(8,128)(2,1)S(1)}, u32[]{:S(2)}, u32[]{:S(2)}) collective-permute-start(bf16[256,1024]{1,0:T(8,128)(2,1)} %join.1.after.refs_0_), channel_id=1, source_target_pairs={{0,4},{4,8},{8,12},{12,14},{14,10},{10,6},{6,2},{2,0},{1,5},{5,9},... | collective-permute-start | bytes 1572872 | tf_op jit(solution)/shard_map/ppermute | solution.py:81
  19.0 34.3 %collective-permute-start.9 = (bf16[256,1024]{1,0:T(8,128)(2,1)S(1)}, bf16[256,1024]{1,0:T(8,128)(2,1)S(1)}, u32[]{:S(2)}, u32[]{:S(2)}) collective-permute-start(bf16[256,1024]{1,0:T(8,128)(2,1)S(1)} %collective-permute-done.refs_1_), channel_id=1, source_target_pairs={{0,4},{4,8},{8,12},{12,14},{14,10},{10,6},{6,2},{2,0},{1,5},{5,9},... | collective-permute-start | bytes 1572872 | tf_op jit(solution)/shard_map/ppermute | solution.py:81
  19.5 33.9 %collective-permute-start.10 = (bf16[256,1024]{1,0:T(8,128)(2,1)S(1)}, bf16[256,1024]{1,0:T(8,128)(2,1)S(1)}, u32[]{:S(2)}, u32[]{:S(2)}) collective-permute-start(bf16[256,1024]{1,0:T(8,128)(2,1)S(1)} %collective-permute-done.1.refs_2_), channel_id=1, source_target_pairs={{4,0},{8,4},{12,8},{14,12},{10,14},{6,10},{2,6},{0,2},{5,1},{9,5},... | collective-permute-start | bytes 1572872 | tf_op jit(solution)/shard_map/ppermute | solution.py:82
  21.1 13.1 %collective-permute-start.2 = (bf16[10,32,128]{2,1,0:T(8,128)(2,1)}, bf16[10,32,128]{2,1,0:T(8,128)(2,1)S(1)}, u32[]{:S(2)}, u32[]{:S(2)}) collective-permute-start(bf16[10,32,128]{2,1,0:T(8,128)(2,1)} %get-tuple-element.48), channel_id=1, source_target_pairs={{0,2},{2,0},{4,6},{6,4},{8,10},{10,8},{12,14},{14,12},{1,3},{3,1},... | collective-permute-start | bytes 245768 | tf_op jit(solution)/shard_map/ppermute | solution.py:69
  22.6 12.0 %collective-permute-start.3 = (bf16[10,32,128]{2,1,0:T(8,128)(2,1)}, bf16[10,32,128]{2,1,0:T(8,128)(2,1)S(1)}, u32[]{:S(2)}, u32[]{:S(2)}) collective-permute-start(bf16[10,32,128]{2,1,0:T(8,128)(2,1)} %get-tuple-element.49), channel_id=1, source_target_pairs={{0,4},{2,6},{4,0},{6,2},{8,12},{10,14},{12,8},{14,10},{1,5},{3,7},... | collective-permute-start | bytes 245768 | tf_op jit(solution)/shard_map/ppermute | solution.py:69
  24.2 14.4 %collective-permute-start.4 = (bf16[10,32,128]{2,1,0:T(8,128)(2,1)}, bf16[10,32,128]{2,1,0:T(8,128)(2,1)S(1)}, u32[]{:S(2)}, u32[]{:S(2)}) collective-permute-start(bf16[10,32,128]{2,1,0:T(8,128)(2,1)} %get-tuple-element.50), channel_id=1, source_target_pairs={{0,6},{2,4},{4,2},{6,0},{8,14},{10,12},{12,10},{14,8},{1,7},{3,5},... | collective-permute-start | bytes 245768 | tf_op jit(solution)/shard_map/ppermute | solution.py:69
  34.1 11.3 %collective-permute-start.5 = (bf16[10,32,128]{2,1,0:T(8,128)(2,1)}, bf16[10,32,128]{2,1,0:T(8,128)(2,1)S(1)}, u32[]{:S(2)}, u32[]{:S(2)}) collective-permute-start(bf16[10,32,128]{2,1,0:T(8,128)(2,1)} %get-tuple-element.51), channel_id=1, source_target_pairs={{0,8},{2,10},{4,12},{6,14},{8,0},{10,2},{12,4},{14,6},{1,9},{3,11}... | collective-permute-start | bytes 245768 | tf_op jit(solution)/shard_map/ppermute | solution.py:69
  34.6 12.4 %collective-permute-start.6 = (bf16[10,32,128]{2,1,0:T(8,128)(2,1)}, bf16[10,32,128]{2,1,0:T(8,128)(2,1)S(1)}, u32[]{:S(2)}, u32[]{:S(2)}) collective-permute-start(bf16[10,32,128]{2,1,0:T(8,128)(2,1)} %get-tuple-element.52), channel_id=1, source_target_pairs={{0,10},{2,8},{4,14},{6,12},{8,2},{10,0},{12,6},{14,4},{1,11},{3,9}... | collective-permute-start | bytes 245768 | tf_op jit(solution)/shard_map/ppermute | solution.py:69
  38.6 8.4 %collective-permute-start.7 = (bf16[10,32,128]{2,1,0:T(8,128)(2,1)}, bf16[10,32,128]{2,1,0:T(8,128)(2,1)S(1)}, u32[]{:S(2)}, u32[]{:S(2)}) collective-permute-start(bf16[10,32,128]{2,1,0:T(8,128)(2,1)} %get-tuple-element.53), channel_id=1, source_target_pairs={{0,12},{2,14},{4,8},{6,10},{8,4},{10,6},{12,0},{14,2},{1,13},{3,15... | collective-permute-start | bytes 245768 | tf_op jit(solution)/shard_map/ppermute | solution.py:69
  45.5 7.8 %collective-permute-start.8 = (bf16[10,32,128]{2,1,0:T(8,128)(2,1)}, bf16[10,32,128]{2,1,0:T(8,128)(2,1)S(1)}, u32[]{:S(2)}, u32[]{:S(2)}) collective-permute-start(bf16[10,32,128]{2,1,0:T(8,128)(2,1)} %get-tuple-element.54), channel_id=1, source_target_pairs={{0,14},{2,12},{4,10},{6,8},{8,6},{10,4},{12,2},{14,0},{1,15},{3,13... | collective-permute-start | bytes 245768 | tf_op jit(solution)/shard_map/ppermute | solution.py:69
  53.5 9.8 %collective-permute-start.12 = (bf16[7,10,32,128]{3,2,1,0:T(8,128)(2,1)S(1)}, bf16[7,10,32,128]{3,2,1,0:T(8,128)(2,1)S(1)}, u32[]{:S(2)}, u32[]{:S(2)}) collective-permute-start(bf16[7,10,32,128]{3,2,1,0:T(8,128)(2,1)S(1)} %bitcast_dynamic-update-slice_fusion.w0), channel_id=1, source_target_pairs={{0,16},{16,0},{1,17},{17,1},{2,18},{18,2},{3,19},{19,3},{4,20},{20... | collective-permute-start | bytes 1720328 | tf_op jit(solution)/shard_map/ppermute | solution.py:57
  55.4 9.2 %collective-permute-start.14 = (bf16[256,1024]{1,0:T(8,128)(2,1)S(1)}, bf16[256,1024]{1,0:T(8,128)(2,1)S(1)}, u32[]{:S(2)}, u32[]{:S(2)}) collective-permute-start(bf16[256,1024]{1,0:T(8,128)(2,1)S(1)} %collective-permute-done.9.refs_3_), channel_id=1, source_target_pairs={{0,4},{4,8},{8,12},{12,14},{14,10},{10,6},{6,2},{2,0},{1,5},{5,9},... | collective-permute-start | bytes 1572872 | tf_op jit(solution)/shard_map/ppermute | solution.py:81
  55.4 9.3 %collective-permute-start.15 = (bf16[256,1024]{1,0:T(8,128)(2,1)S(1)}, bf16[256,1024]{1,0:T(8,128)(2,1)S(1)}, u32[]{:S(2)}, u32[]{:S(2)}) collective-permute-start(bf16[256,1024]{1,0:T(8,128)(2,1)S(1)} %collective-permute-done.10.refs_4_), channel_id=1, source_target_pairs={{4,0},{8,4},{12,8},{14,12},{10,14},{6,10},{2,6},{0,2},{5,1},{9,5},... | collective-permute-start | bytes 1572872 | tf_op jit(solution)/shard_map/ppermute | solution.py:82
  57.4 9.3 %collective-permute-start.11 = (bf16[7,10,32,128]{3,2,1,0:T(8,128)(2,1)S(1)}, bf16[7,10,32,128]{3,2,1,0:T(8,128)(2,1)S(1)}, u32[]{:S(2)}, u32[]{:S(2)}) collective-permute-start(bf16[7,10,32,128]{3,2,1,0:T(8,128)(2,1)S(1)} %bitcast_dynamic-update-slice_fusion.w0), channel_id=1, source_target_pairs={{0,1},{1,0},{2,3},{3,2},{4,5},{5,4},{6,7},{7,6},{8,9},{9,8},{10,11... | collective-permute-start | bytes 1720328 | tf_op jit(solution)/shard_map/ppermute | solution.py:57
  63.3 8.9 %collective-permute-start.13 = (bf16[7,10,32,128]{3,2,1,0:T(8,128)(2,1)S(1)}, bf16[7,10,32,128]{3,2,1,0:T(8,128)(2,1)S(1)}, u32[]{:S(2)}, u32[]{:S(2)}) collective-permute-start(bf16[7,10,32,128]{3,2,1,0:T(8,128)(2,1)S(1)} %collective-permute-done.12.w2), channel_id=1, source_target_pairs={{0,1},{1,0},{2,3},{3,2},{4,5},{5,4},{6,7},{7,6},{8,9},{9,8},{10,11... | collective-permute-start | bytes 1720328 | tf_op jit(solution)/shard_map/ppermute | solution.py:57
  81.7 19.7 %collective-permute-start.18 = (bf16[4,80,1024]{2,1,0:T(8,128)(2,1)}, bf16[4,80,1024]{2,1,0:T(8,128)(2,1)S(1)}, u32[]{:S(2)}, u32[]{:S(2)}) collective-permute-start(bf16[4,80,1024]{2,1,0:T(8,128)(2,1)} %get-tuple-element.65), channel_id=1, source_target_pairs={{0,2},{2,0},{4,6},{6,4},{8,10},{10,8},{12,14},{14,12},{1,3},{3,1},... | collective-permute-start | bytes 1966088 | tf_op jit(solution)/shard_map/ppermute | solution.py:69
  84.7 16.2 %collective-permute-start.22 = (bf16[4,48,1024]{2,1,0:T(8,128)(2,1)}, bf16[4,48,1024]{2,1,0:T(8,128)(2,1)S(1)}, u32[]{:S(2)}, u32[]{:S(2)}) collective-permute-start(bf16[4,48,1024]{2,1,0:T(8,128)(2,1)} %get-tuple-element.68), channel_id=1, source_target_pairs={{0,4},{2,6},{4,0},{6,2},{8,12},{10,14},{12,8},{14,10},{1,5},{3,7},... | collective-permute-start | bytes 1179656 | tf_op jit(solution)/shard_map/ppermute | solution.py:69
  90.2 9.8 %collective-permute-start.21 = (bf16[2,384,128]{2,1,0:T(8,128)(2,1)S(1)}, bf16[2,384,128]{2,1,0:T(8,128)(2,1)S(1)}, u32[]{:S(2)}, u32[]{:S(2)}) collective-permute-start(bf16[2,384,128]{2,1,0:T(8,128)(2,1)S(1)} %pad_maximum_fusion.2), channel_id=1, source_target_pairs={{0,4},{2,6},{4,0},{6,2},{8,12},{10,14},{12,8},{14,10},{1,5},{3,7},... | collective-permute-start | bytes 589832 | tf_op jit(solution)/shard_map/ppermute | solution.py:69
  100.9 9.2 %collective-permute-start.24 = (bf16[4,384,128]{2,1,0:T(8,128)(2,1)S(1)}, bf16[4,384,128]{2,1,0:T(8,128)(2,1)S(1)}, u32[]{:S(2)}, u32[]{:S(2)}) collective-permute-start(bf16[4,384,128]{2,1,0:T(8,128)(2,1)S(1)} %pad_maximum_fusion.refs_0_), channel_id=1, source_target_pairs={{0,2},{2,0},{4,6},{6,4},{8,10},{10,8},{12,14},{14,12},{1,3},{3,1},... | collective-permute-start | bytes 1179656 | tf_op jit(solution)/shard_map/ppermute | solution.py:69
  102.8 15.6 %collective-permute-start.19 = (bf16[2,80,1024]{2,1,0:T(8,128)(2,1)S(1)}, bf16[2,80,1024]{2,1,0:T(8,128)(2,1)S(1)}, u32[]{:S(2)}, u32[]{:S(2)}) collective-permute-start(bf16[2,80,1024]{2,1,0:T(8,128)(2,1)S(1)} %slice.55.refs_2_), channel_id=1, source_target_pairs={{0,4},{2,6},{4,0},{6,2},{8,12},{10,14},{12,8},{14,10},{1,5},{3,7},... | collective-permute-start | bytes 983048 | tf_op jit(solution)/shard_map/ppermute | solution.py:69
  103.6 14.8 %collective-permute-start.23 = (bf16[2,48,1024]{2,1,0:T(8,128)(2,1)S(1)}, bf16[2,48,1024]{2,1,0:T(8,128)(2,1)S(1)}, u32[]{:S(2)}, u32[]{:S(2)}) collective-permute-start(bf16[2,48,1024]{2,1,0:T(8,128)(2,1)S(1)} %slice.56.refs_3_), channel_id=1, source_target_pairs={{0,8},{2,10},{4,12},{6,14},{8,0},{10,2},{12,4},{14,6},{1,9},{3,11}... | collective-permute-start | bytes 589832 | tf_op jit(solution)/shard_map/ppermute | solution.py:69
  118.4 11.6 %collective-permute-start.27 = (bf16[48,128,128]{2,1,0:T(8,128)(2,1)}, bf16[48,128,128]{2,1,0:T(8,128)(2,1)S(1)}, u32[]{:S(2)}, u32[]{:S(2)}) collective-permute-start(bf16[48,128,128]{2,1,0:T(8,128)(2,1)} %grads.1), channel_id=1, source_target_pairs={{0,1},{1,0},{2,3},{3,2},{4,5},{5,4},{6,7},{7,6},{8,9},{9,8},{10,11... | collective-permute-start | bytes 4718600 | tf_op jit(solution)/shard_map/ppermute | solution.py:57
  119.0 10.2 %collective-permute-start.25 = (bf16[1,80,1024]{2,1,0:T(8,128)(2,1)S(1)}, bf16[1,80,1024]{2,1,0:T(8,128)(2,1)S(1)}, u32[]{:S(2)}, u32[]{:S(2)}) collective-permute-start(bf16[1,80,1024]{2,1,0:T(8,128)(2,1)S(1)} %slice.58), channel_id=1, source_target_pairs={{0,8},{2,10},{4,12},{6,14},{8,0},{10,2},{12,4},{14,6},{1,9},{3,11}... | collective-permute-start | bytes 491528 | tf_op jit(solution)/shard_map/ppermute | solution.py:69
  (22 other events, 279.7 us)

commit v4 on v3

--- a/solution.py
+++ b/solution.py
@@ -12,7 +12,9 @@
 CAP = 3
 KINDS = 3
 PER = KINDS * CAP
-VMEM_LIMIT = 56 * 1024 * 1024
+EARLY = (4, 5, 1, 2)
+BEFORE_THIRD = ()
+MIB = 1024 * 1024
 
 F32 = jnp.float32
 BF16 = jnp.bfloat16
@@ -21,8 +23,8 @@
 SMEM = pl.BlockSpec(memory_space=pltpu.SMEM)
 
 
-def params():
-    return pltpu.CompilerParams(vmem_limit_bytes=VMEM_LIMIT)
+def params(mebibytes):
+    return pltpu.CompilerParams(vmem_limit_bytes=mebibytes * MIB)
 
 
 def cost(micros):
@@ -31,6 +33,10 @@
 
 def shape(dims, dtype=BF16):
     return jax.ShapeDtypeStruct(dims, dtype)
+
+
+def near(arrays):
+    return [pltpu.with_memory_space_constraint(array, pltpu.VMEM) for array in arrays]
 
 
 def ring_at(place, count):
@@ -69,22 +75,9 @@
     return lax.ppermute(block, axis, [(i, i ^ bit) for i in range(lax.axis_size(axis))])
 
 
-def ring_gather(block, axis, ahead):
-    count = lax.axis_size(axis)
-    onward, back = ring_routes(count)
-    half = block.shape[0] // 2
-    pieces = [(block, 0, 0)]
-    left = right = block
-    for step in range(1, count // 2):
-        if step == 2:
-            left, right, *_ = lax.optimization_barrier((left, right, *ahead))
-        left = lax.ppermute(left, axis, onward)
-        right = lax.ppermute(right, axis, back)
-        pieces.append((left, -step, 0))
-        pieces.append((right, step, 0))
-    pieces.append((lax.ppermute(left[:half], axis, onward), count // 2, 0))
-    pieces.append((lax.ppermute(right[half:], axis, back), count // 2, half))
-    return pieces
+def ring_step(left, right, axis):
+    onward, back = ring_routes(lax.axis_size(axis))
+    return lax.ppermute(left, axis, onward), lax.ppermute(right, axis, back)
 
 
 def join_kernel(tokens, cotangent, both):
@@ -100,7 +93,7 @@
         out_shape=shape((2 * t, width)),
         in_specs=[VMEM] * 2,
         out_specs=VMEM,
-        compiler_params=params(),
+        compiler_params=params(56),
         name="join",
         cost_estimate=cost(2),
     )(tokens, cotangent)
@@ -156,7 +149,7 @@
             pltpu.VMEM((SPREAD, rows, BLK), F32),
             pltpu.SMEM((SPREAD,), jnp.int32),
         ],
-        compiler_params=params(),
+        compiler_params=params(56),
         name="pack",
         cost_estimate=cost(3),
     )(*dests, *row_ids, *blocks, after)
@@ -243,16 +236,10 @@
     gate = jnp.dot(left[0], block_group(0), preferred_element_type=F32)
     upper = jnp.dot(left[1], block_group(1), preferred_element_type=F32)
     nt = (((1,), (1,)), ((), ()))
-    hidden_grad = jnp.zeros((t, BLK), F32)
-    for offset in range(SPREAD):
-        for rank in range(CAP):
-            n = offset * CAP + rank
-            hidden_grad = hidden_grad + lax.dot_general(
-                left[2, :, n * BLK : (n + 1) * BLK],
-                weights[offset, 2 * CAP + rank],
-                nt,
-                preferred_element_type=F32,
-            )
+    across = jnp.concatenate(
+        [weights[n // CAP, 2 * CAP + n % CAP] for n in range(SPREAD * CAP)], axis=1
+    )
+    hidden_grad = lax.dot_general(left[2], across, nt, preferred_element_type=F32)
     sigma = 1.0 / (1.0 + jnp.exp(-gate))
     hidden = (gate * sigma * upper).astype(BF16)
     gate_d = (hidden_grad * upper * sigma * (1.0 + gate * (1.0 - sigma))).astype(BF16)
@@ -314,10 +301,10 @@
             pltpu.SemaphoreType.DMA((len(pieces),)),
             pltpu.SemaphoreType.DMA((9,)),
         ],
-        compiler_params=params(),
+        compiler_params=params(32),
         name="forward",
         cost_estimate=cost(8),
-    )(own, *quarters, *[block for block, _, _ in pieces])
+    )(own, *(near if split else list)([*quarters, *[block for block, _, _ in pieces]]))
 
 
 def grads_kernel(layout, grid, gd, ud, dd, gr, ur, dr, field, *refs):
@@ -352,7 +339,7 @@
             ).astype(BF16)
             return carry
 
-        lax.fori_loop(0, slots, one, 0, unroll=4)
+        lax.fori_loop(0, slots, one, 0, unroll=16)
 
 
 def grads(dests, row_ids, field, arrived, layout, grid, after):
@@ -367,7 +354,7 @@
             pltpu.VMEM((SPREAD, rows, BLK), BF16),
             pltpu.SemaphoreType.DMA((SPREAD,)),
         ],
-        compiler_params=params(),
+        compiler_params=params(32),
         name="grads",
         cost_estimate=cost(7.5),
     )(*dests, *row_ids, field, *arrived, *after)
@@ -395,11 +382,24 @@
     both = join(tokens, cotangent)
     own, *sends = pack(grid, dests, row_ids, (gate_blocks, up_blocks, down_blocks), both)
     if grid:
-        pieces = ring_gather(both, "fsdp", sends)
-        first_step, second_step = ([block for block, _, _ in pieces[n : n + 2]] for n in (1, 3))
-        sends = lax.optimization_barrier((*sends, *first_step))[:-2]
-        slabs = [flip(block, "fsdp", bits) for bits, block in enumerate(sends, 1)]
-        slabs = lax.optimization_barrier((*slabs, *second_step))[:-2]
+        slabs = {}
+        steps = [ring_step(both, both, "fsdp")]
+        for bits in EARLY:
+            slabs[bits] = flip(sends[bits - 1], "fsdp", bits)
+        held = lax.optimization_barrier((*steps[0], *slabs.values()))
+        steps.append(ring_step(*held[:2], "fsdp"))
+        for bits in range(1, SPREAD):
+            if bits not in EARLY:
+                slabs[bits] = flip(tie(sends[bits - 1], *steps[0]), "fsdp", bits)
+        held = lax.optimization_barrier((*steps[1], *[slabs[bits] for bits in BEFORE_THIRD]))
+        steps.append(ring_step(*held[:2], "fsdp"))
+        left, right = steps[2]
+        steps.append(ring_step(left[:t], right[t:], "fsdp"))
+        pieces = [(both, 0, 0)]
+        for step, (left, right) in enumerate(steps, 1):
+            pieces += [(left, -step, 0), (right, step, t if step == count // 2 else 0)]
+        slabs = [slabs[bits] for bits in range(1, SPREAD)]
+        slabs = lax.optimization_barrier((*slabs, *steps[1]))[:-2]
         piece_count = count
     else:
         pieces = [(lax.all_gather(both, "fsdp", axis=1, tiled=True), 0, 0)]

time: 134 us -> 123 us (0.918); the launches traced: 132 us -> 123 us
  Pallas kernels: 21.2 us -> 13.1 us
  waiting for transfers between devices: 69.8 us -> 74.8 us
  other arithmetic: 4.71 us -> 1.8 us
  starting transfers between devices: 32 us -> 29.3 us
    ppermute x16, waiting for transfers between devices: 47.1 us -> 57.8 us  [flip(): lax.ppermute(block, axis, [(i, i ^ bit) for i in range(lax.axis_size(axis...]
    ppermute x8, waiting for transfers between devices: 16.8 us -> 9.23 us  [ring_step(): return (lax.ppermute(left, axis, onward), lax.ppermute(right, axis, back))]
    pallas_call x1, Pallas kernels: 7.4 us -> 2.45 us  [grads(): pl.pallas_call(functools.partial(grads_kernel, layout, grid), out_shape=s...]
    pallas_call x1, Pallas kernels: 8.56 us -> 5.43 us  [forward(): pl.pallas_call(functools.partial(forward_kernel, layout, t, int(split)),...]
    ppermute x16, starting transfers between devices: 20.9 us -> 17.8 us  [flip(): lax.ppermute(block, axis, [(i, i ^ bit) for i in range(lax.axis_size(axis...]
    ppermute x4, waiting for transfers between devices: 5.86 us -> 7.79 us  [swap(): return lax.ppermute(block, axis, [(0, 1), (1, 0)])]
  transfers between devices with their start and end apart: 28 -> 28, of which waited for: 16 -> 15; matrix products, arithmetic and copies ran while one was open for 3% -> 1% of each run, Pallas kernels for 8% -> 5%
where the time goes in v4:
time: 123 us
  waiting for transfers between devices  74.8 us (61%)
  starting transfers between devices  29.3 us (24%)
  Pallas kernels  13.1 us (11%)
  local copies, waits for them, and re-layouts  2.95 us (2%)
  other arithmetic  1.8 us (1%)
    ppermute x16, waiting for transfers between devices, flip(): lax.ppermute(block, axis, [(i, i ^ bit) for i in range(lax.axis_size(axis...  57.8 us
    ppermute x16, starting transfers between devices, flip(): lax.ppermute(block, axis, [(i, i ^ bit) for i in range(lax.axis_size(axis...  17.8 us
    ppermute x8, starting transfers between devices, ring_step(): return (lax.ppermute(left, axis, onward), lax.ppermute(right, axis, back))  9.79 us
    ppermute x8, waiting for transfers between devices, ring_step(): return (lax.ppermute(left, axis, onward), lax.ppermute(right, axis, back))  9.23 us
    ppermute x4, waiting for transfers between devices, swap(): return lax.ppermute(block, axis, [(0, 1), (1, 0)])  7.79 us
    pallas_call x1, Pallas kernels, forward(): pl.pallas_call(functools.partial(forward_kernel, layout, t, int(split)),...  5.43 us
    pallas_call x1, Pallas kernels, pack(): pl.pallas_call(functools.partial(pack_kernel, grid), out_shape=[shape((PE...  3.38 us
  transfers between devices with their start and end apart: 28, of which 15 were waited for; matrix products, arithmetic and copies ran while one was open for 1% of the time, Pallas kernels for 5%

profile of v4, /device:TPU:0, one launch (start us, length us, event | category | flops | bytes accessed | tf_op | source)
XLA Modules:
  0.0 122.9 jit_solution(13826184180193289503)
XLA Ops:
  0.6 1.9 %join.1.after.refs_0_ = bf16[256,1024]{1,0:T(8,128)(2,1)} custom-call(bf16[128,1024]{1,0:T(8,128)(2,1)} %tokens.1, bf16[128,1024]{1,0:T(8,128)(2,1)} %cotangent.1), custom_call_target="tpu_custom_call" | custom-call | bytes 7000000 | tf_op jit(solution)/shard_map/join/pallas_call | solution.py:91
  2.5 2.9 %collective-permute-start.3 = (bf16[256,1024]{1,0:T(8,128)(2,1)}, bf16[256,1024]{1,0:T(8,128)(2,1)S(1)}, u32[]{:S(2)}, u32[]{:S(2)}) collective-permute-start(bf16[256,1024]{1,0:T(8,128)(2,1)} %join.1.after.refs_0_), channel_id=1, source_target_pairs={{4,0},{8,4},{12,8},{14,12},{10,14},{6,10},{2,6},{0,2},{5,1},{9,5},... | collective-permute-start | bytes 1572872 | tf_op jit(solution)/shard_map/ppermute | solution.py:80
  5.5 3.4 %pack.1 = (bf16[10,128,128]{2,1,0:T(8,128)(2,1)}, bf16[10,32,128]{2,1,0:T(8,128)(2,1)}, bf16[10,32,128]{2,1,0:T(8,128)(2,1)}, bf16[10,32,128]{2,1,0:T(8,128)(2,1...) custom-call(s32[16]{0:T(128)} %bitcast.25, ...), custom_call_target="tpu_custom_call" | custom-call | bytes 10500000 | tf_op jit(solution)/shard_map/pack/pallas_call | solution.py:142
  8.9 2.0 %collective-permute-start = (bf16[10,32,128]{2,1,0:T(8,128)(2,1)}, bf16[10,32,128]{2,1,0:T(8,128)(2,1)S(1)}, u32[]{:S(2)}, u32[]{:S(2)}) collective-permute-start(bf16[10,32,128]{2,1,0:T(8,128)(2,1)} %get-tuple-element.39), channel_id=1, source_target_pairs={{0,2},{2,0},{4,6},{6,4},{8,10},{10,8},{12,14},{14,12},{1,3},{3,1},... | collective-permute-start | bytes 245768 | tf_op jit(solution)/shard_map/ppermute | solution.py:75
  12.5 2.6 %collective-permute-start.5 = (bf16[10,32,128]{2,1,0:T(8,128)(2,1)}, bf16[10,32,128]{2,1,0:T(8,128)(2,1)S(1)}, u32[]{:S(2)}, u32[]{:S(2)}) collective-permute-start(bf16[10,32,128]{2,1,0:T(8,128)(2,1)} %get-tuple-element.43), channel_id=1, source_target_pairs={{0,8},{2,10},{4,12},{6,14},{8,0},{10,2},{12,4},{14,6},{1,9},{3,11}... | collective-permute-start | bytes 245768 | tf_op jit(solution)/shard_map/ppermute | solution.py:75
  15.1 5.7 %collective-permute-done = bf16[10,32,128]{2,1,0:T(8,128)(2,1)S(1)} collective-permute-done((bf16[10,32,128]{2,1,0:T(8,128)(2,1)}, bf16[10,32,128]{2,1,0:T(8,128)(2,1)S(1)}, u32[]{:S(2)}, u32[]{:S(2)}) %collective-permute-start) | collective-permute-done | bytes 81952 | tf_op jit(solution)/shard_map/ppermute | solution.py:75
  21.2 7.9 %collective-permute-done.6 = bf16[10,32,128]{2,1,0:T(8,128)(2,1)S(1)} collective-permute-done((bf16[10,32,128]{2,1,0:T(8,128)(2,1)}, bf16[10,32,128]{2,1,0:T(8,128)(2,1)S(1)}, u32[]{:S(2)}, u32[]{:S(2)}) %collective-permute-start.6) | collective-permute-done | bytes 81952 | tf_op jit(solution)/shard_map/ppermute | solution.py:75
  29.1 2.0 %collective-permute-start.10 = (bf16[256,1024]{1,0:T(8,128)(2,1)S(1)}, bf16[256,1024]{1,0:T(8,128)(2,1)S(1)}, u32[]{:S(2)}, u32[]{:S(2)}) collective-permute-start(bf16[256,1024]{1,0:T(8,128)(2,1)S(1)} %collective-permute-done.3.refs_2_), channel_id=1, source_target_pairs={{4,0},{8,4},{12,8},{14,12},{10,14},{6,10},{2,6},{0,2},{5,1},{9,5},... | collective-permute-start | bytes 1572872 | tf_op jit(solution)/shard_map/ppermute | solution.py:80
  31.1 2.1 %collective-permute-start.8 = (bf16[10,32,128]{2,1,0:T(8,128)(2,1)}, bf16[10,32,128]{2,1,0:T(8,128)(2,1)S(1)}, u32[]{:S(2)}, u32[]{:S(2)}) collective-permute-start(bf16[10,32,128]{2,1,0:T(8,128)(2,1)} %get-tuple-element.48), channel_id=1, source_target_pairs={{0,14},{2,12},{4,10},{6,8},{8,6},{10,4},{12,2},{14,0},{1,15},{3,13... | collective-permute-start | bytes 245768 | tf_op jit(solution)/shard_map/ppermute | solution.py:75
  34.4 10.1 %collective-permute-done.8 = bf16[10,32,128]{2,1,0:T(8,128)(2,1)S(1)} collective-permute-done((bf16[10,32,128]{2,1,0:T(8,128)(2,1)}, bf16[10,32,128]{2,1,0:T(8,128)(2,1)S(1)}, u32[]{:S(2)}, u32[]{:S(2)}) %collective-permute-start.8) | collective-permute-done | bytes 81952 | tf_op jit(solution)/shard_map/ppermute | solution.py:75
  48.0 2.1 %collective-permute-start.14 = (bf16[256,1024]{1,0:T(8,128)(2,1)S(1)}, bf16[256,1024]{1,0:T(8,128)(2,1)S(1)}, u32[]{:S(2)}, u32[]{:S(2)}) collective-permute-start(bf16[256,1024]{1,0:T(8,128)(2,1)S(1)} %collective-permute-done.9.refs_3_), channel_id=1, source_target_pairs={{0,4},{4,8},{8,12},{12,14},{14,10},{10,6},{6,2},{2,0},{1,5},{5,9},... | collective-permute-start | bytes 1572872 | tf_op jit(solution)/shard_map/ppermute | solution.py:80
  50.1 7.8 %collective-permute-done.12.w2 = bf16[7,10,32,128]{3,2,1,0:T(8,128)(2,1)S(1)} collective-permute-done((bf16[7,10,32,128]{3,2,1,0:T(8,128)(2,1)S(1)}, bf16[7,10,32,128]{3,2,1,0:T(8,128)(2,1)S(1)}, u32[]{:S(2)}, u32[]{:S(2)}) %collective-permute-start.12) | collective-permute-done | bytes 573472 | tf_op jit(solution)/shard_map/ppermute | solution.py:63
  58.9 2.5 %collective-permute-start.16 = (bf16[128,1024]{1,0:T(8,128)(2,1)S(1)}, bf16[128,1024]{1,0:T(8,128)(2,1)S(1)}, u32[]{:S(2)}, u32[]{:S(2)}) collective-permute-start(bf16[128,1024]{1,0:T(8,128)(2,1)S(1)} %slice.52), channel_id=1, source_target_pairs={{0,4},{4,8},{8,12},{12,14},{14,10},{10,6},{6,2},{2,0},{1,5},{5,9},... | collective-permute-start | bytes 786440 | tf_op jit(solution)/shard_map/ppermute | solution.py:80
  61.6 6.0 %collective-permute-done.16.refs_7_ = bf16[128,1024]{1,0:T(8,128)(2,1)S(1)} collective-permute-done((bf16[128,1024]{1,0:T(8,128)(2,1)S(1)}, bf16[128,1024]{1,0:T(8,128)(2,1)S(1)}, u32[]{:S(2)}, u32[]{:S(2)}) %collective-permute-start.16) | collective-permute-done | bytes 262176 | tf_op jit(solution)/shard_map/ppermute | solution.py:80
  67.5 2.3 %collective-permute-done.17.refs_8_ = bf16[128,1024]{1,0:T(8,128)(2,1)S(1)} collective-permute-done((bf16[128,1024]{1,0:T(8,128)(2,1)S(1)}, bf16[128,1024]{1,0:T(8,128)(2,1)S(1)}, u32[]{:S(2)}, u32[]{:S(2)}) %collective-permute-start.17) | collective-permute-done | bytes 262176 | tf_op jit(solution)/shard_map/ppermute | solution.py:80
  70.8 5.4 %forward.1 = (bf16[8,256,1024]{2,1,0:T(8,128)(2,1)S(1)}, bf16[3,128,128]{2,1,0:T(8,128)(2,1)S(1)}, bf16[4,80,1024]{2,1,0:T(8,128)(2,1)S(1)}, bf16[4,48,1024]{2,1...) custom-call(bf16[10,128,128]{2,1,0:T(8,128)(2,1)S(1)} %copy-done.1, ...), custom_call_target="tpu_custom_call" | custom-call | bytes 28000000 | tf_op jit(solution)/shard_map/forward/pallas_call | solution.py:288
  78.8 4.8 %collective-permute-done.20 = bf16[1,384,128]{2,1,0:T(8,128)(2,1)S(1)} collective-permute-done((bf16[1,384,128]{2,1,0:T(8,128)(2,1)S(1)}, bf16[1,384,128]{2,1,0:T(8,128)(2,1)S(1)}, u32[]{:S(2)}, u32[]{:S(2)}) %collective-permute-start.20) | collective-permute-done | bytes 98336 | tf_op jit(solution)/shard_map/ppermute | solution.py:75
  83.8 10.5 %collective-permute-done.21 = bf16[2,384,128]{2,1,0:T(8,128)(2,1)S(1)} collective-permute-done((bf16[2,384,128]{2,1,0:T(8,128)(2,1)S(1)}, bf16[2,384,128]{2,1,0:T(8,128)(2,1)S(1)}, u32[]{:S(2)}, u32[]{:S(2)}) %collective-permute-start.21) | collective-permute-done | bytes 196640 | tf_op jit(solution)/shard_map/ppermute | solution.py:75
  95.6 1.8 %collective-permute-start.23 = (bf16[2,48,1024]{2,1,0:T(8,128)(2,1)S(1)}, bf16[2,48,1024]{2,1,0:T(8,128)(2,1)S(1)}, u32[]{:S(2)}, u32[]{:S(2)}) collective-permute-start(bf16[2,48,1024]{2,1,0:T(8,128)(2,1)S(1)} %slice.56.refs_3_), channel_id=1, source_target_pairs={{0,8},{2,10},{4,12},{6,14},{8,0},{10,2},{12,4},{14,6},{1,9},{3,11}... | collective-permute-start | bytes 589832 | tf_op jit(solution)/shard_map/ppermute | solution.py:75
  97.5 6.8 %collective-permute-done.24.refs_1_ = bf16[4,384,128]{2,1,0:T(8,128)(2,1)S(1)} collective-permute-done((bf16[4,384,128]{2,1,0:T(8,128)(2,1)S(1)}, bf16[4,384,128]{2,1,0:T(8,128)(2,1)S(1)}, u32[]{:S(2)}, u32[]{:S(2)}) %collective-permute-start.24) | collective-permute-done | bytes 393248 | tf_op jit(solution)/shard_map/ppermute | solution.py:75
  104.3 2.4 %grads.1 = bf16[48,128,128]{2,1,0:T(8,128)(2,1)S(1)} custom-call(s32[16]{0:T(128)S(1)} %bitcast.26, s32[16]{0:T(128)S(1)} %bitcast.28, s32[16]{0:T(128)S(1)} %bitcast.30, s32[16]{0:T(128)S(1)} %copy-done.5, s32[16]{0:T(128)S(1)} %copy-done.6, s32[16]{0:T(128)S(1)} %copy-done.7, bf16[8,256,1024]{2,1,0:T(8,128)(2,1)S(1)} %get-tuple-element.66.field, ...), custom_call_target="tpu_custom_call" | custom-call | bytes 26250000 | tf_op jit(solution)/shard_map/grads/pallas_call | solution.py:348
  107.7 1.8 %collective-permute-start.26 = (bf16[1,48,1024]{2,1,0:T(8,128)(2,1)S(1)}, bf16[1,48,1024]{2,1,0:T(8,128)(2,1)S(1)}, u32[]{:S(2)}, u32[]{:S(2)}) collective-permute-start(bf16[1,48,1024]{2,1,0:T(8,128)(2,1)S(1)} %slice.61), channel_id=1, source_target_pairs={{0,2},{2,0},{4,6},{6,4},{8,10},{10,8},{12,14},{14,12},{1,3},{3,1},... | collective-permute-start | bytes 294920 | tf_op jit(solution)/shard_map/ppermute | solution.py:75
  110.6 2.3 %collective-permute-done.26 = bf16[1,48,1024]{2,1,0:T(8,128)(2,1)S(1)} collective-permute-done((bf16[1,48,1024]{2,1,0:T(8,128)(2,1)S(1)}, bf16[1,48,1024]{2,1,0:T(8,128)(2,1)S(1)}, u32[]{:S(2)}, u32[]{:S(2)}) %collective-permute-start.26) | collective-permute-done | bytes 98336 | tf_op jit(solution)/shard_map/ppermute | solution.py:75
  112.9 6.9 %collective-permute-done.25 = bf16[1,80,1024]{2,1,0:T(8,128)(2,1)S(1)} collective-permute-done((bf16[1,80,1024]{2,1,0:T(8,128)(2,1)S(1)}, bf16[1,80,1024]{2,1,0:T(8,128)(2,1)S(1)}, u32[]{:S(2)}, u32[]{:S(2)}) %collective-permute-start.25) | collective-permute-done | bytes 163872 | tf_op jit(solution)/shard_map/ppermute | solution.py:75
  (76 shorter events, 17.9 us)
Async XLA Ops:
  2.5 26.6 %collective-permute-start.3 = (bf16[256,1024]{1,0:T(8,128)(2,1)}, bf16[256,1024]{1,0:T(8,128)(2,1)S(1)}, u32[]{:S(2)}, u32[]{:S(2)}) collective-permute-start(bf16[256,1024]{1,0:T(8,128)(2,1)} %join.1.after.refs_0_), channel_id=1, source_target_pairs={{4,0},{8,4},{12,8},{14,12},{10,14},{6,10},{2,6},{0,2},{5,1},{9,5},... | collective-permute-start | bytes 1572872 | tf_op jit(solution)/shard_map/ppermute | solution.py:80
  5.4 23.7 %collective-permute-start.2 = (bf16[256,1024]{1,0:T(8,128)(2,1)}, bf16[256,1024]{1,0:T(8,128)(2,1)S(1)}, u32[]{:S(2)}, u32[]{:S(2)}) collective-permute-start(bf16[256,1024]{1,0:T(8,128)(2,1)} %join.1.after.refs_0_), channel_id=1, source_target_pairs={{0,4},{4,8},{8,12},{12,14},{14,10},{10,6},{6,2},{2,0},{1,5},{5,9},... | collective-permute-start | bytes 1572872 | tf_op jit(solution)/shard_map/ppermute | solution.py:80
  8.9 11.9 %collective-permute-start = (bf16[10,32,128]{2,1,0:T(8,128)(2,1)}, bf16[10,32,128]{2,1,0:T(8,128)(2,1)S(1)}, u32[]{:S(2)}, u32[]{:S(2)}) collective-permute-start(bf16[10,32,128]{2,1,0:T(8,128)(2,1)} %get-tuple-element.39), channel_id=1, source_target_pairs={{0,2},{2,0},{4,6},{6,4},{8,10},{10,8},{12,14},{14,12},{1,3},{3,1},... | collective-permute-start | bytes 245768 | tf_op jit(solution)/shard_map/ppermute | solution.py:75
  10.9 10.3 %collective-permute-start.1 = (bf16[10,32,128]{2,1,0:T(8,128)(2,1)}, bf16[10,32,128]{2,1,0:T(8,128)(2,1)S(1)}, u32[]{:S(2)}, u32[]{:S(2)}) collective-permute-start(bf16[10,32,128]{2,1,0:T(8,128)(2,1)} %get-tuple-element.40), channel_id=1, source_target_pairs={{0,4},{2,6},{4,0},{6,2},{8,12},{10,14},{12,8},{14,10},{1,5},{3,7},... | collective-permute-start | bytes 245768 | tf_op jit(solution)/shard_map/ppermute | solution.py:75
  12.5 8.7 %collective-permute-start.5 = (bf16[10,32,128]{2,1,0:T(8,128)(2,1)}, bf16[10,32,128]{2,1,0:T(8,128)(2,1)S(1)}, u32[]{:S(2)}, u32[]{:S(2)}) collective-permute-start(bf16[10,32,128]{2,1,0:T(8,128)(2,1)} %get-tuple-element.43), channel_id=1, source_target_pairs={{0,8},{2,10},{4,12},{6,14},{8,0},{10,2},{12,4},{14,6},{1,9},{3,11}... | collective-permute-start | bytes 245768 | tf_op jit(solution)/shard_map/ppermute | solution.py:75
  29.1 17.1 %collective-permute-start.9 = (bf16[256,1024]{1,0:T(8,128)(2,1)S(1)}, bf16[256,1024]{1,0:T(8,128)(2,1)S(1)}, u32[]{:S(2)}, u32[]{:S(2)}) collective-permute-start(bf16[256,1024]{1,0:T(8,128)(2,1)S(1)} %collective-permute-done.2.refs_1_), channel_id=1, source_target_pairs={{0,4},{4,8},{8,12},{12,14},{14,10},{10,6},{6,2},{2,0},{1,5},{5,9},... | collective-permute-start | bytes 1572872 | tf_op jit(solution)/shard_map/ppermute | solution.py:80
  29.1 17.1 %collective-permute-start.10 = (bf16[256,1024]{1,0:T(8,128)(2,1)S(1)}, bf16[256,1024]{1,0:T(8,128)(2,1)S(1)}, u32[]{:S(2)}, u32[]{:S(2)}) collective-permute-start(bf16[256,1024]{1,0:T(8,128)(2,1)S(1)} %collective-permute-done.3.refs_2_), channel_id=1, source_target_pairs={{4,0},{8,4},{12,8},{14,12},{10,14},{6,10},{2,6},{0,2},{5,1},{9,5},... | collective-permute-start | bytes 1572872 | tf_op jit(solution)/shard_map/ppermute | solution.py:80
  31.1 13.4 %collective-permute-start.8 = (bf16[10,32,128]{2,1,0:T(8,128)(2,1)}, bf16[10,32,128]{2,1,0:T(8,128)(2,1)S(1)}, u32[]{:S(2)}, u32[]{:S(2)}) collective-permute-start(bf16[10,32,128]{2,1,0:T(8,128)(2,1)} %get-tuple-element.48), channel_id=1, source_target_pairs={{0,14},{2,12},{4,10},{6,8},{8,6},{10,4},{12,2},{14,0},{1,15},{3,13... | collective-permute-start | bytes 245768 | tf_op jit(solution)/shard_map/ppermute | solution.py:75
  33.2 13.0 %collective-permute-start.7 = (bf16[10,32,128]{2,1,0:T(8,128)(2,1)}, bf16[10,32,128]{2,1,0:T(8,128)(2,1)S(1)}, u32[]{:S(2)}, u32[]{:S(2)}) collective-permute-start(bf16[10,32,128]{2,1,0:T(8,128)(2,1)} %get-tuple-element.46), channel_id=1, source_target_pairs={{0,12},{2,14},{4,8},{6,10},{8,4},{10,6},{12,0},{14,2},{1,13},{3,15... | collective-permute-start | bytes 245768 | tf_op jit(solution)/shard_map/ppermute | solution.py:75
  34.4 11.9 %collective-permute-start.4 = (bf16[10,32,128]{2,1,0:T(8,128)(2,1)}, bf16[10,32,128]{2,1,0:T(8,128)(2,1)S(1)}, u32[]{:S(2)}, u32[]{:S(2)}) collective-permute-start(bf16[10,32,128]{2,1,0:T(8,128)(2,1)} %get-tuple-element.42), channel_id=1, source_target_pairs={{0,6},{2,4},{4,2},{6,0},{8,14},{10,12},{12,10},{14,8},{1,7},{3,5},... | collective-permute-start | bytes 245768 | tf_op jit(solution)/shard_map/ppermute | solution.py:75
  46.4 11.5 %collective-permute-start.12 = (bf16[7,10,32,128]{3,2,1,0:T(8,128)(2,1)S(1)}, bf16[7,10,32,128]{3,2,1,0:T(8,128)(2,1)S(1)}, u32[]{:S(2)}, u32[]{:S(2)}) collective-permute-start(bf16[7,10,32,128]{3,2,1,0:T(8,128)(2,1)S(1)} %bitcast_dynamic-update-slice_fusion.w0), channel_id=1, source_target_pairs={{0,16},{16,0},{1,17},{17,1},{2,18},{18,2},{3,19},{19,3},{4,20},{20... | collective-permute-start | bytes 1720328 | tf_op jit(solution)/shard_map/ppermute | solution.py:63
  48.0 10.9 %collective-permute-start.14 = (bf16[256,1024]{1,0:T(8,128)(2,1)S(1)}, bf16[256,1024]{1,0:T(8,128)(2,1)S(1)}, u32[]{:S(2)}, u32[]{:S(2)}) collective-permute-start(bf16[256,1024]{1,0:T(8,128)(2,1)S(1)} %collective-permute-done.9.refs_3_), channel_id=1, source_target_pairs={{0,4},{4,8},{8,12},{12,14},{14,10},{10,6},{6,2},{2,0},{1,5},{5,9},... | collective-permute-start | bytes 1572872 | tf_op jit(solution)/shard_map/ppermute | solution.py:80
  50.1 11.3 %collective-permute-start.15 = (bf16[256,1024]{1,0:T(8,128)(2,1)S(1)}, bf16[256,1024]{1,0:T(8,128)(2,1)S(1)}, u32[]{:S(2)}, u32[]{:S(2)}) collective-permute-start(bf16[256,1024]{1,0:T(8,128)(2,1)S(1)} %collective-permute-done.10.refs_4_), channel_id=1, source_target_pairs={{4,0},{8,4},{12,8},{14,12},{10,14},{6,10},{2,6},{0,2},{5,1},{9,5},... | collective-permute-start | bytes 1572872 | tf_op jit(solution)/shard_map/ppermute | solution.py:80
  50.1 11.4 %collective-permute-start.11 = (bf16[7,10,32,128]{3,2,1,0:T(8,128)(2,1)S(1)}, bf16[7,10,32,128]{3,2,1,0:T(8,128)(2,1)S(1)}, u32[]{:S(2)}, u32[]{:S(2)}) collective-permute-start(bf16[7,10,32,128]{3,2,1,0:T(8,128)(2,1)S(1)} %bitcast_dynamic-update-slice_fusion.w0), channel_id=1, source_target_pairs={{0,1},{1,0},{2,3},{3,2},{4,5},{5,4},{6,7},{7,6},{8,9},{9,8},{10,11... | collective-permute-start | bytes 1720328 | tf_op jit(solution)/shard_map/ppermute | solution.py:63
  57.9 11.9 %collective-permute-start.13 = (bf16[7,10,32,128]{3,2,1,0:T(8,128)(2,1)S(1)}, bf16[7,10,32,128]{3,2,1,0:T(8,128)(2,1)S(1)}, u32[]{:S(2)}, u32[]{:S(2)}) collective-permute-start(bf16[7,10,32,128]{3,2,1,0:T(8,128)(2,1)S(1)} %collective-permute-done.12.w2), channel_id=1, source_target_pairs={{0,1},{1,0},{2,3},{3,2},{4,5},{5,4},{6,7},{7,6},{8,9},{9,8},{10,11... | collective-permute-start | bytes 1720328 | tf_op jit(solution)/shard_map/ppermute | solution.py:63
  58.9 8.6 %collective-permute-start.16 = (bf16[128,1024]{1,0:T(8,128)(2,1)S(1)}, bf16[128,1024]{1,0:T(8,128)(2,1)S(1)}, u32[]{:S(2)}, u32[]{:S(2)}) collective-permute-start(bf16[128,1024]{1,0:T(8,128)(2,1)S(1)} %slice.52), channel_id=1, source_target_pairs={{0,4},{4,8},{8,12},{12,14},{14,10},{10,6},{6,2},{2,0},{1,5},{5,9},... | collective-permute-start | bytes 786440 | tf_op jit(solution)/shard_map/ppermute | solution.py:80
  76.3 18.5 %collective-permute-start.18 = (bf16[4,80,1024]{2,1,0:T(8,128)(2,1)S(1)}, bf16[4,80,1024]{2,1,0:T(8,128)(2,1)S(1)}, u32[]{:S(2)}, u32[]{:S(2)}) collective-permute-start(bf16[4,80,1024]{2,1,0:T(8,128)(2,1)S(1)} %get-tuple-element.61), channel_id=1, source_target_pairs={{0,2},{2,0},{4,6},{6,4},{8,10},{10,8},{12,14},{14,12},{1,3},{3,1},... | collective-permute-start | bytes 1966088 | tf_op jit(solution)/shard_map/ppermute | solution.py:75
  78.4 16.0 %collective-permute-start.22 = (bf16[4,48,1024]{2,1,0:T(8,128)(2,1)S(1)}, bf16[4,48,1024]{2,1,0:T(8,128)(2,1)S(1)}, u32[]{:S(2)}, u32[]{:S(2)}) collective-permute-start(bf16[4,48,1024]{2,1,0:T(8,128)(2,1)S(1)} %get-tuple-element.64), channel_id=1, source_target_pairs={{0,4},{2,6},{4,0},{6,2},{8,12},{10,14},{12,8},{14,10},{1,5},{3,7},... | collective-permute-start | bytes 1179656 | tf_op jit(solution)/shard_map/ppermute | solution.py:75
  83.6 10.8 %collective-permute-start.21 = (bf16[2,384,128]{2,1,0:T(8,128)(2,1)S(1)}, bf16[2,384,128]{2,1,0:T(8,128)(2,1)S(1)}, u32[]{:S(2)}, u32[]{:S(2)}) collective-permute-start(bf16[2,384,128]{2,1,0:T(8,128)(2,1)S(1)} %pad_maximum_fusion.2), channel_id=1, source_target_pairs={{0,4},{2,6},{4,0},{6,2},{8,12},{10,14},{12,8},{14,10},{1,5},{3,7},... | collective-permute-start | bytes 589832 | tf_op jit(solution)/shard_map/ppermute | solution.py:75
  94.4 9.9 %collective-permute-start.24 = (bf16[4,384,128]{2,1,0:T(8,128)(2,1)S(1)}, bf16[4,384,128]{2,1,0:T(8,128)(2,1)S(1)}, u32[]{:S(2)}, u32[]{:S(2)}) collective-permute-start(bf16[4,384,128]{2,1,0:T(8,128)(2,1)S(1)} %pad_maximum_fusion.refs_0_), channel_id=1, source_target_pairs={{0,2},{2,0},{4,6},{6,4},{8,10},{10,8},{12,14},{14,12},{1,3},{3,1},... | collective-permute-start | bytes 1179656 | tf_op jit(solution)/shard_map/ppermute | solution.py:75
  95.1 12.4 %collective-permute-start.19 = (bf16[2,80,1024]{2,1,0:T(8,128)(2,1)S(1)}, bf16[2,80,1024]{2,1,0:T(8,128)(2,1)S(1)}, u32[]{:S(2)}, u32[]{:S(2)}) collective-permute-start(bf16[2,80,1024]{2,1,0:T(8,128)(2,1)S(1)} %slice.55.refs_2_), channel_id=1, source_target_pairs={{0,4},{2,6},{4,0},{6,2},{8,12},{10,14},{12,8},{14,10},{1,5},{3,7},... | collective-permute-start | bytes 983048 | tf_op jit(solution)/shard_map/ppermute | solution.py:75
  95.6 11.2 %collective-permute-start.23 = (bf16[2,48,1024]{2,1,0:T(8,128)(2,1)S(1)}, bf16[2,48,1024]{2,1,0:T(8,128)(2,1)S(1)}, u32[]{:S(2)}, u32[]{:S(2)}) collective-permute-start(bf16[2,48,1024]{2,1,0:T(8,128)(2,1)S(1)} %slice.56.refs_3_), channel_id=1, source_target_pairs={{0,8},{2,10},{4,12},{6,14},{8,0},{10,2},{12,4},{14,6},{1,9},{3,11}... | collective-permute-start | bytes 589832 | tf_op jit(solution)/shard_map/ppermute | solution.py:75
  107.5 13.0 %collective-permute-start.27 = (bf16[48,128,128]{2,1,0:T(8,128)(2,1)S(1)}, bf16[48,128,128]{2,1,0:T(8,128)(2,1)S(1)}, u32[]{:S(2)}, u32[]{:S(2)}) collective-permute-start(bf16[48,128,128]{2,1,0:T(8,128)(2,1)S(1)} %grads.1), channel_id=1, source_target_pairs={{0,1},{1,0},{2,3},{3,2},{4,5},{5,4},{6,7},{7,6},{8,9},{9,8},{10,11... | collective-permute-start | bytes 4718600 | tf_op jit(solution)/shard_map/ppermute | solution.py:63
  109.5 10.4 %collective-permute-start.25 = (bf16[1,80,1024]{2,1,0:T(8,128)(2,1)S(1)}, bf16[1,80,1024]{2,1,0:T(8,128)(2,1)S(1)}, u32[]{:S(2)}, u32[]{:S(2)}) collective-permute-start(bf16[1,80,1024]{2,1,0:T(8,128)(2,1)S(1)} %slice.58), channel_id=1, source_target_pairs={{0,8},{2,10},{4,12},{6,14},{8,0},{10,2},{12,4},{14,6},{1,9},{3,11}... | collective-permute-start | bytes 491528 | tf_op jit(solution)/shard_map/ppermute | solution.py:75
  (12 other events, 265.5 us)

commit v5 on v4

--- a/solution.py
+++ b/solution.py
@@ -12,7 +12,8 @@
 CAP = 3
 KINDS = 3
 PER = KINDS * CAP
-EARLY = (4, 5, 1, 2)
+EARLY = (4, 7, 1, 2)
+BEFORE_SECOND = (4, 7, 1, 2)
 BEFORE_THIRD = ()
 MIB = 1024 * 1024
 
@@ -33,6 +34,10 @@
 
 def shape(dims, dtype=BF16):
     return jax.ShapeDtypeStruct(dims, dtype)
+
+
+def far(array):
+    return pltpu.with_memory_space_constraint(array, pltpu.HBM)
 
 
 def near(arrays):
@@ -304,7 +309,7 @@
         compiler_params=params(32),
         name="forward",
         cost_estimate=cost(8),
-    )(own, *(near if split else list)([*quarters, *[block for block, _, _ in pieces]]))
+    )(far(own), *(near if split else list)([*quarters, *[block for block, _, _ in pieces]]))
 
 
 def grads_kernel(layout, grid, gd, ud, dd, gr, ur, dr, field, *refs):
@@ -360,6 +365,12 @@
     )(*dests, *row_ids, field, *arrived, *after)
 
 
+def added(part, slots):
+    other = swap(part, "section")
+    summed = part.astype(F32) + other.astype(F32)
+    return [summed[kind * slots : (kind + 1) * slots] for kind in range(KINDS)]
+
+
 def shards(
     tokens,
     cotangent,
@@ -376,6 +387,7 @@
     count = lax.axis_size("fsdp")
     grid = count == SPREAD and tokens.shape[1] % BLK == 0
     t = tokens.shape[0]
+    slots = gate_blocks.shape[0]
     dests = [target[:, 0] for target in (gate_dest, up_dest, down_dest)]
     row_ids = [gate_rows, up_rows, down_rows]
 
@@ -386,7 +398,7 @@
         steps = [ring_step(both, both, "fsdp")]
         for bits in EARLY:
             slabs[bits] = flip(sends[bits - 1], "fsdp", bits)
-        held = lax.optimization_barrier((*steps[0], *slabs.values()))
+        held = lax.optimization_barrier((*steps[0], *[slabs[bits] for bits in BEFORE_SECOND]))
         steps.append(ring_step(*held[:2], "fsdp"))
         for bits in range(1, SPREAD):
             if bits not in EARLY:
@@ -417,27 +429,30 @@
     if grid:
         send_a, send_b, keep_a, keep_b = partial_input
         got_a = flip(send_a, "fsdp", 1)
-        got_b = flip(send_b, "fsdp", 2)
         two = jnp.concatenate([flat, flip(flat, "fsdp", 4)], axis=0)
-        four = jnp.concatenate([two, flip(two, "fsdp", 2)], axis=0)
-        four, got_b = lax.optimization_barrier((four, got_b))
+        got_b = flip(tie(send_b, two), "fsdp", 2)
+        beside = flip(two, "fsdp", 2)
+        sum_a = keep_a + got_a
+        away_a = tie(sum_a[2:])
+        got_a = flip(away_a, "fsdp", 2)
+        beside, away_a = lax.optimization_barrier((beside, away_a))
+        four = jnp.concatenate([two, beside], axis=0)
         rest = flip(four, "fsdp", 1)
         sum_b = keep_b + got_b
         away_b = tie(sum_b[2:])
         got_b = flip(away_b, "fsdp", 4)
-        sum_a = keep_a + got_a
-        away_a = tie(sum_a[2:])
-        got_a = flip(away_a, "fsdp", 2)
         arrived = [four, rest]
         layout = [(n, row, n + bits) for n in range(2) for row, bits in enumerate((0, 4, 2, 6))]
         part = grads(dests, row_ids, field, arrived, layout, grid, [away_a, away_b])
-        got_a, got_b, part = lax.optimization_barrier((got_a, got_b, part))
+        got_a, part = lax.optimization_barrier((got_a, part))
         sum_a = sum_a[:2] + got_a
         away_a = tie(sum_a[1:])
+        part, got_b, away_a = lax.optimization_barrier((part, got_b, away_a))
         got_a = flip(away_a, "fsdp", 4)
-        part = tie(part, away_a)
         sum_b = sum_b[:2] + got_b
         got_b = flip(sum_b[1:], "fsdp", 1)
+        block_grads = added(part, slots)
+        got_a, got_b, *block_grads = lax.optimization_barrier((got_a, got_b, *block_grads))
         input_grad = jnp.concatenate([sum_a[0] + got_a[0], sum_b[0] + got_b[0]], axis=0)
     else:
         input_grad = lax.psum_scatter(
@@ -446,13 +461,8 @@
         arrived = [flat] + [shift(flat, "fsdp", d) for d in range(1, SPREAD)]
         layout = [(d, 0, d) for d in range(SPREAD)]
         part = grads(dests, row_ids, field, arrived, layout, grid, [])
-    slots = gate_blocks.shape[0]
-    other = swap(part, "section")
-    summed = part.astype(F32) + other.astype(F32)
-    gate_grad, up_grad, down_grad = (
-        summed[kind * slots : (kind + 1) * slots] for kind in range(KINDS)
-    )
-    return input_grad, gate_grad, up_grad, down_grad
+        block_grads = added(part, slots)
+    return input_grad, *block_grads
 
 
 def solution(mesh):

time: 123 us -> 119 us (0.967)
  waiting for transfers between devices: 74.8 us -> 63.8 us
  starting transfers between devices: 29.3 us -> 36.9 us
    ppermute x16, waiting for transfers between devices: 57.8 us -> 48.5 us  [flip(): lax.ppermute(block, axis, [(i, i ^ bit) for i in range(lax.axis_size(axis...]
    ppermute x16, starting transfers between devices: 17.8 us -> 24 us  [flip(): lax.ppermute(block, axis, [(i, i ^ bit) for i in range(lax.axis_size(axis...]
    ppermute x8, waiting for transfers between devices: 9.23 us -> 7.56 us  [ring_step(): return (lax.ppermute(left, axis, onward), lax.ppermute(right, axis, back))]
    ppermute x8, starting transfers between devices: 9.79 us -> 11.2 us  [ring_step(): return (lax.ppermute(left, axis, onward), lax.ppermute(right, axis, back))]
  transfers between devices with their start and end apart: 28 -> 28, of which waited for: 15 -> 15; matrix products, arithmetic and copies ran while one was open for 1% -> 2% of each run, Pallas kernels for 5% -> 5%
where the time goes in v5:
time: 119 us
  waiting for transfers between devices  63.8 us (54%)
  starting transfers between devices  36.9 us (31%)
  Pallas kernels  13.1 us (11%)
  local copies, waits for them, and re-layouts  1.98 us (2%)
  other arithmetic  1.81 us (2%)
    ppermute x16, waiting for transfers between devices, flip(): lax.ppermute(block, axis, [(i, i ^ bit) for i in range(lax.axis_size(axis...  48.5 us
    ppermute x16, starting transfers between devices, flip(): lax.ppermute(block, axis, [(i, i ^ bit) for i in range(lax.axis_size(axis...  24 us
    ppermute x8, starting transfers between devices, ring_step(): return (lax.ppermute(left, axis, onward), lax.ppermute(right, axis, back))  11.2 us
    ppermute x4, waiting for transfers between devices, swap(): return lax.ppermute(block, axis, [(0, 1), (1, 0)])  7.77 us
    ppermute x8, waiting for transfers between devices, ring_step(): return (lax.ppermute(left, axis, onward), lax.ppermute(right, axis, back))  7.56 us
    pallas_call x1, Pallas kernels, forward(): pl.pallas_call(functools.partial(forward_kernel, layout, t, int(split)),...  5.38 us
    pallas_call x1, Pallas kernels, pack(): pl.pallas_call(functools.partial(pack_kernel, grid), out_shape=[shape((PE...  3.38 us
    pallas_call x1, Pallas kernels, grads(): pl.pallas_call(functools.partial(grads_kernel, layout, grid), out_shape=s...  2.44 us
  transfers between devices with their start and end apart: 28, of which 15 were waited for; matrix products, arithmetic and copies ran while one was open for 2% of the time, Pallas kernels for 5%

profile of v5, /device:TPU:0, one launch (start us, length us, event | category | flops | bytes accessed | tf_op | source)
XLA Modules:
  0.0 118.5 jit_solution(11343577551648462875)
XLA Ops:
  0.6 1.9 %join.1.after.refs_0_ = bf16[256,1024]{1,0:T(8,128)(2,1)} custom-call(bf16[128,1024]{1,0:T(8,128)(2,1)} %tokens.1, bf16[128,1024]{1,0:T(8,128)(2,1)} %cotangent.1), custom_call_target="tpu_custom_call" | custom-call | bytes 7000000 | tf_op jit(solution)/shard_map/join/pallas_call | solution.py:96
  2.5 2.9 %collective-permute-start.3 = (bf16[256,1024]{1,0:T(8,128)(2,1)}, bf16[256,1024]{1,0:T(8,128)(2,1)S(1)}, u32[]{:S(2)}, u32[]{:S(2)}) collective-permute-start(bf16[256,1024]{1,0:T(8,128)(2,1)} %join.1.after.refs_0_), channel_id=1, source_target_pairs={{4,0},{8,4},{12,8},{14,12},{10,14},{6,10},{2,6},{0,2},{5,1},{9,5},... | collective-permute-start | bytes 1572872 | tf_op jit(solution)/shard_map/ppermute | solution.py:85
  5.5 3.4 %pack.1 = (bf16[10,128,128]{2,1,0:T(8,128)(2,1)}, bf16[10,32,128]{2,1,0:T(8,128)(2,1)}, bf16[10,32,128]{2,1,0:T(8,128)(2,1)}, bf16[10,32,128]{2,1,0:T(8,128)(2,1...) custom-call(s32[16]{0:T(128)} %bitcast.25, ...), custom_call_target="tpu_custom_call" | custom-call | bytes 10500000 | tf_op jit(solution)/shard_map/pack/pallas_call | solution.py:147
  8.9 2.0 %collective-permute-start = (bf16[10,32,128]{2,1,0:T(8,128)(2,1)}, bf16[10,32,128]{2,1,0:T(8,128)(2,1)S(1)}, u32[]{:S(2)}, u32[]{:S(2)}) collective-permute-start(bf16[10,32,128]{2,1,0:T(8,128)(2,1)} %get-tuple-element.46), channel_id=1, source_target_pairs={{0,2},{2,0},{4,6},{6,4},{8,10},{10,8},{12,14},{14,12},{1,3},{3,1},... | collective-permute-start | bytes 245768 | tf_op jit(solution)/shard_map/ppermute | solution.py:80
  12.5 2.6 %collective-permute-start.5 = (bf16[10,32,128]{2,1,0:T(8,128)(2,1)}, bf16[10,32,128]{2,1,0:T(8,128)(2,1)S(1)}, u32[]{:S(2)}, u32[]{:S(2)}) collective-permute-start(bf16[10,32,128]{2,1,0:T(8,128)(2,1)} %get-tuple-element.50), channel_id=1, source_target_pairs={{0,8},{2,10},{4,12},{6,14},{8,0},{10,2},{12,4},{14,6},{1,9},{3,11}... | collective-permute-start | bytes 245768 | tf_op jit(solution)/shard_map/ppermute | solution.py:80
  15.1 5.7 %collective-permute-done = bf16[10,32,128]{2,1,0:T(8,128)(2,1)S(1)} collective-permute-done((bf16[10,32,128]{2,1,0:T(8,128)(2,1)}, bf16[10,32,128]{2,1,0:T(8,128)(2,1)S(1)}, u32[]{:S(2)}, u32[]{:S(2)}) %collective-permute-start) | collective-permute-done | bytes 81952 | tf_op jit(solution)/shard_map/ppermute | solution.py:80
  20.8 3.6 %collective-permute-start.8 = (bf16[10,32,128]{2,1,0:T(8,128)(2,1)}, bf16[10,32,128]{2,1,0:T(8,128)(2,1)S(1)}, u32[]{:S(2)}, u32[]{:S(2)}) collective-permute-start(bf16[10,32,128]{2,1,0:T(8,128)(2,1)} %get-tuple-element.55), channel_id=1, source_target_pairs={{0,14},{2,12},{4,10},{6,8},{8,6},{10,4},{12,2},{14,0},{1,15},{3,13... | collective-permute-start | bytes 245768 | tf_op jit(solution)/shard_map/ppermute | solution.py:80
  24.4 3.9 %collective-permute-done.8 = bf16[10,32,128]{2,1,0:T(8,128)(2,1)S(1)} collective-permute-done((bf16[10,32,128]{2,1,0:T(8,128)(2,1)}, bf16[10,32,128]{2,1,0:T(8,128)(2,1)S(1)}, u32[]{:S(2)}, u32[]{:S(2)}) %collective-permute-start.8) | collective-permute-done | bytes 81952 | tf_op jit(solution)/shard_map/ppermute | solution.py:80
  30.3 2.3 %collective-permute-start.7 = (bf16[10,32,128]{2,1,0:T(8,128)(2,1)}, bf16[10,32,128]{2,1,0:T(8,128)(2,1)S(1)}, u32[]{:S(2)}, u32[]{:S(2)}) collective-permute-start(bf16[10,32,128]{2,1,0:T(8,128)(2,1)} %get-tuple-element.54), channel_id=1, source_target_pairs={{0,12},{2,14},{4,8},{6,10},{8,4},{10,6},{12,0},{14,2},{1,13},{3,15... | collective-permute-start | bytes 245768 | tf_op jit(solution)/shard_map/ppermute | solution.py:80
  32.6 3.0 %collective-permute-start.4 = (bf16[10,32,128]{2,1,0:T(8,128)(2,1)}, bf16[10,32,128]{2,1,0:T(8,128)(2,1)S(1)}, u32[]{:S(2)}, u32[]{:S(2)}) collective-permute-start(bf16[10,32,128]{2,1,0:T(8,128)(2,1)} %get-tuple-element.49), channel_id=1, source_target_pairs={{0,6},{2,4},{4,2},{6,0},{8,14},{10,12},{12,10},{14,8},{1,7},{3,5},... | collective-permute-start | bytes 245768 | tf_op jit(solution)/shard_map/ppermute | solution.py:80
  35.6 9.9 %collective-permute-done.7 = bf16[10,32,128]{2,1,0:T(8,128)(2,1)S(1)} collective-permute-done((bf16[10,32,128]{2,1,0:T(8,128)(2,1)}, bf16[10,32,128]{2,1,0:T(8,128)(2,1)S(1)}, u32[]{:S(2)}, u32[]{:S(2)}) %collective-permute-start.7) | collective-permute-done | bytes 81952 | tf_op jit(solution)/shard_map/ppermute | solution.py:80
  49.6 2.6 %collective-permute-start.15 = (bf16[256,1024]{1,0:T(8,128)(2,1)S(1)}, bf16[256,1024]{1,0:T(8,128)(2,1)S(1)}, u32[]{:S(2)}, u32[]{:S(2)}) collective-permute-start(bf16[256,1024]{1,0:T(8,128)(2,1)S(1)} %collective-permute-done.10.refs_4_), channel_id=1, source_target_pairs={{4,0},{8,4},{12,8},{14,12},{10,14},{6,10},{2,6},{0,2},{5,1},{9,5},... | collective-permute-start | bytes 1572872 | tf_op jit(solution)/shard_map/ppermute | solution.py:85
  52.2 5.4 %collective-permute-done.12.w2 = bf16[7,10,32,128]{3,2,1,0:T(8,128)(2,1)S(1)} collective-permute-done((bf16[7,10,32,128]{3,2,1,0:T(8,128)(2,1)S(1)}, bf16[7,10,32,128]{3,2,1,0:T(8,128)(2,1)S(1)}, u32[]{:S(2)}, u32[]{:S(2)}) %collective-permute-start.12) | collective-permute-done | bytes 573472 | tf_op jit(solution)/shard_map/ppermute | solution.py:68
  59.5 2.1 %collective-permute-start.17 = (bf16[128,1024]{1,0:T(8,128)(2,1)S(1)}, bf16[128,1024]{1,0:T(8,128)(2,1)S(1)}, u32[]{:S(2)}, u32[]{:S(2)}) collective-permute-start(bf16[128,1024]{1,0:T(8,128)(2,1)S(1)} %slice.53), channel_id=1, source_target_pairs={{4,0},{8,4},{12,8},{14,12},{10,14},{6,10},{2,6},{0,2},{5,1},{9,5},... | collective-permute-start | bytes 786440 | tf_op jit(solution)/shard_map/ppermute | solution.py:85
  61.6 5.4 %collective-permute-done.16.refs_7_ = bf16[128,1024]{1,0:T(8,128)(2,1)S(1)} collective-permute-done((bf16[128,1024]{1,0:T(8,128)(2,1)S(1)}, bf16[128,1024]{1,0:T(8,128)(2,1)S(1)}, u32[]{:S(2)}, u32[]{:S(2)}) %collective-permute-start.16) | collective-permute-done | bytes 262176 | tf_op jit(solution)/shard_map/ppermute | solution.py:85
  67.4 5.4 %forward.1 = (bf16[8,256,1024]{2,1,0:T(8,128)(2,1)S(1)}, bf16[3,128,128]{2,1,0:T(8,128)(2,1)S(1)}, bf16[4,80,1024]{2,1,0:T(8,128)(2,1)S(1)}, bf16[4,48,1024]{2,1...) custom-call(bf16[10,128,128]{2,1,0:T(8,128)(2,1)} %get-tuple-element.45.own, ...), custom_call_target="tpu_custom_call" | custom-call | bytes 28000000 | tf_op jit(solution)/shard_map/forward/pallas_call | solution.py:293
  75.8 4.1 %collective-permute-done.20 = bf16[1,384,128]{2,1,0:T(8,128)(2,1)S(1)} collective-permute-done((bf16[1,384,128]{2,1,0:T(8,128)(2,1)S(1)}, bf16[1,384,128]{2,1,0:T(8,128)(2,1)S(1)}, u32[]{:S(2)}, u32[]{:S(2)}) %collective-permute-start.20) | collective-permute-done | bytes 98336 | tf_op jit(solution)/shard_map/ppermute | solution.py:80
  79.9 1.8 %collective-permute-start.21 = (bf16[2,384,128]{2,1,0:T(8,128)(2,1)S(1)}, bf16[2,384,128]{2,1,0:T(8,128)(2,1)S(1)}, u32[]{:S(2)}, u32[]{:S(2)}) collective-permute-start(bf16[2,384,128]{2,1,0:T(8,128)(2,1)S(1)} %pad_maximum_fusion.2), channel_id=1, source_target_pairs={{0,4},{2,6},{4,0},{6,2},{8,12},{10,14},{12,8},{14,10},{1,5},{3,7},... | collective-permute-start | bytes 589832 | tf_op jit(solution)/shard_map/ppermute | solution.py:80
  82.0 6.3 %collective-permute-done.18 = bf16[4,80,1024]{2,1,0:T(8,128)(2,1)S(1)} collective-permute-done((bf16[4,80,1024]{2,1,0:T(8,128)(2,1)S(1)}, bf16[4,80,1024]{2,1,0:T(8,128)(2,1)S(1)}, u32[]{:S(2)}, u32[]{:S(2)}) %collective-permute-start.18) | collective-permute-done | bytes 655392 | tf_op jit(solution)/shard_map/ppermute | solution.py:80
  91.0 7.4 %collective-permute-done.23 = bf16[4,48,1024]{2,1,0:T(8,128)(2,1)S(1)} collective-permute-done((bf16[4,48,1024]{2,1,0:T(8,128)(2,1)S(1)}, bf16[4,48,1024]{2,1,0:T(8,128)(2,1)S(1)}, u32[]{:S(2)}, u32[]{:S(2)}) %collective-permute-start.23) | collective-permute-done | bytes 393248 | tf_op jit(solution)/shard_map/ppermute | solution.py:80
  99.1 2.4 %grads.1 = bf16[48,128,128]{2,1,0:T(8,128)(2,1)S(1)} custom-call(s32[16]{0:T(128)S(1)} %bitcast.26, s32[16]{0:T(128)S(1)} %bitcast.28, s32[16]{0:T(128)S(1)} %bitcast.30, s32[16]{0:T(128)S(1)} %copy-done.4, s32[16]{0:T(128)S(1)} %copy-done.5, s32[16]{0:T(128)S(1)} %copy-done.6, bf16[8,256,1024]{2,1,0:T(8,128)(2,1)S(1)} %get-tuple-element.69.field, ...), custom_call_target="tpu_custom_call" | custom-call | bytes 26250000 | tf_op jit(solution)/shard_map/grads/pallas_call | solution.py:353
  102.1 5.1 %collective-permute-done.24 = bf16[2,48,1024]{2,1,0:T(8,128)(2,1)S(1)} collective-permute-done((bf16[2,48,1024]{2,1,0:T(8,128)(2,1)S(1)}, bf16[2,48,1024]{2,1,0:T(8,128)(2,1)S(1)}, u32[]{:S(2)}, u32[]{:S(2)}) %collective-permute-start.24) | collective-permute-done | bytes 196640 | tf_op jit(solution)/shard_map/ppermute | solution.py:80
  108.3 2.4 %collective-permute-done.27 = bf16[48,128,128]{2,1,0:T(8,128)(2,1)S(1)} collective-permute-done((bf16[48,128,128]{2,1,0:T(8,128)(2,1)S(1)}, bf16[48,128,128]{2,1,0:T(8,128)(2,1)S(1)}, u32[]{:S(2)}, u32[]{:S(2)}) %collective-permute-start.27) | collective-permute-done | bytes 1572896 | tf_op jit(solution)/shard_map/ppermute | solution.py:68
  113.0 4.8 %collective-permute-done.25 = bf16[1,80,1024]{2,1,0:T(8,128)(2,1)S(1)} collective-permute-done((bf16[1,80,1024]{2,1,0:T(8,128)(2,1)S(1)}, bf16[1,80,1024]{2,1,0:T(8,128)(2,1)S(1)}, u32[]{:S(2)}, u32[]{:S(2)}) %collective-permute-start.25) | collective-permute-done | bytes 163872 | tf_op jit(solution)/shard_map/ppermute | solution.py:80
  (74 shorter events, 21.4 us)
Async XLA Ops:
  2.5 25.7 %collective-permute-start.3 = (bf16[256,1024]{1,0:T(8,128)(2,1)}, bf16[256,1024]{1,0:T(8,128)(2,1)S(1)}, u32[]{:S(2)}, u32[]{:S(2)}) collective-permute-start(bf16[256,1024]{1,0:T(8,128)(2,1)} %join.1.after.refs_0_), channel_id=1, source_target_pairs={{4,0},{8,4},{12,8},{14,12},{10,14},{6,10},{2,6},{0,2},{5,1},{9,5},... | collective-permute-start | bytes 1572872 | tf_op jit(solution)/shard_map/ppermute | solution.py:85
  5.4 22.8 %collective-permute-start.2 = (bf16[256,1024]{1,0:T(8,128)(2,1)}, bf16[256,1024]{1,0:T(8,128)(2,1)S(1)}, u32[]{:S(2)}, u32[]{:S(2)}) collective-permute-start(bf16[256,1024]{1,0:T(8,128)(2,1)} %join.1.after.refs_0_), channel_id=1, source_target_pairs={{0,4},{4,8},{8,12},{12,14},{14,10},{10,6},{6,2},{2,0},{1,5},{5,9},... | collective-permute-start | bytes 1572872 | tf_op jit(solution)/shard_map/ppermute | solution.py:85
  8.9 11.9 %collective-permute-start = (bf16[10,32,128]{2,1,0:T(8,128)(2,1)}, bf16[10,32,128]{2,1,0:T(8,128)(2,1)S(1)}, u32[]{:S(2)}, u32[]{:S(2)}) collective-permute-start(bf16[10,32,128]{2,1,0:T(8,128)(2,1)} %get-tuple-element.46), channel_id=1, source_target_pairs={{0,2},{2,0},{4,6},{6,4},{8,10},{10,8},{12,14},{14,12},{1,3},{3,1},... | collective-permute-start | bytes 245768 | tf_op jit(solution)/shard_map/ppermute | solution.py:80
  10.9 13.4 %collective-permute-start.1 = (bf16[10,32,128]{2,1,0:T(8,128)(2,1)}, bf16[10,32,128]{2,1,0:T(8,128)(2,1)S(1)}, u32[]{:S(2)}, u32[]{:S(2)}) collective-permute-start(bf16[10,32,128]{2,1,0:T(8,128)(2,1)} %get-tuple-element.47), channel_id=1, source_target_pairs={{0,4},{2,6},{4,0},{6,2},{8,12},{10,14},{12,8},{14,10},{1,5},{3,7},... | collective-permute-start | bytes 245768 | tf_op jit(solution)/shard_map/ppermute | solution.py:80
  12.5 11.9 %collective-permute-start.5 = (bf16[10,32,128]{2,1,0:T(8,128)(2,1)}, bf16[10,32,128]{2,1,0:T(8,128)(2,1)S(1)}, u32[]{:S(2)}, u32[]{:S(2)}) collective-permute-start(bf16[10,32,128]{2,1,0:T(8,128)(2,1)} %get-tuple-element.50), channel_id=1, source_target_pairs={{0,8},{2,10},{4,12},{6,14},{8,0},{10,2},{12,4},{14,6},{1,9},{3,11}... | collective-permute-start | bytes 245768 | tf_op jit(solution)/shard_map/ppermute | solution.py:80
  28.2 18.1 %collective-permute-start.9 = (bf16[256,1024]{1,0:T(8,128)(2,1)S(1)}, bf16[256,1024]{1,0:T(8,128)(2,1)S(1)}, u32[]{:S(2)}, u32[]{:S(2)}) collective-permute-start(bf16[256,1024]{1,0:T(8,128)(2,1)S(1)} %collective-permute-done.2.refs_1_), channel_id=1, source_target_pairs={{0,4},{4,8},{8,12},{12,14},{14,10},{10,6},{6,2},{2,0},{1,5},{5,9},... | collective-permute-start | bytes 1572872 | tf_op jit(solution)/shard_map/ppermute | solution.py:85
  28.9 17.4 %collective-permute-start.10 = (bf16[256,1024]{1,0:T(8,128)(2,1)S(1)}, bf16[256,1024]{1,0:T(8,128)(2,1)S(1)}, u32[]{:S(2)}, u32[]{:S(2)}) collective-permute-start(bf16[256,1024]{1,0:T(8,128)(2,1)S(1)} %collective-permute-done.3.refs_2_), channel_id=1, source_target_pairs={{4,0},{8,4},{12,8},{14,12},{10,14},{6,10},{2,6},{0,2},{5,1},{9,5},... | collective-permute-start | bytes 1572872 | tf_op jit(solution)/shard_map/ppermute | solution.py:85
  30.3 15.2 %collective-permute-start.7 = (bf16[10,32,128]{2,1,0:T(8,128)(2,1)}, bf16[10,32,128]{2,1,0:T(8,128)(2,1)S(1)}, u32[]{:S(2)}, u32[]{:S(2)}) collective-permute-start(bf16[10,32,128]{2,1,0:T(8,128)(2,1)} %get-tuple-element.54), channel_id=1, source_target_pairs={{0,12},{2,14},{4,8},{6,10},{8,4},{10,6},{12,0},{14,2},{1,13},{3,15... | collective-permute-start | bytes 245768 | tf_op jit(solution)/shard_map/ppermute | solution.py:80
  32.6 13.8 %collective-permute-start.6 = (bf16[10,32,128]{2,1,0:T(8,128)(2,1)}, bf16[10,32,128]{2,1,0:T(8,128)(2,1)S(1)}, u32[]{:S(2)}, u32[]{:S(2)}) collective-permute-start(bf16[10,32,128]{2,1,0:T(8,128)(2,1)} %get-tuple-element.52), channel_id=1, source_target_pairs={{0,10},{2,8},{4,14},{6,12},{8,2},{10,0},{12,6},{14,4},{1,11},{3,9}... | collective-permute-start | bytes 245768 | tf_op jit(solution)/shard_map/ppermute | solution.py:80
  32.6 13.8 %collective-permute-start.4 = (bf16[10,32,128]{2,1,0:T(8,128)(2,1)}, bf16[10,32,128]{2,1,0:T(8,128)(2,1)S(1)}, u32[]{:S(2)}, u32[]{:S(2)}) collective-permute-start(bf16[10,32,128]{2,1,0:T(8,128)(2,1)} %get-tuple-element.49), channel_id=1, source_target_pairs={{0,6},{2,4},{4,2},{6,0},{8,14},{10,12},{12,10},{14,8},{1,7},{3,5},... | collective-permute-start | bytes 245768 | tf_op jit(solution)/shard_map/ppermute | solution.py:80
  46.5 11.1 %collective-permute-start.12 = (bf16[7,10,32,128]{3,2,1,0:T(8,128)(2,1)S(1)}, bf16[7,10,32,128]{3,2,1,0:T(8,128)(2,1)S(1)}, u32[]{:S(2)}, u32[]{:S(2)}) collective-permute-start(bf16[7,10,32,128]{3,2,1,0:T(8,128)(2,1)S(1)} %bitcast_dynamic-update-slice_fusion.w0), channel_id=1, source_target_pairs={{0,16},{16,0},{1,17},{17,1},{2,18},{18,2},{3,19},{19,3},{4,20},{20... | collective-permute-start | bytes 1720328 | tf_op jit(solution)/shard_map/ppermute | solution.py:68
  48.2 11.2 %collective-permute-start.14 = (bf16[256,1024]{1,0:T(8,128)(2,1)S(1)}, bf16[256,1024]{1,0:T(8,128)(2,1)S(1)}, u32[]{:S(2)}, u32[]{:S(2)}) collective-permute-start(bf16[256,1024]{1,0:T(8,128)(2,1)S(1)} %collective-permute-done.9.refs_3_), channel_id=1, source_target_pairs={{0,4},{4,8},{8,12},{12,14},{14,10},{10,6},{6,2},{2,0},{1,5},{5,9},... | collective-permute-start | bytes 1572872 | tf_op jit(solution)/shard_map/ppermute | solution.py:85
  49.6 9.9 %collective-permute-start.15 = (bf16[256,1024]{1,0:T(8,128)(2,1)S(1)}, bf16[256,1024]{1,0:T(8,128)(2,1)S(1)}, u32[]{:S(2)}, u32[]{:S(2)}) collective-permute-start(bf16[256,1024]{1,0:T(8,128)(2,1)S(1)} %collective-permute-done.10.refs_4_), channel_id=1, source_target_pairs={{4,0},{8,4},{12,8},{14,12},{10,14},{6,10},{2,6},{0,2},{5,1},{9,5},... | collective-permute-start | bytes 1572872 | tf_op jit(solution)/shard_map/ppermute | solution.py:85
  52.2 9.4 %collective-permute-start.11 = (bf16[7,10,32,128]{3,2,1,0:T(8,128)(2,1)S(1)}, bf16[7,10,32,128]{3,2,1,0:T(8,128)(2,1)S(1)}, u32[]{:S(2)}, u32[]{:S(2)}) collective-permute-start(bf16[7,10,32,128]{3,2,1,0:T(8,128)(2,1)S(1)} %bitcast_dynamic-update-slice_fusion.w0), channel_id=1, source_target_pairs={{0,1},{1,0},{2,3},{3,2},{4,5},{5,4},{6,7},{7,6},{8,9},{9,8},{10,11... | collective-permute-start | bytes 1720328 | tf_op jit(solution)/shard_map/ppermute | solution.py:68
  57.6 9.8 %collective-permute-start.13 = (bf16[7,10,32,128]{3,2,1,0:T(8,128)(2,1)S(1)}, bf16[7,10,32,128]{3,2,1,0:T(8,128)(2,1)S(1)}, u32[]{:S(2)}, u32[]{:S(2)}) collective-permute-start(bf16[7,10,32,128]{3,2,1,0:T(8,128)(2,1)S(1)} %collective-permute-done.12.w2), channel_id=1, source_target_pairs={{0,1},{1,0},{2,3},{3,2},{4,5},{5,4},{6,7},{7,6},{8,9},{9,8},{10,11... | collective-permute-start | bytes 1720328 | tf_op jit(solution)/shard_map/ppermute | solution.py:68
  59.4 7.6 %collective-permute-start.16 = (bf16[128,1024]{1,0:T(8,128)(2,1)S(1)}, bf16[128,1024]{1,0:T(8,128)(2,1)S(1)}, u32[]{:S(2)}, u32[]{:S(2)}) collective-permute-start(bf16[128,1024]{1,0:T(8,128)(2,1)S(1)} %slice.52), channel_id=1, source_target_pairs={{0,4},{4,8},{8,12},{12,14},{14,10},{10,6},{6,2},{2,0},{1,5},{5,9},... | collective-permute-start | bytes 786440 | tf_op jit(solution)/shard_map/ppermute | solution.py:85
  59.5 7.9 %collective-permute-start.17 = (bf16[128,1024]{1,0:T(8,128)(2,1)S(1)}, bf16[128,1024]{1,0:T(8,128)(2,1)S(1)}, u32[]{:S(2)}, u32[]{:S(2)}) collective-permute-start(bf16[128,1024]{1,0:T(8,128)(2,1)S(1)} %slice.53), channel_id=1, source_target_pairs={{4,0},{8,4},{12,8},{14,12},{10,14},{6,10},{2,6},{0,2},{5,1},{9,5},... | collective-permute-start | bytes 786440 | tf_op jit(solution)/shard_map/ppermute | solution.py:85
  72.8 15.4 %collective-permute-start.18 = (bf16[4,80,1024]{2,1,0:T(8,128)(2,1)S(1)}, bf16[4,80,1024]{2,1,0:T(8,128)(2,1)S(1)}, u32[]{:S(2)}, u32[]{:S(2)}) collective-permute-start(bf16[4,80,1024]{2,1,0:T(8,128)(2,1)S(1)} %get-tuple-element.68), channel_id=1, source_target_pairs={{0,2},{2,0},{4,6},{6,4},{8,10},{10,8},{12,14},{14,12},{1,3},{3,1},... | collective-permute-start | bytes 1966088 | tf_op jit(solution)/shard_map/ppermute | solution.py:80
  79.9 8.6 %collective-permute-start.21 = (bf16[2,384,128]{2,1,0:T(8,128)(2,1)S(1)}, bf16[2,384,128]{2,1,0:T(8,128)(2,1)S(1)}, u32[]{:S(2)}, u32[]{:S(2)}) collective-permute-start(bf16[2,384,128]{2,1,0:T(8,128)(2,1)S(1)} %pad_maximum_fusion.2), channel_id=1, source_target_pairs={{0,4},{2,6},{4,0},{6,2},{8,12},{10,14},{12,8},{14,10},{1,5},{3,7},... | collective-permute-start | bytes 589832 | tf_op jit(solution)/shard_map/ppermute | solution.py:80
  81.7 16.7 %collective-permute-start.23 = (bf16[4,48,1024]{2,1,0:T(8,128)(2,1)S(1)}, bf16[4,48,1024]{2,1,0:T(8,128)(2,1)S(1)}, u32[]{:S(2)}, u32[]{:S(2)}) collective-permute-start(bf16[4,48,1024]{2,1,0:T(8,128)(2,1)S(1)} %get-tuple-element.75), channel_id=1, source_target_pairs={{0,4},{2,6},{4,0},{6,2},{8,12},{10,14},{12,8},{14,10},{1,5},{3,7},... | collective-permute-start | bytes 1179656 | tf_op jit(solution)/shard_map/ppermute | solution.py:80
  88.6 10.4 %collective-permute-start.22 = (bf16[4,384,128]{2,1,0:T(8,128)(2,1)S(1)}, bf16[4,384,128]{2,1,0:T(8,128)(2,1)S(1)}, u32[]{:S(2)}, u32[]{:S(2)}) collective-permute-start(bf16[4,384,128]{2,1,0:T(8,128)(2,1)S(1)} %pad_maximum_fusion.refs_0_), channel_id=1, source_target_pairs={{0,2},{2,0},{4,6},{6,4},{8,10},{10,8},{12,14},{14,12},{1,3},{3,1},... | collective-permute-start | bytes 1179656 | tf_op jit(solution)/shard_map/ppermute | solution.py:80
  89.5 12.5 %collective-permute-start.19 = (bf16[2,80,1024]{2,1,0:T(8,128)(2,1)S(1)}, bf16[2,80,1024]{2,1,0:T(8,128)(2,1)S(1)}, u32[]{:S(2)}, u32[]{:S(2)}) collective-permute-start(bf16[2,80,1024]{2,1,0:T(8,128)(2,1)S(1)} %slice.55.refs_2_), channel_id=1, source_target_pairs={{0,4},{2,6},{4,0},{6,2},{8,12},{10,14},{12,8},{14,10},{1,5},{3,7},... | collective-permute-start | bytes 983048 | tf_op jit(solution)/shard_map/ppermute | solution.py:80
  98.5 8.7 %collective-permute-start.24 = (bf16[2,48,1024]{2,1,0:T(8,128)(2,1)S(1)}, bf16[2,48,1024]{2,1,0:T(8,128)(2,1)S(1)}, u32[]{:S(2)}, u32[]{:S(2)}) collective-permute-start(bf16[2,48,1024]{2,1,0:T(8,128)(2,1)S(1)} %slice.56.refs_3_), channel_id=1, source_target_pairs={{0,8},{2,10},{4,12},{6,14},{8,0},{10,2},{12,4},{14,6},{1,9},{3,11}... | collective-permute-start | bytes 589832 | tf_op jit(solution)/shard_map/ppermute | solution.py:80
  108.3 9.5 %collective-permute-start.25 = (bf16[1,80,1024]{2,1,0:T(8,128)(2,1)S(1)}, bf16[1,80,1024]{2,1,0:T(8,128)(2,1)S(1)}, u32[]{:S(2)}, u32[]{:S(2)}) collective-permute-start(bf16[1,80,1024]{2,1,0:T(8,128)(2,1)S(1)} %slice.58), channel_id=1, source_target_pairs={{0,8},{2,10},{4,12},{6,14},{8,0},{10,2},{12,4},{14,6},{1,9},{3,11}... | collective-permute-start | bytes 491528 | tf_op jit(solution)/shard_map/ppermute | solution.py:80
  (11 other events, 244.4 us)

commit v6 on v5

--- a/solution.py
+++ b/solution.py
@@ -12,6 +12,8 @@
 CAP = 3
 KINDS = 3
 PER = KINDS * CAP
+PART = BLK // 4
+IDS = 16
 EARLY = (4, 7, 1, 2)
 BEFORE_SECOND = (4, 7, 1, 2)
 BEFORE_THIRD = ()
@@ -73,7 +75,7 @@
 
 
 def first_part(t):
-    return t * 5 // 8 // 16 * 16
+    return t * 11 // 16 // 8 * 8
 
 
 def flip(block, axis, bit):
@@ -131,27 +133,29 @@
 
             @pl.when(offset == 0)
             def _():
-                own[slot] = blocks[j]
+                for part in range(4):
+                    rows_of = pl.ds(pl.multiple_of(slot * PART, PART), PART)
+                    own[part, rows_of, :] = blocks[j, part * PART : (part + 1) * PART, :]
 
             return carry
 
         lax.fori_loop(0, blocks.shape[0], place, 0)
     for offset in range(1, SPREAD):
-        sends[offset - 1][0:PER] = slab[offset]
-        sends[offset - 1][PER] = ids[offset].astype(BF16)
-    own[PER, 0:rows] = ids[0].astype(BF16)
+        sends[offset - 1][0 : PER * PART] = slab[offset].reshape(PER * PART, BLK)
+        sends[offset - 1][PER * PART :] = ids[offset].astype(BF16)
+    own[0, PER * PART :] = ids[0].astype(BF16)
 
 
 def pack(grid, dests, row_ids, blocks, after):
     rows = BLK // 4
     return pl.pallas_call(
         functools.partial(pack_kernel, grid),
-        out_shape=[shape((PER + 1, BLK, BLK))] + [shape((PER + 1, rows, BLK))] * (SPREAD - 1),
+        out_shape=[shape((4, PER * PART + IDS, BLK))] + [shape((PER * PART + IDS, BLK))] * (SPREAD - 1),
         in_specs=[SMEM] * 6 + [VMEM] * 3 + [ANY],
         out_specs=[VMEM] * SPREAD,
         scratch_shapes=[
             pltpu.VMEM((SPREAD, PER, rows, BLK), BF16),
-            pltpu.VMEM((SPREAD, rows, BLK), F32),
+            pltpu.VMEM((SPREAD, IDS, BLK), F32),
             pltpu.SMEM((SPREAD,), jnp.int32),
         ],
         compiler_params=params(56),
@@ -182,18 +186,15 @@
     )
 
     own_copies = [
-        pltpu.make_async_copy(own.at[0:PER], weights.at[0], sems.at[0]),
-        pltpu.make_async_copy(own.at[PER, 0 : BLK // 4], id_rows.at[0], sems.at[1]),
-        pltpu.make_async_copy(w0.at[:, PER], id_rows.at[1:SPREAD], sems.at[2]),
+        pltpu.make_async_copy(own.at[:, 0 : PER * PART], weights.at[0], sems.at[0]),
+        pltpu.make_async_copy(own.at[0, PER * PART :], id_rows.at[0], sems.at[1]),
+        pltpu.make_async_copy(w0.at[:, PER * PART :], id_rows.at[1:SPREAD], sems.at[2]),
     ]
     weight_copies = []
     for n, ref in enumerate((w0, w1, w2, w3)):
-        begin = pl.multiple_of(quarters[n] * (BLK // 4), BLK // 4)
         weight_copies.append(
             pltpu.make_async_copy(
-                ref.at[:, 0:PER],
-                weights.at[1:SPREAD, :, pl.ds(begin, BLK // 4), :],
-                sems.at[3 + n],
+                ref.at[:, 0 : PER * PART], weights.at[1:SPREAD, quarters[n]], sems.at[3 + n]
             )
         )
     shard_copies = []
@@ -209,7 +210,7 @@
     total[...] = jnp.zeros_like(total)
     for copy in own_copies[1:]:
         copy.wait()
-    id_ints[...] = id_rows[:, 0:16, :].astype(F32).astype(jnp.int32)
+    id_ints[...] = id_rows[...].astype(F32).astype(jnp.int32)
     id_copy = pltpu.make_async_copy(id_ints, id_scalars, sems.at[7])
     id_copy.start()
     for copy in shard_copies:
@@ -235,15 +236,18 @@
     for copy in weight_copies:
         copy.wait()
 
-    def block_group(kind):
-        return weights[:, kind * CAP : (kind + 1) * CAP].reshape(SPREAD * CAP * BLK, BLK)
-
-    gate = jnp.dot(left[0], block_group(0), preferred_element_type=F32)
-    upper = jnp.dot(left[1], block_group(1), preferred_element_type=F32)
+    def block(offset, slot):
+        rows = slice(slot * PART, (slot + 1) * PART)
+        return jnp.concatenate([weights[offset, part, rows] for part in range(4)], axis=0)
+
+    def block_group(kind, offsets=range(SPREAD)):
+        slots = range(kind * CAP, (kind + 1) * CAP)
+        return [block(offset, slot) for offset in offsets for slot in slots]
+
+    gate = jnp.dot(left[0], jnp.concatenate(block_group(0), axis=0), preferred_element_type=F32)
+    upper = jnp.dot(left[1], jnp.concatenate(block_group(1), axis=0), preferred_element_type=F32)
     nt = (((1,), (1,)), ((), ()))
-    across = jnp.concatenate(
-        [weights[n // CAP, 2 * CAP + n % CAP] for n in range(SPREAD * CAP)], axis=1
-    )
+    across = jnp.concatenate(block_group(2), axis=1)
     hidden_grad = lax.dot_general(left[2], across, nt, preferred_element_type=F32)
     sigma = 1.0 / (1.0 + jnp.exp(-gate))
     hidden = (gate * sigma * upper).astype(BF16)
@@ -256,7 +260,7 @@
         for offset in range(SPREAD):
             terms = lax.dot_general(
                 grad,
-                weights[offset, kind * CAP : (kind + 1) * CAP].reshape(CAP * BLK, BLK),
+                jnp.concatenate(block_group(kind, [offset]), axis=0),
                 nt,
                 preferred_element_type=F32,
             )
@@ -297,10 +301,10 @@
         out_specs=[ANY] + [VMEM] * (1 + len(outs)),
         scratch_shapes=[
             pltpu.VMEM(field, BF16),
-            pltpu.VMEM((SPREAD, PER, BLK, BLK), BF16),
-            pltpu.VMEM((SPREAD, BLK // 4, BLK), BF16),
-            pltpu.VMEM((SPREAD, 16, BLK), jnp.int32),
-            pltpu.SMEM((SPREAD, 16, BLK), jnp.int32),
+            pltpu.VMEM((SPREAD, 4, PER * PART, BLK), BF16),
+            pltpu.VMEM((SPREAD, IDS, BLK), BF16),
+            pltpu.VMEM((SPREAD, IDS, BLK), jnp.int32),
+            pltpu.SMEM((SPREAD, IDS, BLK), jnp.int32),
             pltpu.VMEM((KINDS, t, SPREAD * CAP * BLK), BF16),
             pltpu.VMEM((piece_count, t, width), F32),
             pltpu.SemaphoreType.DMA((len(pieces),)),
@@ -435,7 +439,7 @@
         sum_a = keep_a + got_a
         away_a = tie(sum_a[2:])
         got_a = flip(away_a, "fsdp", 2)
-        beside, away_a = lax.optimization_barrier((beside, away_a))
+        beside, away_a, got_b = lax.optimization_barrier((beside, away_a, got_b))
         four = jnp.concatenate([two, beside], axis=0)
         rest = flip(four, "fsdp", 1)
         sum_b = keep_b + got_b

time: 119 us -> 118 us (level)
  waiting for transfers between devices: 63.8 us -> 60 us
  starting transfers between devices: 36.9 us -> 38.8 us
    ppermute x16, waiting for transfers between devices: 48.5 us -> 46 us  [flip(): lax.ppermute(block, axis, [(i, i ^ bit) for i in range(lax.axis_size(axis...]
    ppermute x16, starting transfers between devices: 24 us -> 25.7 us  [flip(): lax.ppermute(block, axis, [(i, i ^ bit) for i in range(lax.axis_size(axis...]
    ppermute x4, waiting for transfers between devices: 7.77 us -> 6.25 us  [swap(): return lax.ppermute(block, axis, [(0, 1), (1, 0)])]
  transfers between devices with their start and end apart: 28 -> 28, of which waited for: 15 -> 14; matrix products, arithmetic and copies ran while one was open for 2% -> 2% of each run, Pallas kernels for 5% -> 5%
where the time goes in v6:
time: 118 us; the launch traced here: 117 us
  waiting for transfers between devices  60 us (51%)
  starting transfers between devices  38.8 us (33%)
  Pallas kernels  13.1 us (11%)
  local copies, waits for them, and re-layouts  1.98 us (2%)
  other arithmetic  1.79 us (2%)
    ppermute x16, waiting for transfers between devices, flip(): lax.ppermute(block, axis, [(i, i ^ bit) for i in range(lax.axis_size(axis...  46 us
    ppermute x16, starting transfers between devices, flip(): lax.ppermute(block, axis, [(i, i ^ bit) for i in range(lax.axis_size(axis...  25.7 us
    ppermute x8, starting transfers between devices, ring_step(): return (lax.ppermute(left, axis, onward), lax.ppermute(right, axis, back))  11.3 us
    ppermute x8, waiting for transfers between devices, ring_step(): return (lax.ppermute(left, axis, onward), lax.ppermute(right, axis, back))  7.69 us
    ppermute x4, waiting for transfers between devices, swap(): return lax.ppermute(block, axis, [(0, 1), (1, 0)])  6.25 us
    pallas_call x1, Pallas kernels, forward(): pl.pallas_call(functools.partial(forward_kernel, layout, t, int(split)),...  5.45 us
    pallas_call x1, Pallas kernels, pack(): pl.pallas_call(functools.partial(pack_kernel, grid), out_shape=[shape((4,...  3.37 us
    pallas_call x1, Pallas kernels, grads(): pl.pallas_call(functools.partial(grads_kernel, layout, grid), out_shape=s...  2.43 us
  transfers between devices with their start and end apart: 28, of which 14 were waited for; matrix products, arithmetic and copies ran while one was open for 2% of the time, Pallas kernels for 5%

profile of v6, /device:TPU:0, one launch (start us, length us, event | category | flops | bytes accessed | tf_op | source)
XLA Modules:
  0.0 116.6 jit_solution(2762558248014133075)
XLA Ops:
  2.5 2.9 %collective-permute-start.3 = (bf16[256,1024]{1,0:T(8,128)(2,1)}, bf16[256,1024]{1,0:T(8,128)(2,1)S(1)}, u32[]{:S(2)}, u32[]{:S(2)}) collective-permute-start(bf16[256,1024]{1,0:T(8,128)(2,1)} %join.1.after.refs_0_), channel_id=1, source_target_pairs={{4,0},{8,4},{12,8},{14,12},{10,14},{6,10},{2,6},{0,2},{5,1},{9,5},... | collective-permute-start | bytes 1572872 | tf_op jit(solution)/shard_map/ppermute | solution.py:87
  5.5 3.4 %pack.1 = (bf16[4,304,128]{2,1,0:T(8,128)(2,1)}, bf16[304,128]{1,0:T(8,128)(2,1)}, bf16[304,128]{1,0:T(8,128)(2,1)}, bf16[304,128]{1,0:T(8,128)(2,1)}, bf16[304,...) custom-call(s32[16]{0:T(128)} %bitcast.25, s32[16]{0:T(128)} %bitcast.27, ...), custom_call_target="tpu_custom_call" | custom-call | bytes 10500000 | tf_op jit(solution)/shard_map/pack/pallas_call | solution.py:151
  12.5 2.6 %collective-permute-start.5 = (bf16[304,128]{1,0:T(8,128)(2,1)}, bf16[304,128]{1,0:T(8,128)(2,1)S(1)}, u32[]{:S(2)}, u32[]{:S(2)}) collective-permute-start(bf16[304,128]{1,0:T(8,128)(2,1)} %get-tuple-element.51), channel_id=1, source_target_pairs={{0,8},{2,10},{4,12},{6,14},{8,0},{10,2},{12,4},{14,6},{1,9},{3,11}... | collective-permute-start | bytes 233480 | tf_op jit(solution)/shard_map/ppermute | solution.py:82
  15.1 5.6 %collective-permute-done = bf16[304,128]{1,0:T(8,128)(2,1)S(1)} collective-permute-done((bf16[304,128]{1,0:T(8,128)(2,1)}, bf16[304,128]{1,0:T(8,128)(2,1)S(1)}, u32[]{:S(2)}, u32[]{:S(2)}) %collective-permute-start) | collective-permute-done | bytes 77856 | tf_op jit(solution)/shard_map/ppermute | solution.py:82
  20.7 3.6 %collective-permute-start.8 = (bf16[304,128]{1,0:T(8,128)(2,1)}, bf16[304,128]{1,0:T(8,128)(2,1)S(1)}, u32[]{:S(2)}, u32[]{:S(2)}) collective-permute-start(bf16[304,128]{1,0:T(8,128)(2,1)} %get-tuple-element.56), channel_id=1, source_target_pairs={{0,14},{2,12},{4,10},{6,8},{8,6},{10,4},{12,2},{14,0},{1,15},{3,13... | collective-permute-start | bytes 233480 | tf_op jit(solution)/shard_map/ppermute | solution.py:82
  24.3 3.8 %collective-permute-done.8 = bf16[304,128]{1,0:T(8,128)(2,1)S(1)} collective-permute-done((bf16[304,128]{1,0:T(8,128)(2,1)}, bf16[304,128]{1,0:T(8,128)(2,1)S(1)}, u32[]{:S(2)}, u32[]{:S(2)}) %collective-permute-start.8) | collective-permute-done | bytes 77856 | tf_op jit(solution)/shard_map/ppermute | solution.py:82
  28.1 2.0 %collective-permute-start.10 = (bf16[256,1024]{1,0:T(8,128)(2,1)S(1)}, bf16[256,1024]{1,0:T(8,128)(2,1)S(1)}, u32[]{:S(2)}, u32[]{:S(2)}) collective-permute-start(bf16[256,1024]{1,0:T(8,128)(2,1)S(1)} %collective-permute-done.3.refs_2_), channel_id=1, source_target_pairs={{4,0},{8,4},{12,8},{14,12},{10,14},{6,10},{2,6},{0,2},{5,1},{9,5},... | collective-permute-start | bytes 1572872 | tf_op jit(solution)/shard_map/ppermute | solution.py:87
  30.1 2.3 %collective-permute-start.7 = (bf16[304,128]{1,0:T(8,128)(2,1)}, bf16[304,128]{1,0:T(8,128)(2,1)S(1)}, u32[]{:S(2)}, u32[]{:S(2)}) collective-permute-start(bf16[304,128]{1,0:T(8,128)(2,1)} %get-tuple-element.55), channel_id=1, source_target_pairs={{0,12},{2,14},{4,8},{6,10},{8,4},{10,6},{12,0},{14,2},{1,13},{3,15... | collective-permute-start | bytes 233480 | tf_op jit(solution)/shard_map/ppermute | solution.py:82
  32.4 3.0 %collective-permute-start.4 = (bf16[304,128]{1,0:T(8,128)(2,1)}, bf16[304,128]{1,0:T(8,128)(2,1)S(1)}, u32[]{:S(2)}, u32[]{:S(2)}) collective-permute-start(bf16[304,128]{1,0:T(8,128)(2,1)} %get-tuple-element.50), channel_id=1, source_target_pairs={{0,6},{2,4},{4,2},{6,0},{8,14},{10,12},{12,10},{14,8},{1,7},{3,5},... | collective-permute-start | bytes 233480 | tf_op jit(solution)/shard_map/ppermute | solution.py:82
  35.4 9.8 %collective-permute-done.7 = bf16[304,128]{1,0:T(8,128)(2,1)S(1)} collective-permute-done((bf16[304,128]{1,0:T(8,128)(2,1)}, bf16[304,128]{1,0:T(8,128)(2,1)S(1)}, u32[]{:S(2)}, u32[]{:S(2)}) %collective-permute-start.7) | collective-permute-done | bytes 77856 | tf_op jit(solution)/shard_map/ppermute | solution.py:82
  49.0 2.6 %collective-permute-start.15 = (bf16[256,1024]{1,0:T(8,128)(2,1)S(1)}, bf16[256,1024]{1,0:T(8,128)(2,1)S(1)}, u32[]{:S(2)}, u32[]{:S(2)}) collective-permute-start(bf16[256,1024]{1,0:T(8,128)(2,1)S(1)} %collective-permute-done.10.refs_4_), channel_id=1, source_target_pairs={{4,0},{8,4},{12,8},{14,12},{10,14},{6,10},{2,6},{0,2},{5,1},{9,5},... | collective-permute-start | bytes 1572872 | tf_op jit(solution)/shard_map/ppermute | solution.py:87
  51.6 4.7 %collective-permute-done.12.w2 = bf16[7,304,128]{2,1,0:T(8,128)(2,1)S(1)} collective-permute-done((bf16[7,304,128]{2,1,0:T(8,128)(2,1)S(1)}, bf16[7,304,128]{2,1,0:T(8,128)(2,1)S(1)}, u32[]{:S(2)}, u32[]{:S(2)}) %collective-permute-start.12) | collective-permute-done | bytes 544800 | tf_op jit(solution)/shard_map/ppermute | solution.py:70
  56.3 2.5 %collective-permute-done.14.refs_5_ = bf16[256,1024]{1,0:T(8,128)(2,1)S(1)} collective-permute-done((bf16[256,1024]{1,0:T(8,128)(2,1)S(1)}, bf16[256,1024]{1,0:T(8,128)(2,1)S(1)}, u32[]{:S(2)}, u32[]{:S(2)}) %collective-permute-start.14) | collective-permute-done | bytes 524320 | tf_op jit(solution)/shard_map/ppermute | solution.py:87
  58.9 2.1 %collective-permute-start.17 = (bf16[128,1024]{1,0:T(8,128)(2,1)S(1)}, bf16[128,1024]{1,0:T(8,128)(2,1)S(1)}, u32[]{:S(2)}, u32[]{:S(2)}) collective-permute-start(bf16[128,1024]{1,0:T(8,128)(2,1)S(1)} %slice.53), channel_id=1, source_target_pairs={{4,0},{8,4},{12,8},{14,12},{10,14},{6,10},{2,6},{0,2},{5,1},{9,5},... | collective-permute-start | bytes 786440 | tf_op jit(solution)/shard_map/ppermute | solution.py:87
  61.0 5.1 %collective-permute-done.16.refs_7_ = bf16[128,1024]{1,0:T(8,128)(2,1)S(1)} collective-permute-done((bf16[128,1024]{1,0:T(8,128)(2,1)S(1)}, bf16[128,1024]{1,0:T(8,128)(2,1)S(1)}, u32[]{:S(2)}, u32[]{:S(2)}) %collective-permute-start.16) | collective-permute-done | bytes 262176 | tf_op jit(solution)/shard_map/ppermute | solution.py:87
  66.2 5.4 %forward.1 = (bf16[8,256,1024]{2,1,0:T(8,128)(2,1)S(1)}, bf16[3,128,128]{2,1,0:T(8,128)(2,1)S(1)}, bf16[4,88,1024]{2,1,0:T(8,128)(2,1)S(1)}, bf16[4,40,1024]{2,1...) custom-call(bf16[4,304,128]{2,1,0:T(8,128)(2,1)} %get-tuple-element.46.own, ...), custom_call_target="tpu_custom_call" | custom-call | bytes 28000000 | tf_op jit(solution)/shard_map/forward/pallas_call | solution.py:297
  74.9 4.1 %collective-permute-done.20 = bf16[1,384,128]{2,1,0:T(8,128)(2,1)S(1)} collective-permute-done((bf16[1,384,128]{2,1,0:T(8,128)(2,1)S(1)}, bf16[1,384,128]{2,1,0:T(8,128)(2,1)S(1)}, u32[]{:S(2)}, u32[]{:S(2)}) %collective-permute-start.20) | collective-permute-done | bytes 98336 | tf_op jit(solution)/shard_map/ppermute | solution.py:82
  79.0 2.1 %collective-permute-start.22 = (bf16[4,40,1024]{2,1,0:T(8,128)(2,1)S(1)}, bf16[4,40,1024]{2,1,0:T(8,128)(2,1)S(1)}, u32[]{:S(2)}, u32[]{:S(2)}) collective-permute-start(bf16[4,40,1024]{2,1,0:T(8,128)(2,1)S(1)} %get-tuple-element.73), channel_id=1, source_target_pairs={{0,4},{2,6},{4,0},{6,2},{8,12},{10,14},{12,8},{14,10},{1,5},{3,7},... | collective-permute-start | bytes 983048 | tf_op jit(solution)/shard_map/ppermute | solution.py:82
  81.3 6.7 %collective-permute-done.18 = bf16[4,88,1024]{2,1,0:T(8,128)(2,1)S(1)} collective-permute-done((bf16[4,88,1024]{2,1,0:T(8,128)(2,1)S(1)}, bf16[4,88,1024]{2,1,0:T(8,128)(2,1)S(1)}, u32[]{:S(2)}, u32[]{:S(2)}) %collective-permute-start.18) | collective-permute-done | bytes 720928 | tf_op jit(solution)/shard_map/ppermute | solution.py:82
  88.2 4.6 %collective-permute-done.21 = bf16[2,384,128]{2,1,0:T(8,128)(2,1)S(1)} collective-permute-done((bf16[2,384,128]{2,1,0:T(8,128)(2,1)S(1)}, bf16[2,384,128]{2,1,0:T(8,128)(2,1)S(1)}, u32[]{:S(2)}, u32[]{:S(2)}) %collective-permute-start.21) | collective-permute-done | bytes 196640 | tf_op jit(solution)/shard_map/ppermute | solution.py:82
  93.2 3.3 %collective-permute-start.24 = (bf16[2,40,1024]{2,1,0:T(8,128)(2,1)S(1)}, bf16[2,40,1024]{2,1,0:T(8,128)(2,1)S(1)}, u32[]{:S(2)}, u32[]{:S(2)}) collective-permute-start(bf16[2,40,1024]{2,1,0:T(8,128)(2,1)S(1)} %slice.56.refs_3_), channel_id=1, source_target_pairs={{0,8},{2,10},{4,12},{6,14},{8,0},{10,2},{12,4},{14,6},{1,9},{3,11}... | collective-permute-start | bytes 491528 | tf_op jit(solution)/shard_map/ppermute | solution.py:82
  96.5 4.2 %collective-permute-done.23.refs_1_ = bf16[4,384,128]{2,1,0:T(8,128)(2,1)S(1)} collective-permute-done((bf16[4,384,128]{2,1,0:T(8,128)(2,1)S(1)}, bf16[4,384,128]{2,1,0:T(8,128)(2,1)S(1)}, u32[]{:S(2)}, u32[]{:S(2)}) %collective-permute-start.23) | collective-permute-done | bytes 393248 | tf_op jit(solution)/shard_map/ppermute | solution.py:82
  100.7 2.4 %grads.1 = bf16[48,128,128]{2,1,0:T(8,128)(2,1)S(1)} custom-call(s32[16]{0:T(128)S(1)} %bitcast.26, s32[16]{0:T(128)S(1)} %bitcast.28, s32[16]{0:T(128)S(1)} %bitcast.30, s32[16]{0:T(128)S(1)} %copy-done.4, s32[16]{0:T(128)S(1)} %copy-done.5, s32[16]{0:T(128)S(1)} %copy-done.6, bf16[8,256,1024]{2,1,0:T(8,128)(2,1)S(1)} %get-tuple-element.70.field, ...), custom_call_target="tpu_custom_call" | custom-call | bytes 26250000 | tf_op jit(solution)/shard_map/grads/pallas_call | solution.py:357
  109.1 6.8 %collective-permute-done.25 = bf16[1,88,1024]{2,1,0:T(8,128)(2,1)S(1)} collective-permute-done((bf16[1,88,1024]{2,1,0:T(8,128)(2,1)S(1)}, bf16[1,88,1024]{2,1,0:T(8,128)(2,1)S(1)}, u32[]{:S(2)}, u32[]{:S(2)}) %collective-permute-start.25) | collective-permute-done | bytes 180256 | tf_op jit(solution)/shard_map/ppermute | solution.py:82
  (74 shorter events, 20.1 us)
Async XLA Ops:
  2.5 25.6 %collective-permute-start.3 = (bf16[256,1024]{1,0:T(8,128)(2,1)}, bf16[256,1024]{1,0:T(8,128)(2,1)S(1)}, u32[]{:S(2)}, u32[]{:S(2)}) collective-permute-start(bf16[256,1024]{1,0:T(8,128)(2,1)} %join.1.after.refs_0_), channel_id=1, source_target_pairs={{4,0},{8,4},{12,8},{14,12},{10,14},{6,10},{2,6},{0,2},{5,1},{9,5},... | collective-permute-start | bytes 1572872 | tf_op jit(solution)/shard_map/ppermute | solution.py:87
  5.4 22.7 %collective-permute-start.2 = (bf16[256,1024]{1,0:T(8,128)(2,1)}, bf16[256,1024]{1,0:T(8,128)(2,1)S(1)}, u32[]{:S(2)}, u32[]{:S(2)}) collective-permute-start(bf16[256,1024]{1,0:T(8,128)(2,1)} %join.1.after.refs_0_), channel_id=1, source_target_pairs={{0,4},{4,8},{8,12},{12,14},{14,10},{10,6},{6,2},{2,0},{1,5},{5,9},... | collective-permute-start | bytes 1572872 | tf_op jit(solution)/shard_map/ppermute | solution.py:87
  8.9 11.8 %collective-permute-start = (bf16[304,128]{1,0:T(8,128)(2,1)}, bf16[304,128]{1,0:T(8,128)(2,1)S(1)}, u32[]{:S(2)}, u32[]{:S(2)}) collective-permute-start(bf16[304,128]{1,0:T(8,128)(2,1)} %get-tuple-element.47), channel_id=1, source_target_pairs={{0,2},{2,0},{4,6},{6,4},{8,10},{10,8},{12,14},{14,12},{1,3},{3,1},... | collective-permute-start | bytes 233480 | tf_op jit(solution)/shard_map/ppermute | solution.py:82
  10.9 13.4 %collective-permute-start.1 = (bf16[304,128]{1,0:T(8,128)(2,1)}, bf16[304,128]{1,0:T(8,128)(2,1)S(1)}, u32[]{:S(2)}, u32[]{:S(2)}) collective-permute-start(bf16[304,128]{1,0:T(8,128)(2,1)} %get-tuple-element.48), channel_id=1, source_target_pairs={{0,4},{2,6},{4,0},{6,2},{8,12},{10,14},{12,8},{14,10},{1,5},{3,7},... | collective-permute-start | bytes 233480 | tf_op jit(solution)/shard_map/ppermute | solution.py:82
  12.5 11.8 %collective-permute-start.5 = (bf16[304,128]{1,0:T(8,128)(2,1)}, bf16[304,128]{1,0:T(8,128)(2,1)S(1)}, u32[]{:S(2)}, u32[]{:S(2)}) collective-permute-start(bf16[304,128]{1,0:T(8,128)(2,1)} %get-tuple-element.51), channel_id=1, source_target_pairs={{0,8},{2,10},{4,12},{6,14},{8,0},{10,2},{12,4},{14,6},{1,9},{3,11}... | collective-permute-start | bytes 233480 | tf_op jit(solution)/shard_map/ppermute | solution.py:82
  20.7 7.4 %collective-permute-start.8 = (bf16[304,128]{1,0:T(8,128)(2,1)}, bf16[304,128]{1,0:T(8,128)(2,1)S(1)}, u32[]{:S(2)}, u32[]{:S(2)}) collective-permute-start(bf16[304,128]{1,0:T(8,128)(2,1)} %get-tuple-element.56), channel_id=1, source_target_pairs={{0,14},{2,12},{4,10},{6,8},{8,6},{10,4},{12,2},{14,0},{1,15},{3,13... | collective-permute-start | bytes 233480 | tf_op jit(solution)/shard_map/ppermute | solution.py:82
  28.1 17.5 %collective-permute-start.9 = (bf16[256,1024]{1,0:T(8,128)(2,1)S(1)}, bf16[256,1024]{1,0:T(8,128)(2,1)S(1)}, u32[]{:S(2)}, u32[]{:S(2)}) collective-permute-start(bf16[256,1024]{1,0:T(8,128)(2,1)S(1)} %collective-permute-done.2.refs_1_), channel_id=1, source_target_pairs={{0,4},{4,8},{8,12},{12,14},{14,10},{10,6},{6,2},{2,0},{1,5},{5,9},... | collective-permute-start | bytes 1572872 | tf_op jit(solution)/shard_map/ppermute | solution.py:87
  28.1 17.5 %collective-permute-start.10 = (bf16[256,1024]{1,0:T(8,128)(2,1)S(1)}, bf16[256,1024]{1,0:T(8,128)(2,1)S(1)}, u32[]{:S(2)}, u32[]{:S(2)}) collective-permute-start(bf16[256,1024]{1,0:T(8,128)(2,1)S(1)} %collective-permute-done.3.refs_2_), channel_id=1, source_target_pairs={{4,0},{8,4},{12,8},{14,12},{10,14},{6,10},{2,6},{0,2},{5,1},{9,5},... | collective-permute-start | bytes 1572872 | tf_op jit(solution)/shard_map/ppermute | solution.py:87
  30.1 15.1 %collective-permute-start.7 = (bf16[304,128]{1,0:T(8,128)(2,1)}, bf16[304,128]{1,0:T(8,128)(2,1)S(1)}, u32[]{:S(2)}, u32[]{:S(2)}) collective-permute-start(bf16[304,128]{1,0:T(8,128)(2,1)} %get-tuple-element.55), channel_id=1, source_target_pairs={{0,12},{2,14},{4,8},{6,10},{8,4},{10,6},{12,0},{14,2},{1,13},{3,15... | collective-permute-start | bytes 233480 | tf_op jit(solution)/shard_map/ppermute | solution.py:82
  32.4 13.2 %collective-permute-start.6 = (bf16[304,128]{1,0:T(8,128)(2,1)}, bf16[304,128]{1,0:T(8,128)(2,1)S(1)}, u32[]{:S(2)}, u32[]{:S(2)}) collective-permute-start(bf16[304,128]{1,0:T(8,128)(2,1)} %get-tuple-element.53), channel_id=1, source_target_pairs={{0,10},{2,8},{4,14},{6,12},{8,2},{10,0},{12,6},{14,4},{1,11},{3,9}... | collective-permute-start | bytes 233480 | tf_op jit(solution)/shard_map/ppermute | solution.py:82
  32.4 13.2 %collective-permute-start.4 = (bf16[304,128]{1,0:T(8,128)(2,1)}, bf16[304,128]{1,0:T(8,128)(2,1)S(1)}, u32[]{:S(2)}, u32[]{:S(2)}) collective-permute-start(bf16[304,128]{1,0:T(8,128)(2,1)} %get-tuple-element.50), channel_id=1, source_target_pairs={{0,6},{2,4},{4,2},{6,0},{8,14},{10,12},{12,10},{14,8},{1,7},{3,5},... | collective-permute-start | bytes 233480 | tf_op jit(solution)/shard_map/ppermute | solution.py:82
  45.8 10.5 %collective-permute-start.12 = (bf16[7,304,128]{2,1,0:T(8,128)(2,1)S(1)}, bf16[7,304,128]{2,1,0:T(8,128)(2,1)S(1)}, u32[]{:S(2)}, u32[]{:S(2)}) collective-permute-start(bf16[7,304,128]{2,1,0:T(8,128)(2,1)S(1)} %bitcast_dynamic-update-slice_fusion.w0), channel_id=1, source_target_pairs={{0,16},{16,0},{1,17},{17,1},{2,18},{18,2},{3,19},{19,3},{4,20},{20... | collective-permute-start | bytes 1634312 | tf_op jit(solution)/shard_map/ppermute | solution.py:70
  47.5 11.3 %collective-permute-start.14 = (bf16[256,1024]{1,0:T(8,128)(2,1)S(1)}, bf16[256,1024]{1,0:T(8,128)(2,1)S(1)}, u32[]{:S(2)}, u32[]{:S(2)}) collective-permute-start(bf16[256,1024]{1,0:T(8,128)(2,1)S(1)} %collective-permute-done.9.refs_3_), channel_id=1, source_target_pairs={{0,4},{4,8},{8,12},{12,14},{14,10},{10,6},{6,2},{2,0},{1,5},{5,9},... | collective-permute-start | bytes 1572872 | tf_op jit(solution)/shard_map/ppermute | solution.py:87
  49.0 9.8 %collective-permute-start.15 = (bf16[256,1024]{1,0:T(8,128)(2,1)S(1)}, bf16[256,1024]{1,0:T(8,128)(2,1)S(1)}, u32[]{:S(2)}, u32[]{:S(2)}) collective-permute-start(bf16[256,1024]{1,0:T(8,128)(2,1)S(1)} %collective-permute-done.10.refs_4_), channel_id=1, source_target_pairs={{4,0},{8,4},{12,8},{14,12},{10,14},{6,10},{2,6},{0,2},{5,1},{9,5},... | collective-permute-start | bytes 1572872 | tf_op jit(solution)/shard_map/ppermute | solution.py:87
  51.6 9.4 %collective-permute-start.11 = (bf16[7,304,128]{2,1,0:T(8,128)(2,1)S(1)}, bf16[7,304,128]{2,1,0:T(8,128)(2,1)S(1)}, u32[]{:S(2)}, u32[]{:S(2)}) collective-permute-start(bf16[7,304,128]{2,1,0:T(8,128)(2,1)S(1)} %bitcast_dynamic-update-slice_fusion.w0), channel_id=1, source_target_pairs={{0,1},{1,0},{2,3},{3,2},{4,5},{5,4},{6,7},{7,6},{8,9},{9,8},{10,11... | collective-permute-start | bytes 1634312 | tf_op jit(solution)/shard_map/ppermute | solution.py:70
  56.3 9.9 %collective-permute-start.13 = (bf16[7,304,128]{2,1,0:T(8,128)(2,1)S(1)}, bf16[7,304,128]{2,1,0:T(8,128)(2,1)S(1)}, u32[]{:S(2)}, u32[]{:S(2)}) collective-permute-start(bf16[7,304,128]{2,1,0:T(8,128)(2,1)S(1)} %collective-permute-done.12.w2), channel_id=1, source_target_pairs={{0,1},{1,0},{2,3},{3,2},{4,5},{5,4},{6,7},{7,6},{8,9},{9,8},{10,11... | collective-permute-start | bytes 1634312 | tf_op jit(solution)/shard_map/ppermute | solution.py:70
  58.9 7.3 %collective-permute-start.17 = (bf16[128,1024]{1,0:T(8,128)(2,1)S(1)}, bf16[128,1024]{1,0:T(8,128)(2,1)S(1)}, u32[]{:S(2)}, u32[]{:S(2)}) collective-permute-start(bf16[128,1024]{1,0:T(8,128)(2,1)S(1)} %slice.53), channel_id=1, source_target_pairs={{4,0},{8,4},{12,8},{14,12},{10,14},{6,10},{2,6},{0,2},{5,1},{9,5},... | collective-permute-start | bytes 786440 | tf_op jit(solution)/shard_map/ppermute | solution.py:87
  71.7 16.2 %collective-permute-start.18 = (bf16[4,88,1024]{2,1,0:T(8,128)(2,1)S(1)}, bf16[4,88,1024]{2,1,0:T(8,128)(2,1)S(1)}, u32[]{:S(2)}, u32[]{:S(2)}) collective-permute-start(bf16[4,88,1024]{2,1,0:T(8,128)(2,1)S(1)} %get-tuple-element.69), channel_id=1, source_target_pairs={{0,2},{2,0},{4,6},{6,4},{8,10},{10,8},{12,14},{14,12},{1,3},{3,1},... | collective-permute-start | bytes 2162696 | tf_op jit(solution)/shard_map/ppermute | solution.py:82
  79.0 13.8 %collective-permute-start.22 = (bf16[4,40,1024]{2,1,0:T(8,128)(2,1)S(1)}, bf16[4,40,1024]{2,1,0:T(8,128)(2,1)S(1)}, u32[]{:S(2)}, u32[]{:S(2)}) collective-permute-start(bf16[4,40,1024]{2,1,0:T(8,128)(2,1)S(1)} %get-tuple-element.73), channel_id=1, source_target_pairs={{0,4},{2,6},{4,0},{6,2},{8,12},{10,14},{12,8},{14,10},{1,5},{3,7},... | collective-permute-start | bytes 983048 | tf_op jit(solution)/shard_map/ppermute | solution.py:82
  81.2 11.6 %collective-permute-start.21 = (bf16[2,384,128]{2,1,0:T(8,128)(2,1)S(1)}, bf16[2,384,128]{2,1,0:T(8,128)(2,1)S(1)}, u32[]{:S(2)}, u32[]{:S(2)}) collective-permute-start(bf16[2,384,128]{2,1,0:T(8,128)(2,1)S(1)} %pad_maximum_fusion.2), channel_id=1, source_target_pairs={{0,4},{2,6},{4,0},{6,2},{8,12},{10,14},{12,8},{14,10},{1,5},{3,7},... | collective-permute-start | bytes 589832 | tf_op jit(solution)/shard_map/ppermute | solution.py:82
  92.9 7.8 %collective-permute-start.23 = (bf16[4,384,128]{2,1,0:T(8,128)(2,1)S(1)}, bf16[4,384,128]{2,1,0:T(8,128)(2,1)S(1)}, u32[]{:S(2)}, u32[]{:S(2)}) collective-permute-start(bf16[4,384,128]{2,1,0:T(8,128)(2,1)S(1)} %pad_maximum_fusion.refs_0_), channel_id=1, source_target_pairs={{0,2},{2,0},{4,6},{6,4},{8,10},{10,8},{12,14},{14,12},{1,3},{3,1},... | collective-permute-start | bytes 1179656 | tf_op jit(solution)/shard_map/ppermute | solution.py:82
  92.9 10.2 %collective-permute-start.19 = (bf16[2,88,1024]{2,1,0:T(8,128)(2,1)S(1)}, bf16[2,88,1024]{2,1,0:T(8,128)(2,1)S(1)}, u32[]{:S(2)}, u32[]{:S(2)}) collective-permute-start(bf16[2,88,1024]{2,1,0:T(8,128)(2,1)S(1)} %slice.55.refs_2_), channel_id=1, source_target_pairs={{0,4},{2,6},{4,0},{6,2},{8,12},{10,14},{12,8},{14,10},{1,5},{3,7},... | collective-permute-start | bytes 1081352 | tf_op jit(solution)/shard_map/ppermute | solution.py:82
  93.2 10.1 %collective-permute-start.24 = (bf16[2,40,1024]{2,1,0:T(8,128)(2,1)S(1)}, bf16[2,40,1024]{2,1,0:T(8,128)(2,1)S(1)}, u32[]{:S(2)}, u32[]{:S(2)}) collective-permute-start(bf16[2,40,1024]{2,1,0:T(8,128)(2,1)S(1)} %slice.56.refs_3_), channel_id=1, source_target_pairs={{0,8},{2,10},{4,12},{6,14},{8,0},{10,2},{12,4},{14,6},{1,9},{3,11}... | collective-permute-start | bytes 491528 | tf_op jit(solution)/shard_map/ppermute | solution.py:82
  104.4 11.4 %collective-permute-start.25 = (bf16[1,88,1024]{2,1,0:T(8,128)(2,1)S(1)}, bf16[1,88,1024]{2,1,0:T(8,128)(2,1)S(1)}, u32[]{:S(2)}, u32[]{:S(2)}) collective-permute-start(bf16[1,88,1024]{2,1,0:T(8,128)(2,1)S(1)} %slice.58), channel_id=1, source_target_pairs={{0,8},{2,10},{4,12},{6,14},{8,0},{10,2},{12,4},{14,6},{1,9},{3,11}... | collective-permute-start | bytes 540680 | tf_op jit(solution)/shard_map/ppermute | solution.py:82
  (11 other events, 259.9 us)

commit v7 on v6

--- a/solution.py
+++ b/solution.py
@@ -170,7 +170,7 @@
     refs = refs[count:]
     field_out, hidden_out = refs[0], refs[1]
     outs = refs[2 : 3 + 3 * split]
-    field, weights, id_rows, id_ints, id_scalars, left, total, shard_sems, sems = refs[3 + 3 * split :]
+    field, weights, id_rows, id_ints, id_scalars, total, shard_sems, sems = refs[3 + 3 * split :]
     width = field.shape[2]
     per_piece = width // BLK
     t = tokens_here
@@ -223,15 +223,15 @@
         row = id_scalars[offset, kind * CAP + rank, 0]
         return row // per_piece, pl.multiple_of((row % per_piece) * BLK, BLK)
 
-    for kind in range(KINDS):
+    def left(kind):
         first = t if kind == 2 else 0
+        parts = []
         for offset in range(SPREAD):
             for rank in range(CAP):
                 piece, column = where(offset, kind, rank)
-                n = offset * CAP + rank
-                left[kind, :, n * BLK : (n + 1) * BLK] = field[
-                    piece, first : first + t, pl.ds(column, BLK)
-                ]
+                parts.append(field[piece, first : first + t, pl.ds(column, BLK)])
+        return jnp.concatenate(parts, axis=1)
+
     own_copies[0].wait()
     for copy in weight_copies:
         copy.wait()
@@ -244,11 +244,11 @@
         slots = range(kind * CAP, (kind + 1) * CAP)
         return [block(offset, slot) for offset in offsets for slot in slots]
 
-    gate = jnp.dot(left[0], jnp.concatenate(block_group(0), axis=0), preferred_element_type=F32)
-    upper = jnp.dot(left[1], jnp.concatenate(block_group(1), axis=0), preferred_element_type=F32)
+    gate = jnp.dot(left(0), jnp.concatenate(block_group(0), axis=0), preferred_element_type=F32)
+    upper = jnp.dot(left(1), jnp.concatenate(block_group(1), axis=0), preferred_element_type=F32)
     nt = (((1,), (1,)), ((), ()))
     across = jnp.concatenate(block_group(2), axis=1)
-    hidden_grad = lax.dot_general(left[2], across, nt, preferred_element_type=F32)
+    hidden_grad = lax.dot_general(left(2), across, nt, preferred_element_type=F32)
     sigma = 1.0 / (1.0 + jnp.exp(-gate))
     hidden = (gate * sigma * upper).astype(BF16)
     gate_d = (hidden_grad * upper * sigma * (1.0 + gate * (1.0 - sigma))).astype(BF16)
@@ -305,7 +305,6 @@
             pltpu.VMEM((SPREAD, IDS, BLK), BF16),
             pltpu.VMEM((SPREAD, IDS, BLK), jnp.int32),
             pltpu.SMEM((SPREAD, IDS, BLK), jnp.int32),
-            pltpu.VMEM((KINDS, t, SPREAD * CAP * BLK), BF16),
             pltpu.VMEM((piece_count, t, width), F32),
             pltpu.SemaphoreType.DMA((len(pieces),)),
             pltpu.SemaphoreType.DMA((9,)),

time: 118 us -> 118 us (level)
  no operation moved by 1% of the time
where the time goes in v7:
time: 118 us; the launch traced here: 116 us
  waiting for transfers between devices  59.9 us (51%)
  starting transfers between devices  38.8 us (33%)
  Pallas kernels  12.5 us (11%)
  local copies, waits for them, and re-layouts  1.98 us (2%)
  other arithmetic  1.79 us (2%)
    ppermute x16, waiting for transfers between devices, flip(): lax.ppermute(block, axis, [(i, i ^ bit) for i in range(lax.axis_size(axis...  46 us
    ppermute x16, starting transfers between devices, flip(): lax.ppermute(block, axis, [(i, i ^ bit) for i in range(lax.axis_size(axis...  25.7 us
    ppermute x8, starting transfers between devices, ring_step(): return (lax.ppermute(left, axis, onward), lax.ppermute(right, axis, back))  11.3 us
    ppermute x8, waiting for transfers between devices, ring_step(): return (lax.ppermute(left, axis, onward), lax.ppermute(right, axis, back))  7.69 us
    ppermute x4, waiting for transfers between devices, swap(): return lax.ppermute(block, axis, [(0, 1), (1, 0)])  6.22 us
    pallas_call x1, Pallas kernels, forward(): pl.pallas_call(functools.partial(forward_kernel, layout, t, int(split)),...  4.88 us
    pallas_call x1, Pallas kernels, pack(): pl.pallas_call(functools.partial(pack_kernel, grid), out_shape=[shape((4,...  3.37 us
    pallas_call x1, Pallas kernels, grads(): pl.pallas_call(functools.partial(grads_kernel, layout, grid), out_shape=s...  2.44 us
  transfers between devices with their start and end apart: 28, of which 14 were waited for; matrix products, arithmetic and copies ran while one was open for 2% of the time, Pallas kernels for 5%

profile of v7, /device:TPU:0, one launch (start us, length us, event | category | flops | bytes accessed | tf_op | source)
XLA Modules:
  0.0 116.0 jit_solution(5925026540014345763)
XLA Ops:
  2.5 2.9 %collective-permute-start.3 = (bf16[256,1024]{1,0:T(8,128)(2,1)}, bf16[256,1024]{1,0:T(8,128)(2,1)S(1)}, u32[]{:S(2)}, u32[]{:S(2)}) collective-permute-start(bf16[256,1024]{1,0:T(8,128)(2,1)} %join.1.after.refs_0_), channel_id=1, source_target_pairs={{4,0},{8,4},{12,8},{14,12},{10,14},{6,10},{2,6},{0,2},{5,1},{9,5},... | collective-permute-start | bytes 1572872 | tf_op jit(solution)/shard_map/ppermute | solution.py:87
  5.5 3.4 %pack.1 = (bf16[4,304,128]{2,1,0:T(8,128)(2,1)}, bf16[304,128]{1,0:T(8,128)(2,1)}, bf16[304,128]{1,0:T(8,128)(2,1)}, bf16[304,128]{1,0:T(8,128)(2,1)}, bf16[304,...) custom-call(s32[16]{0:T(128)} %bitcast.25, s32[16]{0:T(128)} %bitcast.27, ...), custom_call_target="tpu_custom_call" | custom-call | bytes 10500000 | tf_op jit(solution)/shard_map/pack/pallas_call | solution.py:151
  12.5 2.6 %collective-permute-start.5 = (bf16[304,128]{1,0:T(8,128)(2,1)}, bf16[304,128]{1,0:T(8,128)(2,1)S(1)}, u32[]{:S(2)}, u32[]{:S(2)}) collective-permute-start(bf16[304,128]{1,0:T(8,128)(2,1)} %get-tuple-element.51), channel_id=1, source_target_pairs={{0,8},{2,10},{4,12},{6,14},{8,0},{10,2},{12,4},{14,6},{1,9},{3,11}... | collective-permute-start | bytes 233480 | tf_op jit(solution)/shard_map/ppermute | solution.py:82
  15.1 5.6 %collective-permute-done = bf16[304,128]{1,0:T(8,128)(2,1)S(1)} collective-permute-done((bf16[304,128]{1,0:T(8,128)(2,1)}, bf16[304,128]{1,0:T(8,128)(2,1)S(1)}, u32[]{:S(2)}, u32[]{:S(2)}) %collective-permute-start) | collective-permute-done | bytes 77856 | tf_op jit(solution)/shard_map/ppermute | solution.py:82
  20.7 3.6 %collective-permute-start.8 = (bf16[304,128]{1,0:T(8,128)(2,1)}, bf16[304,128]{1,0:T(8,128)(2,1)S(1)}, u32[]{:S(2)}, u32[]{:S(2)}) collective-permute-start(bf16[304,128]{1,0:T(8,128)(2,1)} %get-tuple-element.56), channel_id=1, source_target_pairs={{0,14},{2,12},{4,10},{6,8},{8,6},{10,4},{12,2},{14,0},{1,15},{3,13... | collective-permute-start | bytes 233480 | tf_op jit(solution)/shard_map/ppermute | solution.py:82
  24.3 3.8 %collective-permute-done.8 = bf16[304,128]{1,0:T(8,128)(2,1)S(1)} collective-permute-done((bf16[304,128]{1,0:T(8,128)(2,1)}, bf16[304,128]{1,0:T(8,128)(2,1)S(1)}, u32[]{:S(2)}, u32[]{:S(2)}) %collective-permute-start.8) | collective-permute-done | bytes 77856 | tf_op jit(solution)/shard_map/ppermute | solution.py:82
  28.1 2.0 %collective-permute-start.10 = (bf16[256,1024]{1,0:T(8,128)(2,1)S(1)}, bf16[256,1024]{1,0:T(8,128)(2,1)S(1)}, u32[]{:S(2)}, u32[]{:S(2)}) collective-permute-start(bf16[256,1024]{1,0:T(8,128)(2,1)S(1)} %collective-permute-done.3.refs_2_), channel_id=1, source_target_pairs={{4,0},{8,4},{12,8},{14,12},{10,14},{6,10},{2,6},{0,2},{5,1},{9,5},... | collective-permute-start | bytes 1572872 | tf_op jit(solution)/shard_map/ppermute | solution.py:87
  30.1 2.3 %collective-permute-start.7 = (bf16[304,128]{1,0:T(8,128)(2,1)}, bf16[304,128]{1,0:T(8,128)(2,1)S(1)}, u32[]{:S(2)}, u32[]{:S(2)}) collective-permute-start(bf16[304,128]{1,0:T(8,128)(2,1)} %get-tuple-element.55), channel_id=1, source_target_pairs={{0,12},{2,14},{4,8},{6,10},{8,4},{10,6},{12,0},{14,2},{1,13},{3,15... | collective-permute-start | bytes 233480 | tf_op jit(solution)/shard_map/ppermute | solution.py:82
  32.4 3.0 %collective-permute-start.4 = (bf16[304,128]{1,0:T(8,128)(2,1)}, bf16[304,128]{1,0:T(8,128)(2,1)S(1)}, u32[]{:S(2)}, u32[]{:S(2)}) collective-permute-start(bf16[304,128]{1,0:T(8,128)(2,1)} %get-tuple-element.50), channel_id=1, source_target_pairs={{0,6},{2,4},{4,2},{6,0},{8,14},{10,12},{12,10},{14,8},{1,7},{3,5},... | collective-permute-start | bytes 233480 | tf_op jit(solution)/shard_map/ppermute | solution.py:82
  35.4 9.8 %collective-permute-done.7 = bf16[304,128]{1,0:T(8,128)(2,1)S(1)} collective-permute-done((bf16[304,128]{1,0:T(8,128)(2,1)}, bf16[304,128]{1,0:T(8,128)(2,1)S(1)}, u32[]{:S(2)}, u32[]{:S(2)}) %collective-permute-start.7) | collective-permute-done | bytes 77856 | tf_op jit(solution)/shard_map/ppermute | solution.py:82
  49.0 2.6 %collective-permute-start.15 = (bf16[256,1024]{1,0:T(8,128)(2,1)S(1)}, bf16[256,1024]{1,0:T(8,128)(2,1)S(1)}, u32[]{:S(2)}, u32[]{:S(2)}) collective-permute-start(bf16[256,1024]{1,0:T(8,128)(2,1)S(1)} %collective-permute-done.10.refs_4_), channel_id=1, source_target_pairs={{4,0},{8,4},{12,8},{14,12},{10,14},{6,10},{2,6},{0,2},{5,1},{9,5},... | collective-permute-start | bytes 1572872 | tf_op jit(solution)/shard_map/ppermute | solution.py:87
  51.6 4.7 %collective-permute-done.12.w2 = bf16[7,304,128]{2,1,0:T(8,128)(2,1)S(1)} collective-permute-done((bf16[7,304,128]{2,1,0:T(8,128)(2,1)S(1)}, bf16[7,304,128]{2,1,0:T(8,128)(2,1)S(1)}, u32[]{:S(2)}, u32[]{:S(2)}) %collective-permute-start.12) | collective-permute-done | bytes 544800 | tf_op jit(solution)/shard_map/ppermute | solution.py:70
  56.3 2.5 %collective-permute-done.14.refs_5_ = bf16[256,1024]{1,0:T(8,128)(2,1)S(1)} collective-permute-done((bf16[256,1024]{1,0:T(8,128)(2,1)S(1)}, bf16[256,1024]{1,0:T(8,128)(2,1)S(1)}, u32[]{:S(2)}, u32[]{:S(2)}) %collective-permute-start.14) | collective-permute-done | bytes 524320 | tf_op jit(solution)/shard_map/ppermute | solution.py:87
  58.9 2.1 %collective-permute-start.17 = (bf16[128,1024]{1,0:T(8,128)(2,1)S(1)}, bf16[128,1024]{1,0:T(8,128)(2,1)S(1)}, u32[]{:S(2)}, u32[]{:S(2)}) collective-permute-start(bf16[128,1024]{1,0:T(8,128)(2,1)S(1)} %slice.53), channel_id=1, source_target_pairs={{4,0},{8,4},{12,8},{14,12},{10,14},{6,10},{2,6},{0,2},{5,1},{9,5},... | collective-permute-start | bytes 786440 | tf_op jit(solution)/shard_map/ppermute | solution.py:87
  61.0 5.1 %collective-permute-done.16.refs_7_ = bf16[128,1024]{1,0:T(8,128)(2,1)S(1)} collective-permute-done((bf16[128,1024]{1,0:T(8,128)(2,1)S(1)}, bf16[128,1024]{1,0:T(8,128)(2,1)S(1)}, u32[]{:S(2)}, u32[]{:S(2)}) %collective-permute-start.16) | collective-permute-done | bytes 262176 | tf_op jit(solution)/shard_map/ppermute | solution.py:87
  66.2 4.9 %forward.1 = (bf16[8,256,1024]{2,1,0:T(8,128)(2,1)S(1)}, bf16[3,128,128]{2,1,0:T(8,128)(2,1)S(1)}, bf16[4,88,1024]{2,1,0:T(8,128)(2,1)S(1)}, bf16[4,40,1024]{2,1...) custom-call(bf16[4,304,128]{2,1,0:T(8,128)(2,1)} %get-tuple-element.46.own, ...), custom_call_target="tpu_custom_call" | custom-call | bytes 28000000 | tf_op jit(solution)/shard_map/forward/pallas_call | solution.py:297
  74.3 4.1 %collective-permute-done.20 = bf16[1,384,128]{2,1,0:T(8,128)(2,1)S(1)} collective-permute-done((bf16[1,384,128]{2,1,0:T(8,128)(2,1)S(1)}, bf16[1,384,128]{2,1,0:T(8,128)(2,1)S(1)}, u32[]{:S(2)}, u32[]{:S(2)}) %collective-permute-start.20) | collective-permute-done | bytes 98336 | tf_op jit(solution)/shard_map/ppermute | solution.py:82
  78.5 2.1 %collective-permute-start.22 = (bf16[4,40,1024]{2,1,0:T(8,128)(2,1)S(1)}, bf16[4,40,1024]{2,1,0:T(8,128)(2,1)S(1)}, u32[]{:S(2)}, u32[]{:S(2)}) collective-permute-start(bf16[4,40,1024]{2,1,0:T(8,128)(2,1)S(1)} %get-tuple-element.73), channel_id=1, source_target_pairs={{0,4},{2,6},{4,0},{6,2},{8,12},{10,14},{12,8},{14,10},{1,5},{3,7},... | collective-permute-start | bytes 983048 | tf_op jit(solution)/shard_map/ppermute | solution.py:82
  80.7 6.7 %collective-permute-done.18 = bf16[4,88,1024]{2,1,0:T(8,128)(2,1)S(1)} collective-permute-done((bf16[4,88,1024]{2,1,0:T(8,128)(2,1)S(1)}, bf16[4,88,1024]{2,1,0:T(8,128)(2,1)S(1)}, u32[]{:S(2)}, u32[]{:S(2)}) %collective-permute-start.18) | collective-permute-done | bytes 720928 | tf_op jit(solution)/shard_map/ppermute | solution.py:82
  87.7 4.6 %collective-permute-done.21 = bf16[2,384,128]{2,1,0:T(8,128)(2,1)S(1)} collective-permute-done((bf16[2,384,128]{2,1,0:T(8,128)(2,1)S(1)}, bf16[2,384,128]{2,1,0:T(8,128)(2,1)S(1)}, u32[]{:S(2)}, u32[]{:S(2)}) %collective-permute-start.21) | collective-permute-done | bytes 196640 | tf_op jit(solution)/shard_map/ppermute | solution.py:82
  92.6 3.4 %collective-permute-start.24 = (bf16[2,40,1024]{2,1,0:T(8,128)(2,1)S(1)}, bf16[2,40,1024]{2,1,0:T(8,128)(2,1)S(1)}, u32[]{:S(2)}, u32[]{:S(2)}) collective-permute-start(bf16[2,40,1024]{2,1,0:T(8,128)(2,1)S(1)} %slice.56.refs_3_), channel_id=1, source_target_pairs={{0,8},{2,10},{4,12},{6,14},{8,0},{10,2},{12,4},{14,6},{1,9},{3,11}... | collective-permute-start | bytes 491528 | tf_op jit(solution)/shard_map/ppermute | solution.py:82
  95.9 4.2 %collective-permute-done.23.refs_1_ = bf16[4,384,128]{2,1,0:T(8,128)(2,1)S(1)} collective-permute-done((bf16[4,384,128]{2,1,0:T(8,128)(2,1)S(1)}, bf16[4,384,128]{2,1,0:T(8,128)(2,1)S(1)}, u32[]{:S(2)}, u32[]{:S(2)}) %collective-permute-start.23) | collective-permute-done | bytes 393248 | tf_op jit(solution)/shard_map/ppermute | solution.py:82
  100.2 2.4 %grads.1 = bf16[48,128,128]{2,1,0:T(8,128)(2,1)S(1)} custom-call(s32[16]{0:T(128)S(1)} %bitcast.26, s32[16]{0:T(128)S(1)} %bitcast.28, s32[16]{0:T(128)S(1)} %bitcast.30, s32[16]{0:T(128)S(1)} %copy-done.4, s32[16]{0:T(128)S(1)} %copy-done.5, s32[16]{0:T(128)S(1)} %copy-done.6, bf16[8,256,1024]{2,1,0:T(8,128)(2,1)S(1)} %get-tuple-element.70.field, ...), custom_call_target="tpu_custom_call" | custom-call | bytes 26250000 | tf_op jit(solution)/shard_map/grads/pallas_call | solution.py:356
  108.5 6.8 %collective-permute-done.25 = bf16[1,88,1024]{2,1,0:T(8,128)(2,1)S(1)} collective-permute-done((bf16[1,88,1024]{2,1,0:T(8,128)(2,1)S(1)}, bf16[1,88,1024]{2,1,0:T(8,128)(2,1)S(1)}, u32[]{:S(2)}, u32[]{:S(2)}) %collective-permute-start.25) | collective-permute-done | bytes 180256 | tf_op jit(solution)/shard_map/ppermute | solution.py:82
  (74 shorter events, 20.1 us)
Async XLA Ops:
  2.5 25.6 %collective-permute-start.3 = (bf16[256,1024]{1,0:T(8,128)(2,1)}, bf16[256,1024]{1,0:T(8,128)(2,1)S(1)}, u32[]{:S(2)}, u32[]{:S(2)}) collective-permute-start(bf16[256,1024]{1,0:T(8,128)(2,1)} %join.1.after.refs_0_), channel_id=1, source_target_pairs={{4,0},{8,4},{12,8},{14,12},{10,14},{6,10},{2,6},{0,2},{5,1},{9,5},... | collective-permute-start | bytes 1572872 | tf_op jit(solution)/shard_map/ppermute | solution.py:87
  5.4 22.7 %collective-permute-start.2 = (bf16[256,1024]{1,0:T(8,128)(2,1)}, bf16[256,1024]{1,0:T(8,128)(2,1)S(1)}, u32[]{:S(2)}, u32[]{:S(2)}) collective-permute-start(bf16[256,1024]{1,0:T(8,128)(2,1)} %join.1.after.refs_0_), channel_id=1, source_target_pairs={{0,4},{4,8},{8,12},{12,14},{14,10},{10,6},{6,2},{2,0},{1,5},{5,9},... | collective-permute-start | bytes 1572872 | tf_op jit(solution)/shard_map/ppermute | solution.py:87
  8.9 11.8 %collective-permute-start = (bf16[304,128]{1,0:T(8,128)(2,1)}, bf16[304,128]{1,0:T(8,128)(2,1)S(1)}, u32[]{:S(2)}, u32[]{:S(2)}) collective-permute-start(bf16[304,128]{1,0:T(8,128)(2,1)} %get-tuple-element.47), channel_id=1, source_target_pairs={{0,2},{2,0},{4,6},{6,4},{8,10},{10,8},{12,14},{14,12},{1,3},{3,1},... | collective-permute-start | bytes 233480 | tf_op jit(solution)/shard_map/ppermute | solution.py:82
  10.9 13.4 %collective-permute-start.1 = (bf16[304,128]{1,0:T(8,128)(2,1)}, bf16[304,128]{1,0:T(8,128)(2,1)S(1)}, u32[]{:S(2)}, u32[]{:S(2)}) collective-permute-start(bf16[304,128]{1,0:T(8,128)(2,1)} %get-tuple-element.48), channel_id=1, source_target_pairs={{0,4},{2,6},{4,0},{6,2},{8,12},{10,14},{12,8},{14,10},{1,5},{3,7},... | collective-permute-start | bytes 233480 | tf_op jit(solution)/shard_map/ppermute | solution.py:82
  12.5 11.8 %collective-permute-start.5 = (bf16[304,128]{1,0:T(8,128)(2,1)}, bf16[304,128]{1,0:T(8,128)(2,1)S(1)}, u32[]{:S(2)}, u32[]{:S(2)}) collective-permute-start(bf16[304,128]{1,0:T(8,128)(2,1)} %get-tuple-element.51), channel_id=1, source_target_pairs={{0,8},{2,10},{4,12},{6,14},{8,0},{10,2},{12,4},{14,6},{1,9},{3,11}... | collective-permute-start | bytes 233480 | tf_op jit(solution)/shard_map/ppermute | solution.py:82
  20.7 7.4 %collective-permute-start.8 = (bf16[304,128]{1,0:T(8,128)(2,1)}, bf16[304,128]{1,0:T(8,128)(2,1)S(1)}, u32[]{:S(2)}, u32[]{:S(2)}) collective-permute-start(bf16[304,128]{1,0:T(8,128)(2,1)} %get-tuple-element.56), channel_id=1, source_target_pairs={{0,14},{2,12},{4,10},{6,8},{8,6},{10,4},{12,2},{14,0},{1,15},{3,13... | collective-permute-start | bytes 233480 | tf_op jit(solution)/shard_map/ppermute | solution.py:82
  28.1 17.5 %collective-permute-start.9 = (bf16[256,1024]{1,0:T(8,128)(2,1)S(1)}, bf16[256,1024]{1,0:T(8,128)(2,1)S(1)}, u32[]{:S(2)}, u32[]{:S(2)}) collective-permute-start(bf16[256,1024]{1,0:T(8,128)(2,1)S(1)} %collective-permute-done.2.refs_1_), channel_id=1, source_target_pairs={{0,4},{4,8},{8,12},{12,14},{14,10},{10,6},{6,2},{2,0},{1,5},{5,9},... | collective-permute-start | bytes 1572872 | tf_op jit(solution)/shard_map/ppermute | solution.py:87
  28.1 17.5 %collective-permute-start.10 = (bf16[256,1024]{1,0:T(8,128)(2,1)S(1)}, bf16[256,1024]{1,0:T(8,128)(2,1)S(1)}, u32[]{:S(2)}, u32[]{:S(2)}) collective-permute-start(bf16[256,1024]{1,0:T(8,128)(2,1)S(1)} %collective-permute-done.3.refs_2_), channel_id=1, source_target_pairs={{4,0},{8,4},{12,8},{14,12},{10,14},{6,10},{2,6},{0,2},{5,1},{9,5},... | collective-permute-start | bytes 1572872 | tf_op jit(solution)/shard_map/ppermute | solution.py:87
  30.1 15.1 %collective-permute-start.7 = (bf16[304,128]{1,0:T(8,128)(2,1)}, bf16[304,128]{1,0:T(8,128)(2,1)S(1)}, u32[]{:S(2)}, u32[]{:S(2)}) collective-permute-start(bf16[304,128]{1,0:T(8,128)(2,1)} %get-tuple-element.55), channel_id=1, source_target_pairs={{0,12},{2,14},{4,8},{6,10},{8,4},{10,6},{12,0},{14,2},{1,13},{3,15... | collective-permute-start | bytes 233480 | tf_op jit(solution)/shard_map/ppermute | solution.py:82
  32.4 13.2 %collective-permute-start.6 = (bf16[304,128]{1,0:T(8,128)(2,1)}, bf16[304,128]{1,0:T(8,128)(2,1)S(1)}, u32[]{:S(2)}, u32[]{:S(2)}) collective-permute-start(bf16[304,128]{1,0:T(8,128)(2,1)} %get-tuple-element.53), channel_id=1, source_target_pairs={{0,10},{2,8},{4,14},{6,12},{8,2},{10,0},{12,6},{14,4},{1,11},{3,9}... | collective-permute-start | bytes 233480 | tf_op jit(solution)/shard_map/ppermute | solution.py:82
  32.4 13.2 %collective-permute-start.4 = (bf16[304,128]{1,0:T(8,128)(2,1)}, bf16[304,128]{1,0:T(8,128)(2,1)S(1)}, u32[]{:S(2)}, u32[]{:S(2)}) collective-permute-start(bf16[304,128]{1,0:T(8,128)(2,1)} %get-tuple-element.50), channel_id=1, source_target_pairs={{0,6},{2,4},{4,2},{6,0},{8,14},{10,12},{12,10},{14,8},{1,7},{3,5},... | collective-permute-start | bytes 233480 | tf_op jit(solution)/shard_map/ppermute | solution.py:82
  45.8 10.5 %collective-permute-start.12 = (bf16[7,304,128]{2,1,0:T(8,128)(2,1)S(1)}, bf16[7,304,128]{2,1,0:T(8,128)(2,1)S(1)}, u32[]{:S(2)}, u32[]{:S(2)}) collective-permute-start(bf16[7,304,128]{2,1,0:T(8,128)(2,1)S(1)} %bitcast_dynamic-update-slice_fusion.w0), channel_id=1, source_target_pairs={{0,16},{16,0},{1,17},{17,1},{2,18},{18,2},{3,19},{19,3},{4,20},{20... | collective-permute-start | bytes 1634312 | tf_op jit(solution)/shard_map/ppermute | solution.py:70
  47.5 11.3 %collective-permute-start.14 = (bf16[256,1024]{1,0:T(8,128)(2,1)S(1)}, bf16[256,1024]{1,0:T(8,128)(2,1)S(1)}, u32[]{:S(2)}, u32[]{:S(2)}) collective-permute-start(bf16[256,1024]{1,0:T(8,128)(2,1)S(1)} %collective-permute-done.9.refs_3_), channel_id=1, source_target_pairs={{0,4},{4,8},{8,12},{12,14},{14,10},{10,6},{6,2},{2,0},{1,5},{5,9},... | collective-permute-start | bytes 1572872 | tf_op jit(solution)/shard_map/ppermute | solution.py:87
  49.0 9.8 %collective-permute-start.15 = (bf16[256,1024]{1,0:T(8,128)(2,1)S(1)}, bf16[256,1024]{1,0:T(8,128)(2,1)S(1)}, u32[]{:S(2)}, u32[]{:S(2)}) collective-permute-start(bf16[256,1024]{1,0:T(8,128)(2,1)S(1)} %collective-permute-done.10.refs_4_), channel_id=1, source_target_pairs={{4,0},{8,4},{12,8},{14,12},{10,14},{6,10},{2,6},{0,2},{5,1},{9,5},... | collective-permute-start | bytes 1572872 | tf_op jit(solution)/shard_map/ppermute | solution.py:87
  51.6 9.4 %collective-permute-start.11 = (bf16[7,304,128]{2,1,0:T(8,128)(2,1)S(1)}, bf16[7,304,128]{2,1,0:T(8,128)(2,1)S(1)}, u32[]{:S(2)}, u32[]{:S(2)}) collective-permute-start(bf16[7,304,128]{2,1,0:T(8,128)(2,1)S(1)} %bitcast_dynamic-update-slice_fusion.w0), channel_id=1, source_target_pairs={{0,1},{1,0},{2,3},{3,2},{4,5},{5,4},{6,7},{7,6},{8,9},{9,8},{10,11... | collective-permute-start | bytes 1634312 | tf_op jit(solution)/shard_map/ppermute | solution.py:70
  56.3 9.9 %collective-permute-start.13 = (bf16[7,304,128]{2,1,0:T(8,128)(2,1)S(1)}, bf16[7,304,128]{2,1,0:T(8,128)(2,1)S(1)}, u32[]{:S(2)}, u32[]{:S(2)}) collective-permute-start(bf16[7,304,128]{2,1,0:T(8,128)(2,1)S(1)} %collective-permute-done.12.w2), channel_id=1, source_target_pairs={{0,1},{1,0},{2,3},{3,2},{4,5},{5,4},{6,7},{7,6},{8,9},{9,8},{10,11... | collective-permute-start | bytes 1634312 | tf_op jit(solution)/shard_map/ppermute | solution.py:70
  58.9 7.3 %collective-permute-start.17 = (bf16[128,1024]{1,0:T(8,128)(2,1)S(1)}, bf16[128,1024]{1,0:T(8,128)(2,1)S(1)}, u32[]{:S(2)}, u32[]{:S(2)}) collective-permute-start(bf16[128,1024]{1,0:T(8,128)(2,1)S(1)} %slice.53), channel_id=1, source_target_pairs={{4,0},{8,4},{12,8},{14,12},{10,14},{6,10},{2,6},{0,2},{5,1},{9,5},... | collective-permute-start | bytes 786440 | tf_op jit(solution)/shard_map/ppermute | solution.py:87
  71.2 16.2 %collective-permute-start.18 = (bf16[4,88,1024]{2,1,0:T(8,128)(2,1)S(1)}, bf16[4,88,1024]{2,1,0:T(8,128)(2,1)S(1)}, u32[]{:S(2)}, u32[]{:S(2)}) collective-permute-start(bf16[4,88,1024]{2,1,0:T(8,128)(2,1)S(1)} %get-tuple-element.69), channel_id=1, source_target_pairs={{0,2},{2,0},{4,6},{6,4},{8,10},{10,8},{12,14},{14,12},{1,3},{3,1},... | collective-permute-start | bytes 2162696 | tf_op jit(solution)/shard_map/ppermute | solution.py:82
  78.5 13.8 %collective-permute-start.22 = (bf16[4,40,1024]{2,1,0:T(8,128)(2,1)S(1)}, bf16[4,40,1024]{2,1,0:T(8,128)(2,1)S(1)}, u32[]{:S(2)}, u32[]{:S(2)}) collective-permute-start(bf16[4,40,1024]{2,1,0:T(8,128)(2,1)S(1)} %get-tuple-element.73), channel_id=1, source_target_pairs={{0,4},{2,6},{4,0},{6,2},{8,12},{10,14},{12,8},{14,10},{1,5},{3,7},... | collective-permute-start | bytes 983048 | tf_op jit(solution)/shard_map/ppermute | solution.py:82
  80.6 11.6 %collective-permute-start.21 = (bf16[2,384,128]{2,1,0:T(8,128)(2,1)S(1)}, bf16[2,384,128]{2,1,0:T(8,128)(2,1)S(1)}, u32[]{:S(2)}, u32[]{:S(2)}) collective-permute-start(bf16[2,384,128]{2,1,0:T(8,128)(2,1)S(1)} %pad_maximum_fusion.2), channel_id=1, source_target_pairs={{0,4},{2,6},{4,0},{6,2},{8,12},{10,14},{12,8},{14,10},{1,5},{3,7},... | collective-permute-start | bytes 589832 | tf_op jit(solution)/shard_map/ppermute | solution.py:82
  92.3 7.8 %collective-permute-start.23 = (bf16[4,384,128]{2,1,0:T(8,128)(2,1)S(1)}, bf16[4,384,128]{2,1,0:T(8,128)(2,1)S(1)}, u32[]{:S(2)}, u32[]{:S(2)}) collective-permute-start(bf16[4,384,128]{2,1,0:T(8,128)(2,1)S(1)} %pad_maximum_fusion.refs_0_), channel_id=1, source_target_pairs={{0,2},{2,0},{4,6},{6,4},{8,10},{10,8},{12,14},{14,12},{1,3},{3,1},... | collective-permute-start | bytes 1179656 | tf_op jit(solution)/shard_map/ppermute | solution.py:82
  92.4 10.3 %collective-permute-start.19 = (bf16[2,88,1024]{2,1,0:T(8,128)(2,1)S(1)}, bf16[2,88,1024]{2,1,0:T(8,128)(2,1)S(1)}, u32[]{:S(2)}, u32[]{:S(2)}) collective-permute-start(bf16[2,88,1024]{2,1,0:T(8,128)(2,1)S(1)} %slice.55.refs_2_), channel_id=1, source_target_pairs={{0,4},{2,6},{4,0},{6,2},{8,12},{10,14},{12,8},{14,10},{1,5},{3,7},... | collective-permute-start | bytes 1081352 | tf_op jit(solution)/shard_map/ppermute | solution.py:82
  92.6 10.1 %collective-permute-start.24 = (bf16[2,40,1024]{2,1,0:T(8,128)(2,1)S(1)}, bf16[2,40,1024]{2,1,0:T(8,128)(2,1)S(1)}, u32[]{:S(2)}, u32[]{:S(2)}) collective-permute-start(bf16[2,40,1024]{2,1,0:T(8,128)(2,1)S(1)} %slice.56.refs_3_), channel_id=1, source_target_pairs={{0,8},{2,10},{4,12},{6,14},{8,0},{10,2},{12,4},{14,6},{1,9},{3,11}... | collective-permute-start | bytes 491528 | tf_op jit(solution)/shard_map/ppermute | solution.py:82
  103.8 11.4 %collective-permute-start.25 = (bf16[1,88,1024]{2,1,0:T(8,128)(2,1)S(1)}, bf16[1,88,1024]{2,1,0:T(8,128)(2,1)S(1)}, u32[]{:S(2)}, u32[]{:S(2)}) collective-permute-start(bf16[1,88,1024]{2,1,0:T(8,128)(2,1)S(1)} %slice.58), channel_id=1, source_target_pairs={{0,8},{2,10},{4,12},{6,14},{8,0},{10,2},{12,4},{14,6},{1,9},{3,11}... | collective-permute-start | bytes 540680 | tf_op jit(solution)/shard_map/ppermute | solution.py:82
  (11 other events, 259.7 us)
